TPU v7x, 32 devices: a whole 2x2x4 slice. The times are simulated.
32 devices in a mesh: span: 2 (over x), seq: 16 (over z, y, core).
Axes of the slice: x: 2, y: 2, z: 4, core: 2. Of those that a mesh axis runs over, the one named last changes fastest.
Arguments:
- queries: bfloat16 [1536, 3072], P(('span', 'seq')), may hold values from -6 to 6
- keyvals: bfloat16 [1536, 1024], P(('span', 'seq')), may hold values from -6 to 6
- clip_index: int32 [2], replicated, may hold values from 0 to 7, as said below
- noise_step: int32 [2], replicated, may hold values from 0 to 63
- valid_count: int32 [2], replicated, may hold values from 384 to 768
- gate_table: float32 [64, 3072], replicated, may hold values from 0.5 to 2
Outputs:
- attended: bfloat16 [1536, 3072], P(('span', 'seq'))
Inputs may be any that keep to these rules, and one draw needn't show every extreme that they name: `clip_index`: each group has a different clip index; some group's clip index is 7.
All inputs are finite; a program needn't handle non-finite values.
Results may differ from a plain program's by a relative error of at most 0.0044.
Values may be sent and summed in bfloat16 or wider, within the bound.
No kernel may reach another device: no remote copies, remote signals or barrier semaphores. Data moves between devices by JAX's collectives and lax.ppermute only.
A program may use at most 128 MiB of HBM per device.

v0:
```python
import math

import jax
import jax.numpy as jnp
from jax import lax
from jax.sharding import PartitionSpec as P

QUERY_HEADS = 24
KEY_VALUE_HEADS = 4
HEAD_WIDTH = 128


NEGATIVE = -1e30


def block_size(total_rows):
    largest = 1
    for candidate in range(1, min(total_rows, 2048) + 1):
        if total_rows % candidate == 0:
            largest = candidate
    return largest


def attend_block(state_now, query_fourfold, key_row_block, value_row_block, usable):
    inv_root = 1.0 / math.sqrt(HEAD_WIDTH)

    def compute(state_in):
        big_max, weight_sum, numerator = state_in
        scores = (
            jnp.einsum(
                "thrd,khd->hrtk", query_fourfold, key_row_block, preferred_element_type=jnp.float32
            )
            * inv_root
        )
        scores = jnp.where(usable, scores, NEGATIVE)
        new_max = jnp.maximum(big_max, scores.max(-1))
        weights = jnp.where(usable, jnp.exp(scores - new_max[..., None]), 0.0)
        factor = jnp.exp(big_max - new_max)
        weight_sum = weight_sum * factor + weights.sum(-1)
        update = jnp.einsum(
            "hrtk,khd->hrtd",
            weights.astype(jnp.bfloat16),
            value_row_block,
            preferred_element_type=jnp.float32,
        )
        numerator = numerator * factor[..., None] + update
        return (new_max, weight_sum, numerator)

    return lax.cond(jnp.any(usable), compute, lambda state_in: state_in, state_now)


def start_offset_for(head_count, query_per_key_ratio, query_count):
    return (
        jnp.full((head_count, query_per_key_ratio, query_count), NEGATIVE, jnp.float32),
        jnp.zeros((head_count, query_per_key_ratio, query_count), jnp.float32),
        jnp.zeros((head_count, query_per_key_ratio, query_count, HEAD_WIDTH), jnp.float32),
    )


def per_device(queries, keyvals, clip_index, noise_step, valid_count, gate_table):
    token_count = queries.shape[0]
    n_groups = clip_index.shape[0]
    query_per_key_ratio = QUERY_HEADS // KEY_VALUE_HEADS
    key_row_width = KEY_VALUE_HEADS * HEAD_WIDTH
    group_id = lax.axis_index("span")
    group_numbers = jnp.arange(n_groups, dtype=jnp.int32)
    mine = group_numbers == group_id
    own_clip = jnp.sum(jnp.where(mine, clip_index, 0))
    own_step = jnp.sum(jnp.where(mine, noise_step, 0))
    own_count = jnp.sum(jnp.where(mine, valid_count, 0))
    visible = clip_index <= own_clip
    step_hot = (jnp.arange(gate_table.shape[0], dtype=jnp.int32) == own_step).astype(jnp.float32)
    gate_row = jnp.dot(step_hot[None, :], gate_table, precision=lax.Precision.HIGHEST)[0]
    query_fourfold = queries.reshape(token_count, KEY_VALUE_HEADS, query_per_key_ratio, HEAD_WIDTH)
    initial_state = start_offset_for(KEY_VALUE_HEADS, query_per_key_ratio, token_count)
    stacked = lax.all_gather(keyvals, "span", axis=0, tiled=True).reshape(
        n_groups, token_count, 2 * key_row_width
    )
    shard_rows = lax.all_gather(stacked, "seq", axis=1, tiled=True)
    row_width = shard_rows.shape[1]
    flat_ids = jnp.arange(n_groups * row_width, dtype=jnp.int32)
    flattened_rows = shard_rows.reshape(n_groups * row_width, 2 * key_row_width)
    key_row_block = flattened_rows[:, :key_row_width].reshape(-1, KEY_VALUE_HEADS, HEAD_WIDTH)
    value_row_block = flattened_rows[:, key_row_width:].reshape(-1, KEY_VALUE_HEADS, HEAD_WIDTH)
    onehot = (flat_ids // row_width)[:, None] == group_numbers[None, :]
    seen_clip = jnp.any(onehot & visible[None, :], axis=1)
    row_limit = jnp.sum(jnp.where(onehot, valid_count[None, :], 0), axis=1)
    usable = seen_clip & (flat_ids % row_width < row_limit)
    total_rows = key_row_block.shape[0]
    head_count = key_row_block.shape[1]
    block_rows = block_size(total_rows)
    blocks = total_rows // block_rows
    key_blocks = key_row_block.reshape(blocks, block_rows, head_count, HEAD_WIDTH)
    value_blocks = value_row_block.reshape(blocks, block_rows, head_count, HEAD_WIDTH)

    def step_block(state_in, block_data):
        return (
            attend_block(state_in, query_fourfold, block_data[0], block_data[1], block_data[2]),
            None,
        )

    state_out, unused = lax.scan(
        step_block, initial_state, (key_blocks, value_blocks, usable.reshape(blocks, block_rows))
    )
    big_max, weight_sum, numerator = state_out
    attended = (
        (numerator / weight_sum[..., None])
        .transpose(2, 0, 1, 3)
        .reshape(token_count, QUERY_HEADS * HEAD_WIDTH)
    )
    positions = lax.axis_index("seq") * token_count + jnp.arange(token_count, dtype=jnp.int32)
    live_rows = (positions < own_count).astype(jnp.float32)
    return (attended * gate_row[None, :] * live_rows[:, None]).astype(jnp.bfloat16)


def solution(mesh):
    return jax.shard_map(
        per_device,
        mesh=mesh,
        in_specs=(P(("span", "seq"), None), P(("span", "seq"), None), P(), P(), P(), P()),
        out_specs=P(("span", "seq"), None),
        check_vma=False,
    )
```

profile of v0, /device:TPU:0, one launch (start us, length us, event | category | flops | bytes accessed | tf_op | source)
XLA Modules:
  0.0 88.0 jit_solution(12815534316764402791)
XLA Ops:
  6.5 8.3 %all_gather.6 = bf16[96,1024]{1,0:T(8,128)(2,1)} all-gather(bf16[48,1024]{1,0:T(8,128)(2,1)} %param.9), channel_id=1, replica_groups=mesh['span'=2,'seq'=16] {'span'}, dimensions={0}, use_global_device_ids=true | all-gather | bytes 294912 | tf_op jit(solution)/shard_map/all_gather | solution.py:76
  14.9 0.0 all-gather.2.cloned.1.call-update
  14.9 1.3 %select_reduce_fusion.3 = s32[]{:T(128)} fusion(s32[2]{0:T(128)} %param.10, s32[]{:T(128)S(6)} %axis_index.23), kind=kLoop, calls=%fused_computation.44 | loop fusion | flops 5 | bytes 16 | tf_op jit(solution)/shard_map/reduce_sum | solution.py:68
  16.2 1.3 %broadcast_compare_fusion = pred[2]{0:T(512)(128)(4,1)S(1)} fusion(s32[2]{0:T(128)} %param.10, s32[]{:T(128)} %select_reduce_fusion.3), kind=kLoop, calls=%fused_computation.47 | loop fusion | flops 2 | bytes 14 | tf_op jit(solution)/shard_map/le | solution.py:71
  17.5 0.1 and_reduce_fusion
  17.6 0.7 select_reduce_fusion
  18.4 0.6 fusion.30
  19.7 1.4 %select_reduce_fusion.1 = (s32[]{:T(128)}, s32[]{:T(128)}) fusion(s32[2]{0:T(128)} %param.12, s32[]{:T(128)S(6)} %axis_index.23, s32[2]{0:T(128)} %param.11), kind=kLoop, calls=%fused_computation.41 | loop fusion | flops 8 | bytes 28 | tf_op jit(solution)/shard_map/reduce_sum | solution.py:70
  21.1 0.6 compare_convert_fusion
  21.8 1.0 %fusion.25 = f32[1,3072]{1,0:T(1,128)S(1)} fusion(f32[64,3072]{1,0:T(8,128)S(1)} %copy-done, s32[]{:T(128)} %get-tuple-element.120), kind=kOutput, calls=%fused_computation.37 | convolution fusion | flops 2359360 | bytes 798724 | tf_op jit(solution)/shard_map/dot_general | solution.py:73
  22.8 37.8 %all-gather.2.cloned.1.call-done = bf16[2,768,1024]{2,1,0:T(8,128)(2,1)} async-done(((bf16[2,48,1024]{2,1,0:T(8,128)(2,1)}), bf16[2,768,1024]{2,1,0:T(8,128)(2,1)}) %all-gather.2.cloned.1.call-update) | async-done | bytes 3145744 | tf_op jit(solution)/shard_map/all_gather | solution.py:79
  60.6 19.1 %conditional.1 = ((f32[4,6,48]{2,1,0:T(8,128)S(1)}, f32[4,6,48,128]{3,2,1,0:T(8,128)S(1)})) conditional(s32[]{:T(128)} %convert_element_type.21, (f32[4,6,48]{2,1,0:T(8,128)S(1)}, f32[4,6,48,128]{3,2,1,0:T(8,128)S(1)}) %tuple.26, (pred[1536]{0:T(1024)(128)(4,1)S(1)}, bf16[2,768,1024]{2,1,0:T(8,128)(2,1)}, bf16[48,3072]{1,0:T(8,128)(2,1)}, ...), branch_computations={%region_4.5_spmd, %region_5.8_spmd} | conditional | flops 929271168 | bytes 73689680 | solution.py:49
  60.6 3.8 %fusion.32 = (bf16[1536,512]{1,0:T(8,128)(2,1)}, bf16[1536,512]{1,0:T(8,128)(2,1)}) fusion(bf16[1536,1024]{1,0:T(8,128)(2,1)} %bitcast.36), kind=kLoop, calls=%fused_computation.49 | loop fusion | bytes 6291456 | tf_op jit(solution)/shard_map/slice | solution.py:84
  64.4 1.7 %copy.32 = bf16[1536,512]{0,1:T(8,128)(2,1)S(1)} copy(bf16[1536,512]{1,0:T(8,128)(2,1)} %get-tuple-element.114) | data formatting | bytes 3145728 | tf_op jit(solution)/shard_map/while/body/eval_jaxpr/cond
  66.1 1.3 %reshape.47 = bf16[48,4,6,128]{3,2,1,0:T(8,128)(2,1)S(1)} reshape(bf16[48,3072]{1,0:T(8,128)(2,1)} %get-tuple-element.100) | data formatting | bytes 589824 | tf_op jit(solution)/shard_map/reshape | solution.py:74
  67.4 1.3 %bitcast_reduce_fusion = (f32[4,6,48]{2,1,0:T(8,128)S(1)}, f32[4,1536,48,6]{1,2,3,0:T(8,128)S(1)}) fusion(pred[1536]{0:T(1024)(128)(4,1)S(1)} %get-tuple-element.91, bf16[1536,4,128,1]{0,2,3,1:T(8,128)(2,1)S(1)} %bitcast.35, bf16[48,4,6,128]{3,2,1,0:T(8,128)(2,1)S(1)} %reshape.47), kind=kOutput, calls=%fused_computation.1 | convolution fusion | flops 458292096 | bytes 8951808 | tf_op jit(solution)/shard_map/while/body/eval_jaxpr/cond/branch_1_fun/thrd,khd->hrtk/dot_general | solution.py:30
  68.7 2.9 %copy-done.1 = f32[4,1536,48,6]{1,2,3,0:T(8,128)} copy-done((f32[4,1536,48,6]{1,2,3,0:T(8,128)}, f32[4,1536,48,6]{1,2,3,0:T(8,128)S(1)}, u32[]{:S(2)}) %copy-start.1) | copy-done | bytes 7077912 | tf_op jit(solution)/shard_map/while/body/eval_jaxpr/cond
  71.6 1.9 %fusion.3 = f32[4,6,48]{2,1,0:T(8,128)S(1)} fusion(f32[4,1536,48,6]{1,2,3,0:T(8,128)S(1)} %get-tuple-element.118, f32[4,6,48]{2,1,0:T(8,128)S(1)} %broadcast_maximum_fusion, pred[1536]{0:T(1024)(128)(4,1)S(1)} %get-tuple-element.91), kind=kLoop, calls=%fused_computation.6 | loop fusion | flops 8846208 | bytes 7088640 | tf_op jit(solution)/shard_map/while/body/eval_jaxpr/cond/branch_1_fun/reduce_sum | solution.py:39
  73.5 1.6 %copy.33 = bf16[1536,512]{0,1:T(8,128)(2,1)} copy(bf16[1536,512]{1,0:T(8,128)(2,1)S(1)} %copy-done.2) | data formatting | bytes 3145728 | tf_op jit(solution)/shard_map/while/body/eval_jaxpr/cond
  75.1 4.6 %fusion.8 = f32[4,6,48,128]{3,2,1,0:T(8,128)S(1)} fusion(bf16[1536,4,128,1]{0,2,3,1:T(8,128)(2,1)} %bitcast.37, f32[4,1536,48,6]{1,2,3,0:T(8,128)} %copy-done.1, f32[4,6,48]{2,1,0:T(8,128)S(1)} %broadcast_maximum_fusion, pred[1536]{0:T(1024)(128)(4,1)S(1)} %get-tuple-element.91, f32[4,6,48,128]{3,2,1,0:T(8,128)S(1)} %get-tuple-element.94, ...), kind=kOutput, calls=%fused_computation.10 | convolution fusion | flops 462127104 | bytes 9841152 | tf_op jit(solution)/shard_map/while/body/eval_jaxpr/cond/branch_1_fun/hrtk,khd->hrtd/dot_general | solution.py:40
  79.7 0.2 divide_bitcast_fusion
  80.0 0.2 copy.24
  80.2 0.1 reshape.51
  80.3 0.8 multiply_convert_fusion
  (11 shorter events, 0.1 us)
Async XLA Ops:
  6.5 15.2 %copy-start = (f32[64,3072]{1,0:T(8,128)S(1)}, f32[64,3072]{1,0:T(8,128)}, u32[]{:S(2)}) copy-start(f32[64,3072]{1,0:T(8,128)} %param.13) | copy-start | bytes 2359300
  6.5 54.1 %all-gather.2.cloned.1.call-start = ((), (), s32[]{:S(2)}) async-start(), calls=%async_computation | async-start | bytes 3342336 | tf_op jit(solution)/shard_map/all_gather | solution.py:79
  68.7 2.9 %copy-start.1 = (f32[4,1536,48,6]{1,2,3,0:T(8,128)}, f32[4,1536,48,6]{1,2,3,0:T(8,128)S(1)}, u32[]{:S(2)}) copy-start(f32[4,1536,48,6]{1,2,3,0:T(8,128)S(1)} %get-tuple-element.118) | copy-start | bytes 21233668 | tf_op jit(solution)/shard_map/while/body/eval_jaxpr/cond
  68.7 4.8 %copy-start.2 = (bf16[1536,512]{1,0:T(8,128)(2,1)S(1)}, bf16[1536,512]{1,0:T(8,128)(2,1)}, u32[]{:S(2)}) copy-start(bf16[1536,512]{1,0:T(8,128)(2,1)} %get-tuple-element.113) | copy-start | bytes 4718596 | tf_op jit(solution)/shard_map/while/body/eval_jaxpr/cond
Sparse Core Ops, SparseCore 0:
  15.0 45.5 all-gather.1
where the time goes:
time: 88.2 us; the launch traced here: 88 us
  waiting for transfers between devices  37.8 us (43%)
  between operations  14.1 us (16%)
  local copies, waits for them, and re-layouts  11.7 us (13%)
  other arithmetic  9.06 us (10%)
  blocking collectives  8.34 us (9%)
  matrix products  6.87 us (8%)
    all_gather x1, waiting for transfers between devices, per_device(): shard_rows = lax.all_gather(stacked, 'seq', axis=1, tiled=True)  37.8 us
    all_gather x1, blocking collectives, per_device(): lax.all_gather(keyvals, 'span', axis=0, tiled=True)  8.34 us
    cond x6, local copies, waits for them, and re-layouts  6.2 us
    dot_general x1, matrix products, compute(): jnp.einsum('hrtk,khd->hrtd', weights.astype(jnp.bfloat16), value_row_bloc...  4.57 us
    slice x1, local copies, waits for them, and re-layouts, per_device(): flattened_rows[:, key_row_width:].reshape(-1, KEY_VALUE_HEADS, HEAD_WIDTH)  3.77 us
    reduce_sum x1, other arithmetic, compute(): weight_sum = weight_sum * factor + weights.sum(-1)  1.88 us
  transfers between devices with their start and end apart: 1, of which 1 were waited for; matrix products, arithmetic and copies ran while one was open for 8% of the time, Pallas kernels for 0%

commit v1 on v0

v1 whole, which is shorter than its diff:
```python
import functools
import math

import jax
import jax.numpy as jnp
import numpy as np
from jax import lax
from jax.experimental import pallas as pl
from jax.experimental.pallas import tpu as pltpu
from jax.sharding import PartitionSpec as P

QUERY_HEADS = 24
KEY_VALUE_HEADS = 4
HEAD_WIDTH = 128
RATIO = QUERY_HEADS // KEY_VALUE_HEADS
KEY_WIDTH = KEY_VALUE_HEADS * HEAD_WIDTH
NEGATIVE = -1e30
LOG2E = math.log2(math.e)
TILE = 384
MOST_PARTNERS = 3


def attend_kernel(n_kv, carried, last, place_ref, q_ref, *refs):
    kv_refs, bias_refs, refs = refs[:n_kv], refs[n_kv : 2 * n_kv], refs[2 * n_kv :]
    state_in = None
    if carried:
        state_in, refs = refs[:3], refs[3:]
    if last:
        gate_ref, out_ref = refs
    else:
        state_out = refs
    tokens = q_ref.shape[0]
    rows = RATIO * tokens
    scale = LOG2E / math.sqrt(HEAD_WIDTH)
    if last:
        positions = place_ref[0] + lax.broadcasted_iota(jnp.int32, (tokens, 1), 0)
        live = (positions < place_ref[1]).astype(jnp.float32)
    for head in range(KEY_VALUE_HEADS):
        first = head * RATIO
        query = jnp.concatenate(
            [
                q_ref[:, (first + r) * HEAD_WIDTH : (first + r + 1) * HEAD_WIDTH]
                for r in range(RATIO)
            ],
            axis=0,
        )

        def step(kv_ref, bias_ref, start, size, state):
            key = kv_ref[pl.ds(start, size), head * HEAD_WIDTH : (head + 1) * HEAD_WIDTH]
            value = kv_ref[
                pl.ds(start, size),
                KEY_WIDTH + head * HEAD_WIDTH : KEY_WIDTH + (head + 1) * HEAD_WIDTH,
            ]
            scores = lax.dot_general(
                query, key, (((1,), (1,)), ((), ())), preferred_element_type=jnp.float32
            )
            scores = scores * scale + bias_ref[:, pl.ds(start, size)]
            top = jnp.max(scores, axis=1, keepdims=True)
            if state is not None:
                top = jnp.maximum(top, state[0])
            weights = jnp.exp2(scores - top)
            total = jnp.sum(weights, axis=1, keepdims=True)
            numerator = jnp.dot(
                weights.astype(jnp.bfloat16), value, preferred_element_type=jnp.float32
            )
            if state is not None:
                factor = jnp.exp2(state[0] - top)
                total = total + state[1] * factor
                numerator = numerator + state[2] * factor
            return top, total, numerator

        span = pl.ds(head * rows, rows)
        state = tuple(ref[span, :] for ref in state_in) if carried else None
        for kv_ref, bias_ref in zip(kv_refs, bias_refs):
            state = step(kv_ref, bias_ref, 0, kv_ref.shape[0], state)
        if not last:
            for ref, part in zip(state_out, state):
                ref[span, :] = part
            continue
        result = state[2] * (1.0 / state[1])
        for r in range(RATIO):
            columns = slice((first + r) * HEAD_WIDTH, (first + r + 1) * HEAD_WIDTH)
            part = result[r * tokens : (r + 1) * tokens]
            out_ref[:, columns] = (part * gate_ref[:, columns] * live).astype(out_ref.dtype)


def attend(place, queries, keyvals, biases, state=None, gate=None):
    tokens = queries.shape[0]
    rows = QUERY_HEADS * tokens
    keys = sum(kv.shape[0] for kv in keyvals)
    last = gate is not None
    operands = [place, queries, *keyvals, *biases, *(state or ())] + ([gate] if last else [])
    whole = pl.BlockSpec(memory_space=pltpu.VMEM)
    if last:
        out_shape = jax.ShapeDtypeStruct(queries.shape, jnp.bfloat16)
    else:
        out_shape = (
            jax.ShapeDtypeStruct((rows, 1), jnp.float32),
            jax.ShapeDtypeStruct((rows, 1), jnp.float32),
            jax.ShapeDtypeStruct((rows, HEAD_WIDTH), jnp.float32),
        )
    return pl.pallas_call(
        functools.partial(attend_kernel, len(keyvals), state is not None, last),
        out_shape=out_shape,
        in_specs=[pl.BlockSpec(memory_space=pltpu.SMEM)] + [whole] * (len(operands) - 1),
        out_specs=whole if last else (whole,) * 3,
        compiler_params=pltpu.CompilerParams(vmem_limit_bytes=40 * 1024 * 1024),
        cost_estimate=pl.CostEstimate(
            flops=4 * rows * keys * HEAD_WIDTH,
            bytes_accessed=keys * 2 * KEY_WIDTH * 2,
            transcendentals=rows * keys,
        ),
    )(*operands)


def streamed_kernel(place_ref, q_ref, kv_ref, bias_ref, gate_ref, out_ref, top_ref, total_ref, numerator_ref):
    tokens = q_ref.shape[0]
    rows = RATIO * tokens
    scale = LOG2E / math.sqrt(HEAD_WIDTH)

    @pl.when(pl.program_id(0) == 0)
    def _():
        top_ref[...] = jnp.full_like(top_ref, NEGATIVE)
        total_ref[...] = jnp.zeros_like(total_ref)
        numerator_ref[...] = jnp.zeros_like(numerator_ref)

    for head in range(KEY_VALUE_HEADS):
        first = head * RATIO
        span = slice(head * rows, (head + 1) * rows)
        columns = [slice((first + r) * HEAD_WIDTH, (first + r + 1) * HEAD_WIDTH) for r in range(RATIO)]
        query = jnp.concatenate([q_ref[:, c] for c in columns], axis=0)
        key = kv_ref[:, head * HEAD_WIDTH : (head + 1) * HEAD_WIDTH]
        value = kv_ref[:, KEY_WIDTH + head * HEAD_WIDTH : KEY_WIDTH + (head + 1) * HEAD_WIDTH]
        scores = lax.dot_general(
            query, key, (((1,), (1,)), ((), ())), preferred_element_type=jnp.float32
        )
        scores = scores * scale + bias_ref[...]
        top = jnp.maximum(top_ref[span, :], jnp.max(scores, axis=1, keepdims=True))
        weights = jnp.exp2(scores - top)
        factor = jnp.exp2(top_ref[span, :] - top)
        top_ref[span, :] = top
        total_ref[span, :] = total_ref[span, :] * factor + jnp.sum(weights, axis=1, keepdims=True)
        numerator_ref[span, :] = numerator_ref[span, :] * factor + jnp.dot(
            weights.astype(jnp.bfloat16), value, preferred_element_type=jnp.float32
        )

    @pl.when(pl.program_id(0) == pl.num_programs(0) - 1)
    def _():
        positions = place_ref[0] + lax.broadcasted_iota(jnp.int32, (tokens, 1), 0)
        live = (positions < place_ref[1]).astype(jnp.float32)
        for h in range(QUERY_HEADS):
            span = slice(h * tokens, (h + 1) * tokens)
            columns = slice(h * HEAD_WIDTH, (h + 1) * HEAD_WIDTH)
            part = numerator_ref[span, :] / total_ref[span, :]
            out_ref[:, columns] = (part * gate_ref[:, columns] * live).astype(out_ref.dtype)


def streamed(place, queries, keyvals, bias, gate):
    rows = QUERY_HEADS * queries.shape[0]
    keys = keyvals.shape[0]
    tile = TILE if keys % TILE == 0 else keys
    whole = pl.BlockSpec(memory_space=pltpu.VMEM)
    return pl.pallas_call(
        streamed_kernel,
        grid=(keys // tile,),
        out_shape=jax.ShapeDtypeStruct(queries.shape, jnp.bfloat16),
        in_specs=[
            pl.BlockSpec(memory_space=pltpu.SMEM),
            whole,
            pl.BlockSpec((tile, keyvals.shape[1]), lambda t: (t, 0)),
            pl.BlockSpec((1, tile), lambda t: (0, t)),
            whole,
        ],
        out_specs=whole,
        scratch_shapes=[
            pltpu.VMEM((rows, 1), jnp.float32),
            pltpu.VMEM((rows, 1), jnp.float32),
            pltpu.VMEM((rows, HEAD_WIDTH), jnp.float32),
        ],
        compiler_params=pltpu.CompilerParams(vmem_limit_bytes=40 * 1024 * 1024),
    )(place, queries, keyvals, bias, gate)


def per_device(n_span, n_seq, queries, keyvals, clip_index, noise_step, valid_count, gate_table):
    tokens = queries.shape[0]
    devices = n_span * n_seq
    span_id, seq_id = lax.axis_index("span"), lax.axis_index("seq")
    me = span_id * n_seq + seq_id

    def exchange(block, distance):
        pairs = [(i, i ^ distance) for i in range(devices)]
        return lax.ppermute(block, ("span", "seq"), pairs)

    groups = jnp.arange(n_span, dtype=jnp.int32)
    own = lambda values: jnp.sum(jnp.where(groups == span_id, values, 0))
    own_clip, own_step, own_count = own(clip_index), own(noise_step), own(valid_count)
    limits = jnp.where(clip_index <= own_clip, valid_count, 0)

    def bias_of(distances):
        if distances is None:
            source = jnp.arange(devices * tokens, dtype=jnp.int32)[None, :] // tokens
            within = jnp.arange(devices * tokens, dtype=jnp.int32)[None, :] % tokens
        else:
            source = me ^ jnp.asarray(np.repeat(np.array(distances, np.int32), tokens)[None, :])
            within = jnp.asarray(np.tile(np.arange(tokens, dtype=np.int32), len(distances))[None, :])
        position = (source % n_seq) * tokens + within
        group = source // n_seq
        limit = jnp.zeros_like(position)
        for g in range(n_span):
            limit = jnp.where(group == g, limits[g], limit)
        return jnp.where(position < limit, 0.0, NEGATIVE).astype(jnp.float32)

    gate = lax.dynamic_slice(gate_table, (own_step, 0), (1, gate_table.shape[1]))
    place = jnp.stack([seq_id * tokens, own_count])
    far = [4 * i for i in range(n_seq // 4)]
    plane = [2] + [s * n_seq + y for s in range(1, n_span) for y in (2, 0)]
    if len(far) not in (2, 4) or len(plane) > MOST_PARTNERS or devices & (devices - 1):
        rows = lax.all_gather(lax.all_gather(keyvals, "seq", tiled=True), "span", tiled=True)
        return streamed(place, queries, rows, bias_of(None), gate)
    blocks = {0: keyvals}
    for d in far[1:]:
        blocks[d] = exchange(keyvals, d)
    half = len(far) // 2
    gathered = []
    for part in (far[:half], far[half:]):
        column = jnp.concatenate([blocks[d] for d in part], axis=0)
        rows = jnp.concatenate([column] + [exchange(column, d) for d in plane], axis=0)
        order = [p ^ d for p in [0] + plane for d in part]
        gathered.append((rows, bias_of(order), exchange(rows, 1), bias_of([d ^ 1 for d in order])))
    (near, near_bias, near_twin, near_twin_bias), (away, away_bias, away_twin, away_twin_bias) = gathered
    state = attend(place, queries, [near, near_twin], [near_bias, near_twin_bias])
    state = attend(place, queries, [away], [away_bias], state)
    return attend(place, queries, [away_twin], [away_twin_bias], state, gate)


def solution(mesh):
    return jax.shard_map(
        functools.partial(per_device, mesh.shape["span"], mesh.shape["seq"]),
        mesh=mesh,
        in_specs=(P(("span", "seq"), None), P(("span", "seq"), None), P(), P(), P(), P()),
        out_specs=P(("span", "seq"), None),
        check_vma=False,
    )
```

time: 88.2 us -> 44.7 us (0.51)
  waiting for transfers between devices: 37.8 us -> 11.3 us
  starting transfers between devices: 0.01 us -> 14.2 us
  between operations: 14.1 us -> 2.11 us
  Pallas kernels: 0 us -> 9.06 us
  blocking collectives: 8.34 us -> 0 us
  local copies, waits for them, and re-layouts: 11.7 us -> 3.68 us
  matrix products: 6.87 us -> 0 us
  other arithmetic: 9.06 us -> 3.99 us
    all_gather x1 -> x0, waiting for transfers between devices: 37.8 us -> none  [per_device(): shard_rows = lax.all_gather(stacked, 'seq', axis=1, tiled=True)]
    ppermute x0 -> x11, starting transfers between devices: none -> 14.2 us  [exchange(): return lax.ppermute(block, ('span', 'seq'), pairs)]
    ppermute x0 -> x11, waiting for transfers between devices: none -> 11.3 us  [exchange(): return lax.ppermute(block, ('span', 'seq'), pairs)]
    pallas_call x0 -> x3, Pallas kernels: none -> 9.06 us  [attend(): pl.pallas_call(functools.partial(attend_kernel, len(keyvals), state is no...]
    all_gather x1 -> x0, blocking collectives: 8.34 us -> none  [per_device(): lax.all_gather(keyvals, 'span', axis=0, tiled=True)]
    dot_general x3 -> x0, matrix products: 6.87 us -> none  [the longest x1 4.57 us: compute(): jnp.einsum('hrtk,khd->hrtd', weights.astype(jnp.bfloat16), value_row_bloc...]
    cond x6 -> x0, local copies, waits for them, and re-layouts: 6.2 us -> none
    reduce_sum x4 -> x1, other arithmetic: 5.3 us -> 0.63 us  [per_device(): own = lambda values: jnp.sum(jnp.where(groups == span_id, values, 0))]
  transfers between devices with their start and end apart: 1 -> 11, of which waited for: 1 -> 5; matrix products, arithmetic and copies ran while one was open for 8% -> 13% of each run, Pallas kernels for 0% -> 12%
where the time goes in v1:
time: 44.7 us; the launch traced here: 44.4 us
  starting transfers between devices  14.2 us (32%)
  waiting for transfers between devices  11.3 us (25%)
  Pallas kernels  9.06 us (20%)
  other arithmetic  3.99 us (9%)
  local copies, waits for them, and re-layouts  3.68 us (8%)
  between operations  2.11 us (5%)
    ppermute x11, starting transfers between devices, exchange(): return lax.ppermute(block, ('span', 'seq'), pairs)  14.2 us
    ppermute x11, waiting for transfers between devices, exchange(): return lax.ppermute(block, ('span', 'seq'), pairs)  11.3 us
    pallas_call x3, Pallas kernels, attend(): pl.pallas_call(functools.partial(attend_kernel, len(keyvals), state is no...  9.06 us
    unnamed x26, local copies, waits for them, and re-layouts  3.01 us
    select_n x1, other arithmetic, per_device(): limits = jnp.where(clip_index <= own_clip, valid_count, 0)  1.34 us
    select_n x1, other arithmetic, bias_of(): return jnp.where(position < limit, 0.0, NEGATIVE).astype(jnp.float32)  1.33 us
  transfers between devices with their start and end apart: 11, of which 5 were waited for; matrix products, arithmetic and copies ran while one was open for 13% of the time, Pallas kernels for 12%

profile of v1, /device:TPU:0, one launch (start us, length us, event | category | flops | bytes accessed | tf_op | source)
XLA Modules:
  0.0 44.4 jit_solution(11436511367386902074)
XLA Ops:
  0.0 3.0 %collective-permute-start.6 = (bf16[48,1024]{1,0:T(8,128)(2,1)}, bf16[48,1024]{1,0:T(8,128)(2,1)S(1)}, u32[]{:S(2)}, u32[]{:S(2)}) collective-permute-start(bf16[48,1024]{1,0:T(8,128)(2,1)} %param.15), channel_id=1, source_target_pairs={{0,4},{1,5},{2,6},{3,7},{4,0},{5,1},{6,2},{7,3},{8,12},{9,13},{10,... | collective-permute-start | bytes 294920 | tf_op jit(solution)/shard_map/ppermute | solution.py:192
  3.0 2.6 %collective-permute-start = (bf16[48,1024]{1,0:T(8,128)(2,1)}, bf16[48,1024]{1,0:T(8,128)(2,1)S(1)}, u32[]{:S(2)}, u32[]{:S(2)}) collective-permute-start(bf16[48,1024]{1,0:T(8,128)(2,1)} %param.15), channel_id=1, source_target_pairs={{0,8},{1,9},{2,10},{3,11},{4,12},{5,13},{6,14},{7,15},{8,0},{9,1},... | collective-permute-start | bytes 294920 | tf_op jit(solution)/shard_map/ppermute | solution.py:192
  5.6 0.7 %copy-done.8 = s32[2]{0:T(128)S(1)} copy-done((s32[2]{0:T(128)S(1)}, s32[2]{0:T(128)}, u32[]{:S(2)}) %copy-start.8) | copy-done | bytes 32
  6.3 0.6 %select_reduce_fusion.1 = s32[]{:T(128)} fusion(s32[2]{0:T(128)S(1)} %copy-done.8, s32[]{:T(128)S(6)} %axis_index.25), kind=kLoop, calls=%fused_computation.61 | loop fusion | flops 5 | bytes 16 | tf_op jit(solution)/shard_map/reduce_sum | solution.py:195
  6.9 0.7 %copy-done.7 = s32[2]{0:T(128)S(1)} copy-done((s32[2]{0:T(128)S(1)}, s32[2]{0:T(128)}, u32[]{:S(2)}) %copy-start.7) | copy-done | bytes 32
  7.6 1.3 %compare_select_fusion.24 = (s32[2]{0:T(128)S(1)}, s32[]{:T(128)}, s32[]{:T(128)}) fusion(s32[2]{0:T(128)S(1)} %copy-done.7, s32[2]{0:T(128)S(1)} %copy-done.8, s32[]{:T(128)} %select_reduce_fusion.1, s32[]{:T(128)S(6)} %axis_index.25, s32[2]{0:T(128)S(1)} %copy-done.9), kind=kLoop, calls=%fused_computation.46 | loop fusion | flops 12 | bytes 48 | tf_op jit(solution)/shard_map/jit(_where)/select_n | solution.py:197
  8.9 0.9 %constant_dynamic-update-slice_fusion.8 = (bf16[96,1024]{1,0:T(8,128)(2,1)S(1)}, bf16[384,1024]{1,0:T(8,128)(2,1)S(1)}) fusion(bf16[48,1024]{1,0:T(8,128)(2,1)} %param.15), kind=kLoop, calls=%fused_computation.8 | loop fusion | bytes 294912
  9.9 1.8 %collective-permute-start.7 = (bf16[96,1024]{1,0:T(8,128)(2,1)S(1)}, bf16[96,1024]{1,0:T(8,128)(2,1)S(1)}, u32[]{:S(2)}, u32[]{:S(2)}) collective-permute-start(bf16[96,1024]{1,0:T(8,128)(2,1)S(1)} %get-tuple-element.17), channel_id=1, source_target_pairs={{0,2},{1,3},{2,0},{3,1},{4,6},{5,7},{6,4},{7,5},{8,10},{9,11},{10,... | collective-permute-start | bytes 589832 | tf_op jit(solution)/shard_map/ppermute | solution.py:192
  11.7 1.4 %collective-permute-start.8 = (bf16[96,1024]{1,0:T(8,128)(2,1)S(1)}, bf16[96,1024]{1,0:T(8,128)(2,1)S(1)}, u32[]{:S(2)}, u32[]{:S(2)}) collective-permute-start(bf16[96,1024]{1,0:T(8,128)(2,1)S(1)} %get-tuple-element.17), channel_id=1, source_target_pairs={{0,18},{1,19},{2,16},{3,17},{4,22},{5,23},{6,20},{7,21},{8,26},{9,... | collective-permute-start | bytes 589832 | tf_op jit(solution)/shard_map/ppermute | solution.py:192
  13.1 0.3 collective-permute-start.9
  13.4 0.3 collective-permute-done
  13.7 1.6 %collective-permute-start.2 = (bf16[96,1024]{1,0:T(8,128)(2,1)S(1)}, bf16[96,1024]{1,0:T(8,128)(2,1)S(1)}, u32[]{:S(2)}, u32[]{:S(2)}) collective-permute-start(bf16[96,1024]{1,0:T(8,128)(2,1)S(1)} %get-tuple-element.21), channel_id=1, source_target_pairs={{0,2},{1,3},{2,0},{3,1},{4,6},{5,7},{6,4},{7,5},{8,10},{9,11},{10,... | collective-permute-start | bytes 589832 | tf_op jit(solution)/shard_map/ppermute | solution.py:192
  15.3 1.4 %collective-permute-start.3 = (bf16[96,1024]{1,0:T(8,128)(2,1)S(1)}, bf16[96,1024]{1,0:T(8,128)(2,1)S(1)}, u32[]{:S(2)}, u32[]{:S(2)}) collective-permute-start(bf16[96,1024]{1,0:T(8,128)(2,1)S(1)} %get-tuple-element.21), channel_id=1, source_target_pairs={{0,18},{1,19},{2,16},{3,17},{4,22},{5,23},{6,20},{7,21},{8,26},{9,... | collective-permute-start | bytes 589832 | tf_op jit(solution)/shard_map/ppermute | solution.py:192
  16.7 7.0 %collective-permute-done.7 = bf16[96,1024]{1,0:T(8,128)(2,1)S(1)} collective-permute-done((bf16[96,1024]{1,0:T(8,128)(2,1)S(1)}, bf16[96,1024]{1,0:T(8,128)(2,1)S(1)}, u32[]{:S(2)}, u32[]{:S(2)}) %collective-permute-start.7) | collective-permute-done | bytes 196640 | tf_op jit(solution)/shard_map/ppermute | solution.py:192
  23.8 1.9 %collective-permute-start.4 = (bf16[96,1024]{1,0:T(8,128)(2,1)S(1)}, bf16[96,1024]{1,0:T(8,128)(2,1)S(1)}, u32[]{:S(2)}, u32[]{:S(2)}) collective-permute-start(bf16[96,1024]{1,0:T(8,128)(2,1)S(1)} %get-tuple-element.21), channel_id=1, source_target_pairs={{0,16},{1,17},{2,18},{3,19},{4,20},{5,21},{6,22},{7,23},{8,24},{9,... | collective-permute-start | bytes 589832 | tf_op jit(solution)/shard_map/ppermute | solution.py:192
  25.9 2.6 %collective-permute-done.2 = bf16[96,1024]{1,0:T(8,128)(2,1)S(1)} collective-permute-done((bf16[96,1024]{1,0:T(8,128)(2,1)S(1)}, bf16[96,1024]{1,0:T(8,128)(2,1)S(1)}, u32[]{:S(2)}, u32[]{:S(2)}) %collective-permute-start.2) | collective-permute-done | bytes 196640 | tf_op jit(solution)/shard_map/ppermute | solution.py:192
  28.8 1.1 %collective-permute-done.4 = bf16[96,1024]{1,0:T(8,128)(2,1)S(1)} collective-permute-done((bf16[96,1024]{1,0:T(8,128)(2,1)S(1)}, bf16[96,1024]{1,0:T(8,128)(2,1)S(1)}, u32[]{:S(2)}, u32[]{:S(2)}) %collective-permute-start.4) | collective-permute-done | bytes 196640 | tf_op jit(solution)/shard_map/ppermute | solution.py:192
  30.0 0.7 %pad_add_fusion.place_ref = s32[2]{0:T(128)S(1)} fusion(s32[1]{0:T(128)} %bitcast.1, s32[1]{0:T(128)} %bitcast), kind=kLoop, calls=%fused_computation.59 | loop fusion | flops 2 | bytes 16 | tf_op jit(solution)/shard_map/stack | solution.py:214
  32.6 0.6 %fusion.8 = (s32[1]{0:T(128)}, s32[1]{0:T(128)}) fusion(s32[2]{0:T(128)S(1)} %get-tuple-element.31), kind=kLoop, calls=%fused_computation.65 | loop fusion | bytes 16 | tf_op jit(solution)/shard_map/slice | solution.py:210
  33.2 0.7 %copy-done.4 = s32[1,384]{1,0:T(1,128)S(1)} copy-done((s32[1,384]{1,0:T(1,128)S(1)}, s32[1,384]{1,0:T(1,128)}, u32[]{:S(2)}) %copy-start.4) | copy-done | bytes 1560
  33.9 1.3 %compare_select_fusion = (f32[1,384]{1,0:T(1,128)S(1)}, f32[1,384]{1,0:T(1,128)S(1)}, f32[1,384]{1,0:T(1,128)S(1)}, f32[1,384]{1,0:T(1,128)S(1)}) fusion(s32[1,384]{1,0:T(1,128)S(1)} %copy-done.3, s32[1,384]{1,0:T(1,128)S(1)} %copy-done.4, s32[]{:T(128)} %bitcast.3, s32[]{:T(128)} %bitcast.2, s32[]{:T(128)S(6)} %add.40, s32[1,384]{1,0:T(1,128)S(1)} %copy-done.5, ...), kind=kLoop, calls=%fused_computation.14 | loop fusion | flops 43008 | bytes 13836 | tf_op jit(solution)/shard_map/jit(_where)/select_n | solution.py:211
  35.3 3.1 %shard_map.136 = (f32[1152,1]{1,0:T(8,128)S(1)}, f32[1152,1]{1,0:T(8,128)S(1)}, f32[1152,128]{1,0:T(8,128)S(1)}) custom-call(s32[2]{0:T(128)S(1)} %pad_add_fusion.place_ref, bf16[48,3072]{1,0:T(8,128)(2,1)S(1)} %copy-done.1, bf16[384,1024]{1,0:T(8,128)(2,1)S(1)} %constant_dynamic-update-slice_fusion.9.refs_0_, ...), custom_call_target="tpu_custom_call" | custom-call | flops 452984832 | bytes 1572864 | tf_op jit(solution)/shard_map/pallas_call | solution.py:102
  38.4 2.4 %shard_map.137 = (f32[1152,1]{1,0:T(8,128)S(1)}, f32[1152,1]{1,0:T(8,128)S(1)}, f32[1152,128]{1,0:T(8,128)S(1)}) custom-call(s32[2]{0:T(128)S(1)} %pad_add_fusion.place_ref, bf16[48,3072]{1,0:T(8,128)(2,1)S(1)} %copy-done.1, bf16[384,1024]{1,0:T(8,128)(2,1)S(1)} %constant_dynamic-update-slice_fusion.2.refs_0_, f32[1,384]{1,0:T(1,128)S(1)} %get-tuple-element.26.refs_1_, ...), custom_call_target="tpu_custom_call" | custom-call | flops 226492416 | bytes 786432 | tf_op jit(solution)/shard_map/pallas_call | solution.py:102
  40.8 3.6 %shard_map.138 = bf16[48,3072]{1,0:T(8,128)(2,1)} custom-call(s32[2]{0:T(128)S(1)} %pad_add_fusion.place_ref, bf16[48,3072]{1,0:T(8,128)(2,1)S(1)} %copy-done.1, bf16[384,1024]{1,0:T(8,128)(2,1)} %collective-permute-done.5.refs_0_, f32[1,384]{1,0:T(1,128)S(1)} %get-tuple-element.27.refs_1_, f32[1152,1]{1,0:T(8,128)S(1)} %get-tuple-element.14.refs_2_, ...), custom_call_target="tpu_custom_call" | custom-call | flops 226492416 | bytes 786432 | tf_op jit(solution)/shard_map/pallas_call | solution.py:102
  (37 shorter events, 0.6 us)
Async XLA Ops:
  0.0 35.2 %copy-start = (f32[64,3072]{1,0:T(8,128)S(1)}, f32[64,3072]{1,0:T(8,128)}, u32[]{:S(2)}) copy-start(f32[64,3072]{1,0:T(8,128)} %param.19) | copy-start | bytes 2359300
  0.0 9.8 %collective-permute-start.6 = (bf16[48,1024]{1,0:T(8,128)(2,1)}, bf16[48,1024]{1,0:T(8,128)(2,1)S(1)}, u32[]{:S(2)}, u32[]{:S(2)}) collective-permute-start(bf16[48,1024]{1,0:T(8,128)(2,1)} %param.15), channel_id=1, source_target_pairs={{0,4},{1,5},{2,6},{3,7},{4,0},{5,1},{6,2},{7,3},{8,12},{9,13},{10,... | collective-permute-start | bytes 294920 | tf_op jit(solution)/shard_map/ppermute | solution.py:192
  3.0 10.6 %collective-permute-start = (bf16[48,1024]{1,0:T(8,128)(2,1)}, bf16[48,1024]{1,0:T(8,128)(2,1)S(1)}, u32[]{:S(2)}, u32[]{:S(2)}) collective-permute-start(bf16[48,1024]{1,0:T(8,128)(2,1)} %param.15), channel_id=1, source_target_pairs={{0,8},{1,9},{2,10},{3,11},{4,12},{5,13},{6,14},{7,15},{8,0},{9,1},... | collective-permute-start | bytes 294920 | tf_op jit(solution)/shard_map/ppermute | solution.py:192
  5.6 8.1 %collective-permute-start.1 = (bf16[48,1024]{1,0:T(8,128)(2,1)}, bf16[48,1024]{1,0:T(8,128)(2,1)S(1)}, u32[]{:S(2)}, u32[]{:S(2)}) collective-permute-start(bf16[48,1024]{1,0:T(8,128)(2,1)} %param.15), channel_id=1, source_target_pairs={{0,12},{1,13},{2,14},{3,15},{4,8},{5,9},{6,10},{7,11},{8,4},{9,5},... | collective-permute-start | bytes 294920 | tf_op jit(solution)/shard_map/ppermute | solution.py:192
  5.6 0.7 %copy-start.8 = (s32[2]{0:T(128)S(1)}, s32[2]{0:T(128)}, u32[]{:S(2)}) copy-start(s32[2]{0:T(128)} %param.16) | copy-start | bytes 28
  6.9 0.7 %copy-start.7 = (s32[2]{0:T(128)S(1)}, s32[2]{0:T(128)}, u32[]{:S(2)}) copy-start(s32[2]{0:T(128)} %param.18) | copy-start | bytes 28
  6.9 0.7 %copy-start.9 = (s32[2]{0:T(128)S(1)}, s32[2]{0:T(128)}, u32[]{:S(2)}) copy-start(s32[2]{0:T(128)} %param.17) | copy-start | bytes 28
  9.9 13.9 %collective-permute-start.7 = (bf16[96,1024]{1,0:T(8,128)(2,1)S(1)}, bf16[96,1024]{1,0:T(8,128)(2,1)S(1)}, u32[]{:S(2)}, u32[]{:S(2)}) collective-permute-start(bf16[96,1024]{1,0:T(8,128)(2,1)S(1)} %get-tuple-element.17), channel_id=1, source_target_pairs={{0,2},{1,3},{2,0},{3,1},{4,6},{5,7},{6,4},{7,5},{8,10},{9,11},{10,... | collective-permute-start | bytes 589832 | tf_op jit(solution)/shard_map/ppermute | solution.py:192
  11.7 14.0 %collective-permute-start.8 = (bf16[96,1024]{1,0:T(8,128)(2,1)S(1)}, bf16[96,1024]{1,0:T(8,128)(2,1)S(1)}, u32[]{:S(2)}, u32[]{:S(2)}) collective-permute-start(bf16[96,1024]{1,0:T(8,128)(2,1)S(1)} %get-tuple-element.17), channel_id=1, source_target_pairs={{0,18},{1,19},{2,16},{3,17},{4,22},{5,23},{6,20},{7,21},{8,26},{9,... | collective-permute-start | bytes 589832 | tf_op jit(solution)/shard_map/ppermute | solution.py:192
  13.1 12.6 %collective-permute-start.9 = (bf16[96,1024]{1,0:T(8,128)(2,1)S(1)}, bf16[96,1024]{1,0:T(8,128)(2,1)S(1)}, u32[]{:S(2)}, u32[]{:S(2)}) collective-permute-start(bf16[96,1024]{1,0:T(8,128)(2,1)S(1)} %get-tuple-element.17), channel_id=1, source_target_pairs={{0,16},{1,17},{2,18},{3,19},{4,20},{5,21},{6,22},{7,23},{8,24},{9,... | collective-permute-start | bytes 589832 | tf_op jit(solution)/shard_map/ppermute | solution.py:192
  13.7 14.7 %collective-permute-start.2 = (bf16[96,1024]{1,0:T(8,128)(2,1)S(1)}, bf16[96,1024]{1,0:T(8,128)(2,1)S(1)}, u32[]{:S(2)}, u32[]{:S(2)}) collective-permute-start(bf16[96,1024]{1,0:T(8,128)(2,1)S(1)} %get-tuple-element.21), channel_id=1, source_target_pairs={{0,2},{1,3},{2,0},{3,1},{4,6},{5,7},{6,4},{7,5},{8,10},{9,11},{10,... | collective-permute-start | bytes 589832 | tf_op jit(solution)/shard_map/ppermute | solution.py:192
  15.3 13.4 %collective-permute-start.3 = (bf16[96,1024]{1,0:T(8,128)(2,1)S(1)}, bf16[96,1024]{1,0:T(8,128)(2,1)S(1)}, u32[]{:S(2)}, u32[]{:S(2)}) collective-permute-start(bf16[96,1024]{1,0:T(8,128)(2,1)S(1)} %get-tuple-element.21), channel_id=1, source_target_pairs={{0,18},{1,19},{2,16},{3,17},{4,22},{5,23},{6,20},{7,21},{8,26},{9,... | collective-permute-start | bytes 589832 | tf_op jit(solution)/shard_map/ppermute | solution.py:192
  23.8 6.1 %collective-permute-start.4 = (bf16[96,1024]{1,0:T(8,128)(2,1)S(1)}, bf16[96,1024]{1,0:T(8,128)(2,1)S(1)}, u32[]{:S(2)}, u32[]{:S(2)}) collective-permute-start(bf16[96,1024]{1,0:T(8,128)(2,1)S(1)} %get-tuple-element.21), channel_id=1, source_target_pairs={{0,16},{1,17},{2,18},{3,19},{4,20},{5,21},{6,22},{7,23},{8,24},{9,... | collective-permute-start | bytes 589832 | tf_op jit(solution)/shard_map/ppermute | solution.py:192
  25.8 9.5 %collective-permute-start.10 = (bf16[384,1024]{1,0:T(8,128)(2,1)S(1)}, bf16[384,1024]{1,0:T(8,128)(2,1)S(1)}, u32[]{:S(2)}, u32[]{:S(2)}) collective-permute-start(bf16[384,1024]{1,0:T(8,128)(2,1)S(1)} %constant_dynamic-update-slice_fusion.9.refs_0_), channel_id=1, source_target_pairs={{0,1},{1,0},{2,3},{3,2},{4,5},{5,4},{6,7},{7,6},{8,9},{9,8},{10,11... | collective-permute-start | bytes 2359304 | tf_op jit(solution)/shard_map/ppermute | solution.py:192
  28.7 6.5 %copy-start.1 = (bf16[48,3072]{1,0:T(8,128)(2,1)S(1)}, bf16[48,3072]{1,0:T(8,128)(2,1)}, u32[]{:S(2)}) copy-start(bf16[48,3072]{1,0:T(8,128)(2,1)} %q_ref.5) | copy-start | bytes 884740
  29.9 3.3 %copy-start.5 = (s32[1,384]{1,0:T(1,128)S(1)}, s32[1,384]{1,0:T(1,128)}, u32[]{:S(2)}) copy-start(s32[1,384]{1,0:T(1,128)} %constant.98.clone) | copy-start | bytes 4612
  29.9 3.3 %copy-start.6 = (s32[1,384]{1,0:T(1,128)S(1)}, s32[1,384]{1,0:T(1,128)}, u32[]{:S(2)}) copy-start(s32[1,384]{1,0:T(1,128)} %constant.99.clone) | copy-start | bytes 4612
  29.9 10.9 %collective-permute-start.5 = (bf16[384,1024]{1,0:T(8,128)(2,1)S(1)}, bf16[384,1024]{1,0:T(8,128)(2,1)}, u32[]{:S(2)}, u32[]{:S(2)}) collective-permute-start(bf16[384,1024]{1,0:T(8,128)(2,1)S(1)} %constant_dynamic-update-slice_fusion.2.refs_0_), channel_id=1, source_target_pairs={{0,1},{1,0},{2,3},{3,2},{4,5},{5,4},{6,7},{7,6},{8,9},{9,8},{10,11... | collective-permute-start | bytes 2359304 | tf_op jit(solution)/shard_map/ppermute | solution.py:192
  33.2 0.7 %copy-start.4 = (s32[1,384]{1,0:T(1,128)S(1)}, s32[1,384]{1,0:T(1,128)}, u32[]{:S(2)}) copy-start(s32[1,384]{1,0:T(1,128)} %constant.97.clone) | copy-start | bytes 4612
  33.2 0.7 %copy-start.2 = (s32[1,384]{1,0:T(1,128)S(1)}, s32[1,384]{1,0:T(1,128)}, u32[]{:S(2)}) copy-start(s32[1,384]{1,0:T(1,128)} %constant.95.clone) | copy-start | bytes 4612
  33.2 0.7 %copy-start.3 = (s32[1,384]{1,0:T(1,128)S(1)}, s32[1,384]{1,0:T(1,128)}, u32[]{:S(2)}) copy-start(s32[1,384]{1,0:T(1,128)} %constant.96.clone) | copy-start | bytes 4612

commit v2 on v1

v2 whole, which is shorter than its diff:
```python
import functools
import math

import jax
import jax.numpy as jnp
import numpy as np
from jax import lax
from jax.experimental import pallas as pl
from jax.experimental.pallas import tpu as pltpu
from jax.sharding import PartitionSpec as P

QUERY_HEADS = 24
KEY_VALUE_HEADS = 4
HEAD_WIDTH = 128
RATIO = QUERY_HEADS // KEY_VALUE_HEADS
KEY_WIDTH = KEY_VALUE_HEADS * HEAD_WIDTH
NEGATIVE = -1e30
LOG2E = math.log2(math.e)
TILE = 384
MOST_PARTNERS = 3
GATE_ROWS = 8


def key_bias(distances, tokens, n_seq, clip_ref, valid_ref):
    span_id = lax.axis_index("span")
    me = span_id * n_seq + lax.axis_index("seq")
    lane = lax.broadcasted_iota(jnp.int32, (1, len(distances) * tokens), 1)
    bound = jnp.zeros_like(lane)
    for i, distance in enumerate(distances):
        source = me ^ distance
        group = source // n_seq
        limit = jnp.where(clip_ref[group] <= clip_ref[span_id], valid_ref[group], 0)
        usable = jnp.minimum(limit - (source % n_seq) * tokens, tokens)
        bound = jnp.where(lane >= i * tokens, i * tokens + usable, bound)
    return jnp.where(lane < bound, 0.0, NEGATIVE).astype(jnp.float32)


def attend_kernel(orders, stage, n_seq, clip_ref, valid_ref, step_ref, q_ref, *refs):
    kv_refs, refs = refs[: len(orders)], refs[len(orders) :]
    opens, closes = stage == "first", stage == "last"
    tokens = q_ref.shape[0]
    rows = RATIO * tokens
    scale = LOG2E / math.sqrt(HEAD_WIDTH)
    heads = range(KEY_VALUE_HEADS)
    columns = [slice(h * HEAD_WIDTH, (h + 1) * HEAD_WIDTH) for h in range(QUERY_HEADS)]
    if opens:
        table_ref, top_out, part_out, gate_out, gate_ref, gate_sem = refs
        step = step_ref[lax.axis_index("span")]
        first = pl.multiple_of(step - step % GATE_ROWS, GATE_ROWS)
        fetch = pltpu.make_async_copy(table_ref.at[pl.ds(first, GATE_ROWS)], gate_ref, gate_sem)
        fetch.start()
    elif closes:
        top_in, part_in, gate_ref, out_ref, staged_ref, out_sem = refs
        position = lax.axis_index("seq") * tokens + lax.broadcasted_iota(jnp.int32, (tokens, 1), 0)
        live = (position < valid_ref[lax.axis_index("span")]).astype(jnp.float32)
    else:
        top_in, part_in, top_out, part_out = refs
    biases = [key_bias(order, tokens, n_seq, clip_ref, valid_ref) for order in orders]
    scores, tops, writes = {}, {}, []
    for h in heads:
        query = jnp.concatenate([q_ref[:, c] for c in columns[h * RATIO : (h + 1) * RATIO]], axis=0)
        for i, kv_ref in enumerate(kv_refs):
            products = lax.dot_general(
                query, kv_ref[:, columns[h]], (((1,), (1,)), ((), ())), preferred_element_type=jnp.float32
            )
            scores[h, i] = products * scale + biases[i]
    for h in heads:
        found = [jnp.max(scores[h, i], axis=1, keepdims=True) for i in range(len(orders))]
        top = jnp.broadcast_to(functools.reduce(jnp.maximum, found), (rows, HEAD_WIDTH))
        tops[h] = top if opens else jnp.maximum(top, top_in[h * rows : (h + 1) * rows, :])
    for h in heads:
        span = slice(h * rows, (h + 1) * rows)
        total, numerator = jnp.zeros((rows, HEAD_WIDTH), jnp.float32), 0.0
        for i, kv_ref in enumerate(kv_refs):
            repeats = scores[h, i].shape[1] // HEAD_WIDTH
            weights = jnp.exp2(scores[h, i] - jnp.concatenate([tops[h]] * repeats, axis=1))
            total = total + jnp.sum(weights, axis=1, keepdims=True)
            numerator = numerator + jnp.dot(
                weights.astype(jnp.bfloat16),
                kv_ref[:, columns[KEY_VALUE_HEADS + h]],
                preferred_element_type=jnp.float32,
            )
        if not opens:
            factor = jnp.exp2(top_in[span, :] - tops[h])
            total = total + factor
            numerator = numerator + part_in[span, :] * factor
        result = numerator * (1.0 / total)
        if not closes:
            top_out[span, :] = tops[h] + jnp.log2(total)
            part_out[span, :] = result
            continue
        for r in range(RATIO):
            c = columns[h * RATIO + r]
            staged_ref[:, c] = (result[r * tokens : (r + 1) * tokens] * gate_ref[:, c] * live).astype(
                out_ref.dtype
            )
        group = slice(h * RATIO * HEAD_WIDTH, (h + 1) * RATIO * HEAD_WIDTH)
        writes.append(pltpu.make_async_copy(staged_ref.at[:, group], out_ref.at[:, group], out_sem.at[h]))
        writes[-1].start()
    if opens:
        fetch.wait()
        chosen = lax.broadcasted_iota(jnp.int32, (GATE_ROWS, 1), 0) == step % GATE_ROWS
        gate_out[...] = jnp.sum(jnp.where(chosen, gate_ref[...], 0.0), axis=0, keepdims=True)
    for write in writes:
        write.wait()


def attend(scalars, queries, keyvals, orders, n_seq, stage, *carried):
    rows = QUERY_HEADS * queries.shape[0]
    keys = sum(kv.shape[0] for kv in keyvals)
    smem, vmem = pl.BlockSpec(memory_space=pltpu.SMEM), pl.BlockSpec(memory_space=pltpu.VMEM)
    anywhere = pl.BlockSpec(memory_space=pl.ANY)
    operands = [queries, *keyvals, *carried]
    in_specs = [smem] * len(scalars) + [vmem] * len(operands)
    scratch = []
    if stage == "last":
        out_shape, out_specs = jax.ShapeDtypeStruct(queries.shape, jnp.bfloat16), anywhere
        scratch = [
            pltpu.VMEM(queries.shape, jnp.bfloat16),
            pltpu.SemaphoreType.DMA((KEY_VALUE_HEADS,)),
        ]
    else:
        out_shape = [jax.ShapeDtypeStruct((rows, HEAD_WIDTH), jnp.float32)] * 2
        out_specs = [vmem, vmem]
    if stage == "first":
        in_specs[-1] = anywhere
        out_shape.append(jax.ShapeDtypeStruct((1, queries.shape[1]), jnp.float32))
        out_specs.append(vmem)
        scratch = [pltpu.VMEM((GATE_ROWS, queries.shape[1]), jnp.float32), pltpu.SemaphoreType.DMA]
    return pl.pallas_call(
        functools.partial(attend_kernel, orders, stage, n_seq),
        out_shape=out_shape,
        in_specs=in_specs,
        out_specs=out_specs,
        scratch_shapes=scratch,
        compiler_params=pltpu.CompilerParams(vmem_limit_bytes=40 * 1024 * 1024),
        cost_estimate=pl.CostEstimate(
            flops=4 * rows * keys * HEAD_WIDTH,
            bytes_accessed=keys * 2 * KEY_WIDTH * 2,
            transcendentals=rows * keys,
        ),
    )(*scalars, *operands)


def streamed_kernel(place_ref, q_ref, kv_ref, bias_ref, gate_ref, out_ref, top_ref, total_ref, numerator_ref):
    tokens = q_ref.shape[0]
    rows = RATIO * tokens
    scale = LOG2E / math.sqrt(HEAD_WIDTH)

    @pl.when(pl.program_id(0) == 0)
    def _():
        top_ref[...] = jnp.full_like(top_ref, NEGATIVE)
        total_ref[...] = jnp.zeros_like(total_ref)
        numerator_ref[...] = jnp.zeros_like(numerator_ref)

    for head in range(KEY_VALUE_HEADS):
        first = head * RATIO
        span = slice(head * rows, (head + 1) * rows)
        columns = [slice((first + r) * HEAD_WIDTH, (first + r + 1) * HEAD_WIDTH) for r in range(RATIO)]
        query = jnp.concatenate([q_ref[:, c] for c in columns], axis=0)
        key = kv_ref[:, head * HEAD_WIDTH : (head + 1) * HEAD_WIDTH]
        value = kv_ref[:, KEY_WIDTH + head * HEAD_WIDTH : KEY_WIDTH + (head + 1) * HEAD_WIDTH]
        scores = lax.dot_general(
            query, key, (((1,), (1,)), ((), ())), preferred_element_type=jnp.float32
        )
        scores = scores * scale + bias_ref[...]
        top = jnp.maximum(top_ref[span, :], jnp.max(scores, axis=1, keepdims=True))
        weights = jnp.exp2(scores - top)
        factor = jnp.exp2(top_ref[span, :] - top)
        top_ref[span, :] = top
        total_ref[span, :] = total_ref[span, :] * factor + jnp.sum(weights, axis=1, keepdims=True)
        numerator_ref[span, :] = numerator_ref[span, :] * factor + jnp.dot(
            weights.astype(jnp.bfloat16), value, preferred_element_type=jnp.float32
        )

    @pl.when(pl.program_id(0) == pl.num_programs(0) - 1)
    def _():
        positions = place_ref[0] + lax.broadcasted_iota(jnp.int32, (tokens, 1), 0)
        live = (positions < place_ref[1]).astype(jnp.float32)
        for h in range(QUERY_HEADS):
            span = slice(h * tokens, (h + 1) * tokens)
            columns = slice(h * HEAD_WIDTH, (h + 1) * HEAD_WIDTH)
            part = numerator_ref[span, :] / total_ref[span, :]
            out_ref[:, columns] = (part * gate_ref[:, columns] * live).astype(out_ref.dtype)


def streamed(place, queries, keyvals, bias, gate):
    rows = QUERY_HEADS * queries.shape[0]
    keys = keyvals.shape[0]
    tile = TILE if keys % TILE == 0 else keys
    whole = pl.BlockSpec(memory_space=pltpu.VMEM)
    return pl.pallas_call(
        streamed_kernel,
        grid=(keys // tile,),
        out_shape=jax.ShapeDtypeStruct(queries.shape, jnp.bfloat16),
        in_specs=[
            pl.BlockSpec(memory_space=pltpu.SMEM),
            whole,
            pl.BlockSpec((tile, keyvals.shape[1]), lambda t: (t, 0)),
            pl.BlockSpec((1, tile), lambda t: (0, t)),
            whole,
        ],
        out_specs=whole,
        scratch_shapes=[
            pltpu.VMEM((rows, 1), jnp.float32),
            pltpu.VMEM((rows, 1), jnp.float32),
            pltpu.VMEM((rows, HEAD_WIDTH), jnp.float32),
        ],
        compiler_params=pltpu.CompilerParams(vmem_limit_bytes=40 * 1024 * 1024),
    )(place, queries, keyvals, bias, gate)


def gathered_whole(n_span, n_seq, queries, keyvals, clip_index, noise_step, valid_count, gate_table):
    tokens = queries.shape[0]
    span_id, seq_id = lax.axis_index("span"), lax.axis_index("seq")
    groups = jnp.arange(n_span, dtype=jnp.int32)
    own = lambda values: jnp.sum(jnp.where(groups == span_id, values, 0))
    limits = jnp.where(clip_index <= own(clip_index), valid_count, 0)
    usable = jnp.arange(n_seq * tokens, dtype=jnp.int32)[None, :] < limits[:, None]
    bias = jnp.where(usable, 0.0, NEGATIVE).astype(jnp.float32).reshape(1, -1)
    gate = lax.dynamic_slice(gate_table, (own(noise_step), 0), (1, gate_table.shape[1]))
    place = jnp.stack([seq_id * tokens, own(valid_count)])
    rows = lax.all_gather(lax.all_gather(keyvals, "seq", tiled=True), "span", tiled=True)
    return streamed(place, queries, rows, bias, gate)


def per_device(n_span, n_seq, queries, keyvals, clip_index, noise_step, valid_count, gate_table):
    devices = n_span * n_seq
    far = [4 * i for i in range(n_seq // 4)]
    plane = [2] + [s * n_seq + y for s in range(1, n_span) for y in (2, 0)]
    if len(far) not in (2, 4) or len(plane) > MOST_PARTNERS or devices & (devices - 1):
        return gathered_whole(
            n_span, n_seq, queries, keyvals, clip_index, noise_step, valid_count, gate_table
        )

    def exchange(block, distance):
        pairs = [(i, i ^ distance) for i in range(devices)]
        return lax.ppermute(block, ("span", "seq"), pairs)

    scalars = (clip_index, valid_count, noise_step)
    ob = lax.optimization_barrier
    cat = lambda xs: jnp.concatenate(xs, axis=0)
    half = len(far) // 2
    nearz, farz = far[:half], far[half:]
    orders = [[p ^ d for p in [0] + plane for d in part] for part in (nearz, farz)]
    twins = [[d ^ 1 for d in o] for o in orders]
    z={0:keyvals}
    for d in far[1:]: z[d]=exchange(keyvals,d)
    p1=cat([z[d] for d in nearz]); p2=cat([z[d] for d in farz])
    near=cat([p1]+[exchange(p1,d) for d in plane])
    away=cat([p2]+[exchange(p2,d) for d in plane])
    nt=exchange(near,1)
    *st,gate=attend(scalars,queries,[near,nt],[orders[0],twins[0]],n_seq,"first",gate_table)
    at=exchange(away,1)
    st=attend(scalars,queries,[away],[orders[1]],n_seq,"middle",*st)
    return attend(scalars,queries,[at],[twins[1]],n_seq,"last",*st,gate)


def solution(mesh):
    return jax.shard_map(
        functools.partial(per_device, mesh.shape["span"], mesh.shape["seq"]),
        mesh=mesh,
        in_specs=(P(("span", "seq"), None), P(("span", "seq"), None), P(), P(), P(), P()),
        out_specs=P(("span", "seq"), None),
        check_vma=False,
    )
```

time: 44.7 us -> 33.2 us (0.74)
  other arithmetic: 3.99 us -> 0 us
  Pallas kernels: 9.06 us -> 6.17 us
  local copies, waits for them, and re-layouts: 3.68 us -> 1.13 us
  between operations: 2.11 us -> 0.22 us
    pallas_call x3, Pallas kernels: 9.06 us -> 6.17 us  [attend(): pl.pallas_call(functools.partial(attend_kernel, orders, stage, n_seq), ou...]
    select_n x2 -> x0, other arithmetic: 2.66 us -> none  [the longest x1 1.34 us: per_device(): limits = jnp.where(clip_index <= own_clip, valid_count, 0)]
    unnamed x26 -> x16, local copies, waits for them, and re-layouts: 3.01 us -> 1.07 us
    another operation x1 -> x0, other arithmetic: 0.69 us -> none  [per_device(): place = jnp.stack([seq_id * tokens, own_count])]
    reduce_sum x1 -> x0, other arithmetic: 0.63 us -> none  [per_device(): own = lambda values: jnp.sum(jnp.where(groups == span_id, values, 0))]
    slice x1 -> x0, local copies, waits for them, and re-layouts: 0.58 us -> none  [bias_of(): limit = jnp.where(group == g, limits[g], limit)]
  transfers between devices with their start and end apart: 11 -> 11, of which waited for: 5 -> 5; matrix products, arithmetic and copies ran while one was open for 13% -> 3% of each run, Pallas kernels for 12% -> 12%
where the time goes in v2:
time: 33.2 us; the launch traced here: 33 us
  starting transfers between devices  13.8 us (42%)
  waiting for transfers between devices  11.7 us (35%)
  Pallas kernels  6.17 us (19%)
  local copies, waits for them, and re-layouts  1.13 us (3%)
    ppermute x11, starting transfers between devices, exchange(): return lax.ppermute(block, ('span', 'seq'), pairs)  13.8 us
    ppermute x11, waiting for transfers between devices, exchange(): return lax.ppermute(block, ('span', 'seq'), pairs)  11.7 us
    pallas_call x3, Pallas kernels, attend(): pl.pallas_call(functools.partial(attend_kernel, orders, stage, n_seq), ou...  6.17 us
    unnamed x16, local copies, waits for them, and re-layouts  1.07 us
  transfers between devices with their start and end apart: 11, of which 5 were waited for; matrix products, arithmetic and copies ran while one was open for 3% of the time, Pallas kernels for 12%

profile of v2, /device:TPU:0, one launch (start us, length us, event | category | flops | bytes accessed | tf_op | source)
XLA Modules:
  0.0 33.0 jit_solution(15393398357794967552)
XLA Ops:
  0.0 3.0 %collective-permute-start.6 = (bf16[48,1024]{1,0:T(8,128)(2,1)}, bf16[48,1024]{1,0:T(8,128)(2,1)S(1)}, u32[]{:S(2)}, u32[]{:S(2)}) collective-permute-start(bf16[48,1024]{1,0:T(8,128)(2,1)} %param.7), channel_id=1, source_target_pairs={{0,4},{1,5},{2,6},{3,7},{4,0},{5,1},{6,2},{7,3},{8,12},{9,13},{10,... | collective-permute-start | bytes 294920 | tf_op jit(solution)/shard_map/ppermute | solution.py:238
  3.0 2.6 %collective-permute-start = (bf16[48,1024]{1,0:T(8,128)(2,1)}, bf16[48,1024]{1,0:T(8,128)(2,1)S(1)}, u32[]{:S(2)}, u32[]{:S(2)}) collective-permute-start(bf16[48,1024]{1,0:T(8,128)(2,1)} %param.7), channel_id=1, source_target_pairs={{0,8},{1,9},{2,10},{3,11},{4,12},{5,13},{6,14},{7,15},{8,0},{9,1},... | collective-permute-start | bytes 294920 | tf_op jit(solution)/shard_map/ppermute | solution.py:238
  5.6 1.0 %constant_dynamic-update-slice_fusion.8 = (bf16[96,1024]{1,0:T(8,128)(2,1)S(1)}, bf16[384,1024]{1,0:T(8,128)(2,1)S(1)}) fusion(bf16[48,1024]{1,0:T(8,128)(2,1)} %param.7), kind=kLoop, calls=%fused_computation.8 | loop fusion | bytes 294912
  6.6 1.8 %collective-permute-start.7 = (bf16[96,1024]{1,0:T(8,128)(2,1)S(1)}, bf16[96,1024]{1,0:T(8,128)(2,1)S(1)}, u32[]{:S(2)}, u32[]{:S(2)}) collective-permute-start(bf16[96,1024]{1,0:T(8,128)(2,1)S(1)} %get-tuple-element.15), channel_id=1, source_target_pairs={{0,2},{1,3},{2,0},{3,1},{4,6},{5,7},{6,4},{7,5},{8,10},{9,11},{10,... | collective-permute-start | bytes 589832 | tf_op jit(solution)/shard_map/ppermute | solution.py:238
  8.4 1.4 %collective-permute-start.8 = (bf16[96,1024]{1,0:T(8,128)(2,1)S(1)}, bf16[96,1024]{1,0:T(8,128)(2,1)S(1)}, u32[]{:S(2)}, u32[]{:S(2)}) collective-permute-start(bf16[96,1024]{1,0:T(8,128)(2,1)S(1)} %get-tuple-element.15), channel_id=1, source_target_pairs={{0,18},{1,19},{2,16},{3,17},{4,22},{5,23},{6,20},{7,21},{8,26},{9,... | collective-permute-start | bytes 589832 | tf_op jit(solution)/shard_map/ppermute | solution.py:238
  9.8 0.3 %collective-permute-start.9 = (bf16[96,1024]{1,0:T(8,128)(2,1)S(1)}, bf16[96,1024]{1,0:T(8,128)(2,1)S(1)}, u32[]{:S(2)}, u32[]{:S(2)}) collective-permute-start(bf16[96,1024]{1,0:T(8,128)(2,1)S(1)} %get-tuple-element.15), channel_id=1, source_target_pairs={{0,16},{1,17},{2,18},{3,19},{4,20},{5,21},{6,22},{7,23},{8,24},{9,... | collective-permute-start | bytes 589832 | tf_op jit(solution)/shard_map/ppermute | solution.py:238
  10.2 3.5 %collective-permute-done = bf16[48,1024]{1,0:T(8,128)(2,1)S(1)} collective-permute-done((bf16[48,1024]{1,0:T(8,128)(2,1)}, bf16[48,1024]{1,0:T(8,128)(2,1)S(1)}, u32[]{:S(2)}, u32[]{:S(2)}) %collective-permute-start) | collective-permute-done | bytes 98336 | tf_op jit(solution)/shard_map/ppermute | solution.py:238
  13.7 1.6 %collective-permute-start.2 = (bf16[96,1024]{1,0:T(8,128)(2,1)S(1)}, bf16[96,1024]{1,0:T(8,128)(2,1)S(1)}, u32[]{:S(2)}, u32[]{:S(2)}) collective-permute-start(bf16[96,1024]{1,0:T(8,128)(2,1)S(1)} %get-tuple-element.19), channel_id=1, source_target_pairs={{0,2},{1,3},{2,0},{3,1},{4,6},{5,7},{6,4},{7,5},{8,10},{9,11},{10,... | collective-permute-start | bytes 589832 | tf_op jit(solution)/shard_map/ppermute | solution.py:238
  15.3 1.4 %collective-permute-start.3 = (bf16[96,1024]{1,0:T(8,128)(2,1)S(1)}, bf16[96,1024]{1,0:T(8,128)(2,1)S(1)}, u32[]{:S(2)}, u32[]{:S(2)}) collective-permute-start(bf16[96,1024]{1,0:T(8,128)(2,1)S(1)} %get-tuple-element.19), channel_id=1, source_target_pairs={{0,18},{1,19},{2,16},{3,17},{4,22},{5,23},{6,20},{7,21},{8,26},{9,... | collective-permute-start | bytes 589832 | tf_op jit(solution)/shard_map/ppermute | solution.py:238
  16.7 2.6 %collective-permute-done.7 = bf16[96,1024]{1,0:T(8,128)(2,1)S(1)} collective-permute-done((bf16[96,1024]{1,0:T(8,128)(2,1)S(1)}, bf16[96,1024]{1,0:T(8,128)(2,1)S(1)}, u32[]{:S(2)}, u32[]{:S(2)}) %collective-permute-start.7) | collective-permute-done | bytes 196640 | tf_op jit(solution)/shard_map/ppermute | solution.py:238
  19.4 1.5 %collective-permute-start.4 = (bf16[96,1024]{1,0:T(8,128)(2,1)S(1)}, bf16[96,1024]{1,0:T(8,128)(2,1)S(1)}, u32[]{:S(2)}, u32[]{:S(2)}) collective-permute-start(bf16[96,1024]{1,0:T(8,128)(2,1)S(1)} %get-tuple-element.19), channel_id=1, source_target_pairs={{0,16},{1,17},{2,18},{3,19},{4,20},{5,21},{6,22},{7,23},{8,24},{9,... | collective-permute-start | bytes 589832 | tf_op jit(solution)/shard_map/ppermute | solution.py:238
  20.9 0.0 copy-start.1
  21.0 0.1 collective-permute-start.10
  21.1 4.2 %collective-permute-done.2 = bf16[96,1024]{1,0:T(8,128)(2,1)S(1)} collective-permute-done((bf16[96,1024]{1,0:T(8,128)(2,1)S(1)}, bf16[96,1024]{1,0:T(8,128)(2,1)S(1)}, u32[]{:S(2)}, u32[]{:S(2)}) %collective-permute-start.2) | collective-permute-done | bytes 196640 | tf_op jit(solution)/shard_map/ppermute | solution.py:238
  25.3 0.2 collective-permute-done.3
  25.5 0.0 copy-start
  25.5 0.0 copy-start.2
  25.5 0.0 copy-start.3
  25.5 0.0 copy-start.4
  25.6 1.1 %collective-permute-done.4 = bf16[96,1024]{1,0:T(8,128)(2,1)S(1)} collective-permute-done((bf16[96,1024]{1,0:T(8,128)(2,1)S(1)}, bf16[96,1024]{1,0:T(8,128)(2,1)S(1)}, u32[]{:S(2)}, u32[]{:S(2)}) %collective-permute-start.4) | collective-permute-done | bytes 196640 | tf_op jit(solution)/shard_map/ppermute | solution.py:238
  26.7 0.1 collective-permute-start.5
  26.8 2.4 %shard_map.64 = (f32[1152,128]{1,0:T(8,128)S(1)}, f32[1152,128]{1,0:T(8,128)S(1)}, f32[1,3072]{1,0:T(1,128)S(1)}) custom-call(s32[2]{0:T(128)S(1)} %copy-done.2, s32[2]{0:T(128)S(1)} %copy-done.3, s32[2]{0:T(128)S(1)} %copy-done.4, bf16[48,3072]{1,0:T(8,128)(2,1)S(1)} %copy-done, bf16[384,1024]{1,0:T(8,128)(2,1)S(1)} %constant_dynamic-update-slice_fusion.9.refs_0_, ...), custom_call_target="tpu_custom_call" | custom-call | flops 452984832 | bytes 1572864 | tf_op jit(solution)/shard_map/pallas_call | solution.py:130
  29.2 1.6 %shard_map.65 = (f32[1152,128]{1,0:T(8,128)S(1)}, f32[1152,128]{1,0:T(8,128)S(1)}) custom-call(s32[2]{0:T(128)S(1)} %copy-done.2, s32[2]{0:T(128)S(1)} %copy-done.3, s32[2]{0:T(128)S(1)} %copy-done.4, bf16[48,3072]{1,0:T(8,128)(2,1)S(1)} %copy-done, bf16[384,1024]{1,0:T(8,128)(2,1)S(1)} %constant_dynamic-update-slice_fusion.2.refs_0_, ...), custom_call_target="tpu_custom_call" | custom-call | flops 226492416 | bytes 786432 | tf_op jit(solution)/shard_map/pallas_call | solution.py:130
  30.8 2.2 %shard_map.66 = bf16[48,3072]{1,0:T(8,128)(2,1)} custom-call(s32[2]{0:T(128)S(1)} %copy-done.2, s32[2]{0:T(128)S(1)} %copy-done.3, s32[2]{0:T(128)S(1)} %copy-done.4, bf16[48,3072]{1,0:T(8,128)(2,1)S(1)} %copy-done, bf16[384,1024]{1,0:T(8,128)(2,1)S(1)} %collective-permute-done.5.refs_0_, f32[1152,128]{1,0:T(8,128)S(1)} %get-tuple-element.12.refs_1_, ...), custom_call_target="tpu_custom_call" | custom-call | flops 226492416 | bytes 786432 | tf_op jit(solution)/shard_map/pallas_call | solution.py:130
  (21 shorter events, 0.2 us)
Async XLA Ops:
  0.0 6.6 %collective-permute-start.6 = (bf16[48,1024]{1,0:T(8,128)(2,1)}, bf16[48,1024]{1,0:T(8,128)(2,1)S(1)}, u32[]{:S(2)}, u32[]{:S(2)}) collective-permute-start(bf16[48,1024]{1,0:T(8,128)(2,1)} %param.7), channel_id=1, source_target_pairs={{0,4},{1,5},{2,6},{3,7},{4,0},{5,1},{6,2},{7,3},{8,12},{9,13},{10,... | collective-permute-start | bytes 294920 | tf_op jit(solution)/shard_map/ppermute | solution.py:238
  3.0 10.6 %collective-permute-start = (bf16[48,1024]{1,0:T(8,128)(2,1)}, bf16[48,1024]{1,0:T(8,128)(2,1)S(1)}, u32[]{:S(2)}, u32[]{:S(2)}) collective-permute-start(bf16[48,1024]{1,0:T(8,128)(2,1)} %param.7), channel_id=1, source_target_pairs={{0,8},{1,9},{2,10},{3,11},{4,12},{5,13},{6,14},{7,15},{8,0},{9,1},... | collective-permute-start | bytes 294920 | tf_op jit(solution)/shard_map/ppermute | solution.py:238
  5.6 8.1 %collective-permute-start.1 = (bf16[48,1024]{1,0:T(8,128)(2,1)}, bf16[48,1024]{1,0:T(8,128)(2,1)S(1)}, u32[]{:S(2)}, u32[]{:S(2)}) collective-permute-start(bf16[48,1024]{1,0:T(8,128)(2,1)} %param.7), channel_id=1, source_target_pairs={{0,12},{1,13},{2,14},{3,15},{4,8},{5,9},{6,10},{7,11},{8,4},{9,5},... | collective-permute-start | bytes 294920 | tf_op jit(solution)/shard_map/ppermute | solution.py:238
  6.6 12.8 %collective-permute-start.7 = (bf16[96,1024]{1,0:T(8,128)(2,1)S(1)}, bf16[96,1024]{1,0:T(8,128)(2,1)S(1)}, u32[]{:S(2)}, u32[]{:S(2)}) collective-permute-start(bf16[96,1024]{1,0:T(8,128)(2,1)S(1)} %get-tuple-element.15), channel_id=1, source_target_pairs={{0,2},{1,3},{2,0},{3,1},{4,6},{5,7},{6,4},{7,5},{8,10},{9,11},{10,... | collective-permute-start | bytes 589832 | tf_op jit(solution)/shard_map/ppermute | solution.py:238
  8.4 12.5 %collective-permute-start.8 = (bf16[96,1024]{1,0:T(8,128)(2,1)S(1)}, bf16[96,1024]{1,0:T(8,128)(2,1)S(1)}, u32[]{:S(2)}, u32[]{:S(2)}) collective-permute-start(bf16[96,1024]{1,0:T(8,128)(2,1)S(1)} %get-tuple-element.15), channel_id=1, source_target_pairs={{0,18},{1,19},{2,16},{3,17},{4,22},{5,23},{6,20},{7,21},{8,26},{9,... | collective-permute-start | bytes 589832 | tf_op jit(solution)/shard_map/ppermute | solution.py:238
  9.8 11.1 %collective-permute-start.9 = (bf16[96,1024]{1,0:T(8,128)(2,1)S(1)}, bf16[96,1024]{1,0:T(8,128)(2,1)S(1)}, u32[]{:S(2)}, u32[]{:S(2)}) collective-permute-start(bf16[96,1024]{1,0:T(8,128)(2,1)S(1)} %get-tuple-element.15), channel_id=1, source_target_pairs={{0,16},{1,17},{2,18},{3,19},{4,20},{5,21},{6,22},{7,23},{8,24},{9,... | collective-permute-start | bytes 589832 | tf_op jit(solution)/shard_map/ppermute | solution.py:238
  13.7 11.5 %collective-permute-start.2 = (bf16[96,1024]{1,0:T(8,128)(2,1)S(1)}, bf16[96,1024]{1,0:T(8,128)(2,1)S(1)}, u32[]{:S(2)}, u32[]{:S(2)}) collective-permute-start(bf16[96,1024]{1,0:T(8,128)(2,1)S(1)} %get-tuple-element.19), channel_id=1, source_target_pairs={{0,2},{1,3},{2,0},{3,1},{4,6},{5,7},{6,4},{7,5},{8,10},{9,11},{10,... | collective-permute-start | bytes 589832 | tf_op jit(solution)/shard_map/ppermute | solution.py:238
  15.3 10.2 %collective-permute-start.3 = (bf16[96,1024]{1,0:T(8,128)(2,1)S(1)}, bf16[96,1024]{1,0:T(8,128)(2,1)S(1)}, u32[]{:S(2)}, u32[]{:S(2)}) collective-permute-start(bf16[96,1024]{1,0:T(8,128)(2,1)S(1)} %get-tuple-element.19), channel_id=1, source_target_pairs={{0,18},{1,19},{2,16},{3,17},{4,22},{5,23},{6,20},{7,21},{8,26},{9,... | collective-permute-start | bytes 589832 | tf_op jit(solution)/shard_map/ppermute | solution.py:238
  19.4 7.3 %collective-permute-start.4 = (bf16[96,1024]{1,0:T(8,128)(2,1)S(1)}, bf16[96,1024]{1,0:T(8,128)(2,1)S(1)}, u32[]{:S(2)}, u32[]{:S(2)}) collective-permute-start(bf16[96,1024]{1,0:T(8,128)(2,1)S(1)} %get-tuple-element.19), channel_id=1, source_target_pairs={{0,16},{1,17},{2,18},{3,19},{4,20},{5,21},{6,22},{7,23},{8,24},{9,... | collective-permute-start | bytes 589832 | tf_op jit(solution)/shard_map/ppermute | solution.py:238
  20.9 5.8 %copy-start.1 = (f32[64,3072]{1,0:T(8,128)S(1)}, f32[64,3072]{1,0:T(8,128)}, u32[]{:S(2)}) copy-start(f32[64,3072]{1,0:T(8,128)} %refs_2_.1) | copy-start | bytes 2359300
  21.0 5.8 %collective-permute-start.10 = (bf16[384,1024]{1,0:T(8,128)(2,1)S(1)}, bf16[384,1024]{1,0:T(8,128)(2,1)S(1)}, u32[]{:S(2)}, u32[]{:S(2)}) collective-permute-start(bf16[384,1024]{1,0:T(8,128)(2,1)S(1)} %constant_dynamic-update-slice_fusion.9.refs_0_), channel_id=1, source_target_pairs={{0,1},{1,0},{2,3},{3,2},{4,5},{5,4},{6,7},{7,6},{8,9},{9,8},{10,11... | collective-permute-start | bytes 2359304 | tf_op jit(solution)/shard_map/ppermute | solution.py:238
  25.5 1.3 %copy-start = (bf16[48,3072]{1,0:T(8,128)(2,1)S(1)}, bf16[48,3072]{1,0:T(8,128)(2,1)}, u32[]{:S(2)}) copy-start(bf16[48,3072]{1,0:T(8,128)(2,1)} %q_ref.5) | copy-start | bytes 884740
  25.5 1.3 %copy-start.2 = (s32[2]{0:T(128)S(1)}, s32[2]{0:T(128)}, u32[]{:S(2)}) copy-start(s32[2]{0:T(128)} %clip_ref.5) | copy-start | bytes 28
  25.5 1.3 %copy-start.3 = (s32[2]{0:T(128)S(1)}, s32[2]{0:T(128)}, u32[]{:S(2)}) copy-start(s32[2]{0:T(128)} %valid_ref.5) | copy-start | bytes 28
  25.5 1.2 %copy-start.4 = (s32[2]{0:T(128)S(1)}, s32[2]{0:T(128)}, u32[]{:S(2)}) copy-start(s32[2]{0:T(128)} %step_ref.5) | copy-start | bytes 28
  26.7 4.1 %collective-permute-start.5 = (bf16[384,1024]{1,0:T(8,128)(2,1)S(1)}, bf16[384,1024]{1,0:T(8,128)(2,1)S(1)}, u32[]{:S(2)}, u32[]{:S(2)}) collective-permute-start(bf16[384,1024]{1,0:T(8,128)(2,1)S(1)} %constant_dynamic-update-slice_fusion.2.refs_0_), channel_id=1, source_target_pairs={{0,1},{1,0},{2,3},{3,2},{4,5},{5,4},{6,7},{7,6},{8,9},{9,8},{10,11... | collective-permute-start | bytes 2359304 | tf_op jit(solution)/shard_map/ppermute | solution.py:238

commit v3 on v2

--- a/solution.py
+++ b/solution.py
@@ -49,12 +49,10 @@
         first = pl.multiple_of(step - step % GATE_ROWS, GATE_ROWS)
         fetch = pltpu.make_async_copy(table_ref.at[pl.ds(first, GATE_ROWS)], gate_ref, gate_sem)
         fetch.start()
-    elif closes:
+    else:
         top_in, part_in, gate_ref, out_ref, staged_ref, out_sem = refs
         position = lax.axis_index("seq") * tokens + lax.broadcasted_iota(jnp.int32, (tokens, 1), 0)
         live = (position < valid_ref[lax.axis_index("span")]).astype(jnp.float32)
-    else:
-        top_in, part_in, top_out, part_out = refs
     biases = [key_bias(order, tokens, n_seq, clip_ref, valid_ref) for order in orders]
     scores, tops, writes = {}, {}, []
     for h in heads:
@@ -227,7 +225,7 @@
 def per_device(n_span, n_seq, queries, keyvals, clip_index, noise_step, valid_count, gate_table):
     devices = n_span * n_seq
     far = [4 * i for i in range(n_seq // 4)]
-    plane = [2] + [s * n_seq + y for s in range(1, n_span) for y in (2, 0)]
+    plane = [2] + [s * n_seq + y for s in range(1, n_span) for y in (0, 2)]
     if len(far) not in (2, 4) or len(plane) > MOST_PARTNERS or devices & (devices - 1):
         return gathered_whole(
             n_span, n_seq, queries, keyvals, clip_index, noise_step, valid_count, gate_table
@@ -238,22 +236,22 @@
         return lax.ppermute(block, ("span", "seq"), pairs)
 
     scalars = (clip_index, valid_count, noise_step)
-    ob = lax.optimization_barrier
-    cat = lambda xs: jnp.concatenate(xs, axis=0)
+    blocks = {0: keyvals}
+    for d in far[1:]:
+        blocks[d] = exchange(keyvals, d)
     half = len(far) // 2
-    nearz, farz = far[:half], far[half:]
-    orders = [[p ^ d for p in [0] + plane for d in part] for part in (nearz, farz)]
-    twins = [[d ^ 1 for d in o] for o in orders]
-    z={0:keyvals}
-    for d in far[1:]: z[d]=exchange(keyvals,d)
-    p1=cat([z[d] for d in nearz]); p2=cat([z[d] for d in farz])
-    near=cat([p1]+[exchange(p1,d) for d in plane])
-    away=cat([p2]+[exchange(p2,d) for d in plane])
-    nt=exchange(near,1)
-    *st,gate=attend(scalars,queries,[near,nt],[orders[0],twins[0]],n_seq,"first",gate_table)
-    at=exchange(away,1)
-    st=attend(scalars,queries,[away],[orders[1]],n_seq,"middle",*st)
-    return attend(scalars,queries,[at],[twins[1]],n_seq,"last",*st,gate)
+    parts, orders, twins = [], [], []
+    for part in (far[:half], far[half:]):
+        column = jnp.concatenate([blocks[d] for d in part], axis=0)
+        parts.append(jnp.concatenate([column] + [exchange(column, d) for d in plane], axis=0))
+        orders.append([p ^ d for p in [0] + plane for d in part])
+        twins.append([d ^ 1 for d in orders[-1]])
+    near, away = parts
+    near_twin, away_twin = exchange(near, 1), exchange(away, 1)
+    *state, gate = attend(
+        scalars, queries, [near, near_twin, away], [orders[0], twins[0], orders[1]], n_seq, "first", gate_table
+    )
+    return attend(scalars, queries, [away_twin], [twins[1]], n_seq, "last", *state, gate)
 
 
 def solution(mesh):

time: 33.2 us -> 32.4 us (0.976)
  starting transfers between devices: 13.8 us -> 12.9 us
  waiting for transfers between devices: 11.7 us -> 12.6 us
  Pallas kernels: 6.17 us -> 5.43 us
    ppermute x11, starting transfers between devices: 13.8 us -> 12.9 us  [exchange(): return lax.ppermute(block, ('span', 'seq'), pairs)]
    ppermute x11, waiting for transfers between devices: 11.7 us -> 12.6 us  [exchange(): return lax.ppermute(block, ('span', 'seq'), pairs)]
    pallas_call x3 -> x2, Pallas kernels: 6.17 us -> 5.43 us  [attend(): pl.pallas_call(functools.partial(attend_kernel, orders, stage, n_seq), ou...]
  transfers between devices with their start and end apart: 11 -> 11, of which waited for: 5 -> 5; matrix products, arithmetic and copies ran while one was open for 3% -> 3% of each run, Pallas kernels for 12% -> 10%
where the time goes in v3:
time: 32.4 us; the launch traced here: 32.2 us
  starting transfers between devices  12.9 us (40%)
  waiting for transfers between devices  12.6 us (39%)
  Pallas kernels  5.43 us (17%)
  local copies, waits for them, and re-layouts  1.13 us (3%)
    ppermute x11, starting transfers between devices, exchange(): return lax.ppermute(block, ('span', 'seq'), pairs)  12.9 us
    ppermute x11, waiting for transfers between devices, exchange(): return lax.ppermute(block, ('span', 'seq'), pairs)  12.6 us
    pallas_call x2, Pallas kernels, attend(): pl.pallas_call(functools.partial(attend_kernel, orders, stage, n_seq), ou...  5.43 us
    unnamed x16, local copies, waits for them, and re-layouts  1.07 us
  transfers between devices with their start and end apart: 11, of which 5 were waited for; matrix products, arithmetic and copies ran while one was open for 3% of the time, Pallas kernels for 10%

profile of v3, /device:TPU:0, one launch (start us, length us, event | category | flops | bytes accessed | tf_op | source)
XLA Modules:
  0.0 32.2 jit_solution(16249851044842065399)
XLA Ops:
  0.0 3.0 %collective-permute-start.6 = (bf16[48,1024]{1,0:T(8,128)(2,1)}, bf16[48,1024]{1,0:T(8,128)(2,1)S(1)}, u32[]{:S(2)}, u32[]{:S(2)}) collective-permute-start(bf16[48,1024]{1,0:T(8,128)(2,1)} %param.7), channel_id=1, source_target_pairs={{0,4},{1,5},{2,6},{3,7},{4,0},{5,1},{6,2},{7,3},{8,12},{9,13},{10,... | collective-permute-start | bytes 294920 | tf_op jit(solution)/shard_map/ppermute | solution.py:236
  3.0 2.6 %collective-permute-start = (bf16[48,1024]{1,0:T(8,128)(2,1)}, bf16[48,1024]{1,0:T(8,128)(2,1)S(1)}, u32[]{:S(2)}, u32[]{:S(2)}) collective-permute-start(bf16[48,1024]{1,0:T(8,128)(2,1)} %param.7), channel_id=1, source_target_pairs={{0,8},{1,9},{2,10},{3,11},{4,12},{5,13},{6,14},{7,15},{8,0},{9,1},... | collective-permute-start | bytes 294920 | tf_op jit(solution)/shard_map/ppermute | solution.py:236
  5.6 0.0 collective-permute-start.1
  5.6 1.0 %constant_dynamic-update-slice_fusion.8 = (bf16[96,1024]{1,0:T(8,128)(2,1)S(1)}, bf16[384,1024]{1,0:T(8,128)(2,1)S(1)}) fusion(bf16[48,1024]{1,0:T(8,128)(2,1)} %param.7), kind=kLoop, calls=%fused_computation.8 | loop fusion | bytes 294912
  6.6 1.8 %collective-permute-start.7 = (bf16[96,1024]{1,0:T(8,128)(2,1)S(1)}, bf16[96,1024]{1,0:T(8,128)(2,1)S(1)}, u32[]{:S(2)}, u32[]{:S(2)}) collective-permute-start(bf16[96,1024]{1,0:T(8,128)(2,1)S(1)} %get-tuple-element.11), channel_id=1, source_target_pairs={{0,2},{1,3},{2,0},{3,1},{4,6},{5,7},{6,4},{7,5},{8,10},{9,11},{10,... | collective-permute-start | bytes 589832 | tf_op jit(solution)/shard_map/ppermute | solution.py:236
  8.4 1.5 %collective-permute-start.8 = (bf16[96,1024]{1,0:T(8,128)(2,1)S(1)}, bf16[96,1024]{1,0:T(8,128)(2,1)S(1)}, u32[]{:S(2)}, u32[]{:S(2)}) collective-permute-start(bf16[96,1024]{1,0:T(8,128)(2,1)S(1)} %get-tuple-element.11), channel_id=1, source_target_pairs={{0,16},{1,17},{2,18},{3,19},{4,20},{5,21},{6,22},{7,23},{8,24},{9,... | collective-permute-start | bytes 589832 | tf_op jit(solution)/shard_map/ppermute | solution.py:236
  9.9 0.3 collective-permute-start.9
  10.2 3.5 %collective-permute-done = bf16[48,1024]{1,0:T(8,128)(2,1)S(1)} collective-permute-done((bf16[48,1024]{1,0:T(8,128)(2,1)}, bf16[48,1024]{1,0:T(8,128)(2,1)S(1)}, u32[]{:S(2)}, u32[]{:S(2)}) %collective-permute-start) | collective-permute-done | bytes 98336 | tf_op jit(solution)/shard_map/ppermute | solution.py:236
  13.7 1.6 %collective-permute-start.2 = (bf16[96,1024]{1,0:T(8,128)(2,1)S(1)}, bf16[96,1024]{1,0:T(8,128)(2,1)S(1)}, u32[]{:S(2)}, u32[]{:S(2)}) collective-permute-start(bf16[96,1024]{1,0:T(8,128)(2,1)S(1)} %get-tuple-element.15), channel_id=1, source_target_pairs={{0,2},{1,3},{2,0},{3,1},{4,6},{5,7},{6,4},{7,5},{8,10},{9,11},{10,... | collective-permute-start | bytes 589832 | tf_op jit(solution)/shard_map/ppermute | solution.py:236
  15.3 1.5 %collective-permute-start.3 = (bf16[96,1024]{1,0:T(8,128)(2,1)S(1)}, bf16[96,1024]{1,0:T(8,128)(2,1)S(1)}, u32[]{:S(2)}, u32[]{:S(2)}) collective-permute-start(bf16[96,1024]{1,0:T(8,128)(2,1)S(1)} %get-tuple-element.15), channel_id=1, source_target_pairs={{0,16},{1,17},{2,18},{3,19},{4,20},{5,21},{6,22},{7,23},{8,24},{9,... | collective-permute-start | bytes 589832 | tf_op jit(solution)/shard_map/ppermute | solution.py:236
  16.8 0.5 %collective-permute-start.4 = (bf16[96,1024]{1,0:T(8,128)(2,1)S(1)}, bf16[96,1024]{1,0:T(8,128)(2,1)S(1)}, u32[]{:S(2)}, u32[]{:S(2)}) collective-permute-start(bf16[96,1024]{1,0:T(8,128)(2,1)S(1)} %get-tuple-element.15), channel_id=1, source_target_pairs={{0,18},{1,19},{2,16},{3,17},{4,22},{5,23},{6,20},{7,21},{8,26},{9,... | collective-permute-start | bytes 589832 | tf_op jit(solution)/shard_map/ppermute | solution.py:236
  17.3 0.0 copy-start.1
  17.3 2.9 %collective-permute-done.9 = bf16[96,1024]{1,0:T(8,128)(2,1)S(1)} collective-permute-done((bf16[96,1024]{1,0:T(8,128)(2,1)S(1)}, bf16[96,1024]{1,0:T(8,128)(2,1)S(1)}, u32[]{:S(2)}, u32[]{:S(2)}) %collective-permute-start.9) | collective-permute-done | bytes 196640 | tf_op jit(solution)/shard_map/ppermute | solution.py:236
  20.2 0.1 collective-permute-start.10
  20.3 2.4 %collective-permute-done.2 = bf16[96,1024]{1,0:T(8,128)(2,1)S(1)} collective-permute-done((bf16[96,1024]{1,0:T(8,128)(2,1)S(1)}, bf16[96,1024]{1,0:T(8,128)(2,1)S(1)}, u32[]{:S(2)}, u32[]{:S(2)}) %collective-permute-start.2) | collective-permute-done | bytes 196640 | tf_op jit(solution)/shard_map/ppermute | solution.py:236
  22.7 1.8 %collective-permute-done.3 = bf16[96,1024]{1,0:T(8,128)(2,1)S(1)} collective-permute-done((bf16[96,1024]{1,0:T(8,128)(2,1)S(1)}, bf16[96,1024]{1,0:T(8,128)(2,1)S(1)}, u32[]{:S(2)}, u32[]{:S(2)}) %collective-permute-start.3) | collective-permute-done | bytes 196640 | tf_op jit(solution)/shard_map/ppermute | solution.py:236
  24.6 0.0 copy-start
  24.6 0.0 copy-start.2
  24.6 0.0 copy-start.3
  24.6 0.0 copy-start.4
  24.6 2.0 %collective-permute-done.4 = bf16[96,1024]{1,0:T(8,128)(2,1)S(1)} collective-permute-done((bf16[96,1024]{1,0:T(8,128)(2,1)S(1)}, bf16[96,1024]{1,0:T(8,128)(2,1)S(1)}, u32[]{:S(2)}, u32[]{:S(2)}) %collective-permute-start.4) | collective-permute-done | bytes 196640 | tf_op jit(solution)/shard_map/ppermute | solution.py:236
  26.6 0.1 collective-permute-start.5
  26.8 3.2 %shard_map.64 = (f32[1152,128]{1,0:T(8,128)S(1)}, f32[1152,128]{1,0:T(8,128)S(1)}, f32[1,3072]{1,0:T(1,128)S(1)}) custom-call(s32[2]{0:T(128)S(1)} %copy-done.2, s32[2]{0:T(128)S(1)} %copy-done.3, s32[2]{0:T(128)S(1)} %copy-done.4, bf16[48,3072]{1,0:T(8,128)(2,1)S(1)} %copy-done, bf16[384,1024]{1,0:T(8,128)(2,1)S(1)} %constant_dynamic-update-slice_fusion.9.refs_0_, ...), custom_call_target="tpu_custom_call" | custom-call | flops 679477248 | bytes 2359296 | tf_op jit(solution)/shard_map/pallas_call | solution.py:128
  30.0 2.2 %shard_map.65 = bf16[48,3072]{1,0:T(8,128)(2,1)} custom-call(s32[2]{0:T(128)S(1)} %copy-done.2, s32[2]{0:T(128)S(1)} %copy-done.3, s32[2]{0:T(128)S(1)} %copy-done.4, bf16[48,3072]{1,0:T(8,128)(2,1)S(1)} %copy-done, bf16[384,1024]{1,0:T(8,128)(2,1)S(1)} %collective-permute-done.5.refs_0_, f32[1152,128]{1,0:T(8,128)S(1)} %get-tuple-element.8.refs_1_, ...), custom_call_target="tpu_custom_call" | custom-call | flops 226492416 | bytes 786432 | tf_op jit(solution)/shard_map/pallas_call | solution.py:128
  (20 shorter events, 0.2 us)
Async XLA Ops:
  0.0 6.6 %collective-permute-start.6 = (bf16[48,1024]{1,0:T(8,128)(2,1)}, bf16[48,1024]{1,0:T(8,128)(2,1)S(1)}, u32[]{:S(2)}, u32[]{:S(2)}) collective-permute-start(bf16[48,1024]{1,0:T(8,128)(2,1)} %param.7), channel_id=1, source_target_pairs={{0,4},{1,5},{2,6},{3,7},{4,0},{5,1},{6,2},{7,3},{8,12},{9,13},{10,... | collective-permute-start | bytes 294920 | tf_op jit(solution)/shard_map/ppermute | solution.py:236
  3.0 10.6 %collective-permute-start = (bf16[48,1024]{1,0:T(8,128)(2,1)}, bf16[48,1024]{1,0:T(8,128)(2,1)S(1)}, u32[]{:S(2)}, u32[]{:S(2)}) collective-permute-start(bf16[48,1024]{1,0:T(8,128)(2,1)} %param.7), channel_id=1, source_target_pairs={{0,8},{1,9},{2,10},{3,11},{4,12},{5,13},{6,14},{7,15},{8,0},{9,1},... | collective-permute-start | bytes 294920 | tf_op jit(solution)/shard_map/ppermute | solution.py:236
  5.6 8.1 %collective-permute-start.1 = (bf16[48,1024]{1,0:T(8,128)(2,1)}, bf16[48,1024]{1,0:T(8,128)(2,1)S(1)}, u32[]{:S(2)}, u32[]{:S(2)}) collective-permute-start(bf16[48,1024]{1,0:T(8,128)(2,1)} %param.7), channel_id=1, source_target_pairs={{0,12},{1,13},{2,14},{3,15},{4,8},{5,9},{6,10},{7,11},{8,4},{9,5},... | collective-permute-start | bytes 294920 | tf_op jit(solution)/shard_map/ppermute | solution.py:236
  6.6 10.2 %collective-permute-start.7 = (bf16[96,1024]{1,0:T(8,128)(2,1)S(1)}, bf16[96,1024]{1,0:T(8,128)(2,1)S(1)}, u32[]{:S(2)}, u32[]{:S(2)}) collective-permute-start(bf16[96,1024]{1,0:T(8,128)(2,1)S(1)} %get-tuple-element.11), channel_id=1, source_target_pairs={{0,2},{1,3},{2,0},{3,1},{4,6},{5,7},{6,4},{7,5},{8,10},{9,11},{10,... | collective-permute-start | bytes 589832 | tf_op jit(solution)/shard_map/ppermute | solution.py:236
  8.4 8.9 %collective-permute-start.8 = (bf16[96,1024]{1,0:T(8,128)(2,1)S(1)}, bf16[96,1024]{1,0:T(8,128)(2,1)S(1)}, u32[]{:S(2)}, u32[]{:S(2)}) collective-permute-start(bf16[96,1024]{1,0:T(8,128)(2,1)S(1)} %get-tuple-element.11), channel_id=1, source_target_pairs={{0,16},{1,17},{2,18},{3,19},{4,20},{5,21},{6,22},{7,23},{8,24},{9,... | collective-permute-start | bytes 589832 | tf_op jit(solution)/shard_map/ppermute | solution.py:236
  9.9 10.3 %collective-permute-start.9 = (bf16[96,1024]{1,0:T(8,128)(2,1)S(1)}, bf16[96,1024]{1,0:T(8,128)(2,1)S(1)}, u32[]{:S(2)}, u32[]{:S(2)}) collective-permute-start(bf16[96,1024]{1,0:T(8,128)(2,1)S(1)} %get-tuple-element.11), channel_id=1, source_target_pairs={{0,18},{1,19},{2,16},{3,17},{4,22},{5,23},{6,20},{7,21},{8,26},{9,... | collective-permute-start | bytes 589832 | tf_op jit(solution)/shard_map/ppermute | solution.py:236
  13.7 9.0 %collective-permute-start.2 = (bf16[96,1024]{1,0:T(8,128)(2,1)S(1)}, bf16[96,1024]{1,0:T(8,128)(2,1)S(1)}, u32[]{:S(2)}, u32[]{:S(2)}) collective-permute-start(bf16[96,1024]{1,0:T(8,128)(2,1)S(1)} %get-tuple-element.15), channel_id=1, source_target_pairs={{0,2},{1,3},{2,0},{3,1},{4,6},{5,7},{6,4},{7,5},{8,10},{9,11},{10,... | collective-permute-start | bytes 589832 | tf_op jit(solution)/shard_map/ppermute | solution.py:236
  15.3 9.2 %collective-permute-start.3 = (bf16[96,1024]{1,0:T(8,128)(2,1)S(1)}, bf16[96,1024]{1,0:T(8,128)(2,1)S(1)}, u32[]{:S(2)}, u32[]{:S(2)}) collective-permute-start(bf16[96,1024]{1,0:T(8,128)(2,1)S(1)} %get-tuple-element.15), channel_id=1, source_target_pairs={{0,16},{1,17},{2,18},{3,19},{4,20},{5,21},{6,22},{7,23},{8,24},{9,... | collective-permute-start | bytes 589832 | tf_op jit(solution)/shard_map/ppermute | solution.py:236
  16.8 9.8 %collective-permute-start.4 = (bf16[96,1024]{1,0:T(8,128)(2,1)S(1)}, bf16[96,1024]{1,0:T(8,128)(2,1)S(1)}, u32[]{:S(2)}, u32[]{:S(2)}) collective-permute-start(bf16[96,1024]{1,0:T(8,128)(2,1)S(1)} %get-tuple-element.15), channel_id=1, source_target_pairs={{0,18},{1,19},{2,16},{3,17},{4,22},{5,23},{6,20},{7,21},{8,26},{9,... | collective-permute-start | bytes 589832 | tf_op jit(solution)/shard_map/ppermute | solution.py:236
  17.3 9.4 %copy-start.1 = (f32[64,3072]{1,0:T(8,128)S(1)}, f32[64,3072]{1,0:T(8,128)}, u32[]{:S(2)}) copy-start(f32[64,3072]{1,0:T(8,128)} %refs_3_.1) | copy-start | bytes 2359300
  20.2 6.5 %collective-permute-start.10 = (bf16[384,1024]{1,0:T(8,128)(2,1)S(1)}, bf16[384,1024]{1,0:T(8,128)(2,1)S(1)}, u32[]{:S(2)}, u32[]{:S(2)}) collective-permute-start(bf16[384,1024]{1,0:T(8,128)(2,1)S(1)} %constant_dynamic-update-slice_fusion.9.refs_0_), channel_id=1, source_target_pairs={{0,1},{1,0},{2,3},{3,2},{4,5},{5,4},{6,7},{7,6},{8,9},{9,8},{10,11... | collective-permute-start | bytes 2359304 | tf_op jit(solution)/shard_map/ppermute | solution.py:236
  24.6 2.2 %copy-start = (bf16[48,3072]{1,0:T(8,128)(2,1)S(1)}, bf16[48,3072]{1,0:T(8,128)(2,1)}, u32[]{:S(2)}) copy-start(bf16[48,3072]{1,0:T(8,128)(2,1)} %q_ref.3) | copy-start | bytes 884740
  24.6 2.1 %copy-start.2 = (s32[2]{0:T(128)S(1)}, s32[2]{0:T(128)}, u32[]{:S(2)}) copy-start(s32[2]{0:T(128)} %clip_ref.3) | copy-start | bytes 28
  24.6 2.1 %copy-start.3 = (s32[2]{0:T(128)S(1)}, s32[2]{0:T(128)}, u32[]{:S(2)}) copy-start(s32[2]{0:T(128)} %valid_ref.3) | copy-start | bytes 28
  24.6 2.1 %copy-start.4 = (s32[2]{0:T(128)S(1)}, s32[2]{0:T(128)}, u32[]{:S(2)}) copy-start(s32[2]{0:T(128)} %step_ref.3) | copy-start | bytes 28
  26.6 3.4 %collective-permute-start.5 = (bf16[384,1024]{1,0:T(8,128)(2,1)S(1)}, bf16[384,1024]{1,0:T(8,128)(2,1)S(1)}, u32[]{:S(2)}, u32[]{:S(2)}) collective-permute-start(bf16[384,1024]{1,0:T(8,128)(2,1)S(1)} %constant_dynamic-update-slice_fusion.2.refs_2_), channel_id=1, source_target_pairs={{0,1},{1,0},{2,3},{3,2},{4,5},{5,4},{6,7},{7,6},{8,9},{9,8},{10,11... | collective-permute-start | bytes 2359304 | tf_op jit(solution)/shard_map/ppermute | solution.py:236

commit v4 on v3

--- a/solution.py
+++ b/solution.py
@@ -17,7 +17,6 @@
 NEGATIVE = -1e30
 LOG2E = math.log2(math.e)
 TILE = 384
-MOST_PARTNERS = 3
 GATE_ROWS = 8
 
 
@@ -224,9 +223,9 @@
 
 def per_device(n_span, n_seq, queries, keyvals, clip_index, noise_step, valid_count, gate_table):
     devices = n_span * n_seq
+    tokens = queries.shape[0]
     far = [4 * i for i in range(n_seq // 4)]
-    plane = [2] + [s * n_seq + y for s in range(1, n_span) for y in (0, 2)]
-    if len(far) not in (2, 4) or len(plane) > MOST_PARTNERS or devices & (devices - 1):
+    if n_span != 2 or len(far) != 4:
         return gathered_whole(
             n_span, n_seq, queries, keyvals, clip_index, noise_step, valid_count, gate_table
         )
@@ -235,23 +234,23 @@
         pairs = [(i, i ^ distance) for i in range(devices)]
         return lax.ppermute(block, ("span", "seq"), pairs)
 
+    plane = [n_seq + 2, 2, n_seq]
+    away = jnp.concatenate([exchange(keyvals, d) for d in far[2:]], axis=0)
+    column = exchange(keyvals, far[1])
+    home = jnp.concatenate([keyvals] + [exchange(keyvals, d) for d in plane], axis=0)
+    near = jnp.concatenate([home, column, exchange(home[tokens:], far[1])], axis=0)
+    away = jnp.concatenate([away] + [exchange(away, d) for d in plane], axis=0)
+    near_order = [z ^ p for z in far[:2] for p in [0] + plane]
+    away_order = [p ^ z for p in [0] + plane for z in far[2:]]
+    twin = lambda order: [d ^ 1 for d in order]
+    near_twin, away_twin = exchange(near, 1), exchange(away, 1)
     scalars = (clip_index, valid_count, noise_step)
-    blocks = {0: keyvals}
-    for d in far[1:]:
-        blocks[d] = exchange(keyvals, d)
-    half = len(far) // 2
-    parts, orders, twins = [], [], []
-    for part in (far[:half], far[half:]):
-        column = jnp.concatenate([blocks[d] for d in part], axis=0)
-        parts.append(jnp.concatenate([column] + [exchange(column, d) for d in plane], axis=0))
-        orders.append([p ^ d for p in [0] + plane for d in part])
-        twins.append([d ^ 1 for d in orders[-1]])
-    near, away = parts
-    near_twin, away_twin = exchange(near, 1), exchange(away, 1)
     *state, gate = attend(
-        scalars, queries, [near, near_twin, away], [orders[0], twins[0], orders[1]], n_seq, "first", gate_table
+        scalars, queries, [near, away], [near_order, away_order], n_seq, "first", gate_table
     )
-    return attend(scalars, queries, [away_twin], [twins[1]], n_seq, "last", *state, gate)
+    return attend(
+        scalars, queries, [away_twin, near_twin], [twin(away_order), twin(near_order)], n_seq, "last", *state, gate
+    )
 
 
 def solution(mesh):

time: 32.4 us -> 31.1 us (0.960); the launches traced: 32.2 us -> 30.5 us
  waiting for transfers between devices: 12.6 us -> 8.58 us
  starting transfers between devices: 12.9 us -> 15 us
    ppermute x11 -> x12, waiting for transfers between devices: 12.6 us -> 8.58 us  [exchange(): return lax.ppermute(block, ('span', 'seq'), pairs)]
    ppermute x11 -> x12, starting transfers between devices: 12.9 us -> 15 us  [exchange(): return lax.ppermute(block, ('span', 'seq'), pairs)]
    unnamed x16 -> x20, local copies, waits for them, and re-layouts: 1.07 us -> 1.28 us
  transfers between devices with their start and end apart: 11 -> 12, of which waited for: 5 -> 6; matrix products, arithmetic and copies ran while one was open for 3% -> 4% of each run, Pallas kernels for 10% -> 8%
where the time goes in v4:
time: 31.1 us; the launch traced here: 30.5 us
  starting transfers between devices  15 us (48%)
  waiting for transfers between devices  8.58 us (28%)
  Pallas kernels  5.41 us (17%)
  local copies, waits for them, and re-layouts  1.33 us (4%)
    ppermute x12, starting transfers between devices, exchange(): return lax.ppermute(block, ('span', 'seq'), pairs)  15 us
    ppermute x12, waiting for transfers between devices, exchange(): return lax.ppermute(block, ('span', 'seq'), pairs)  8.58 us
    pallas_call x2, Pallas kernels, attend(): pl.pallas_call(functools.partial(attend_kernel, orders, stage, n_seq), ou...  5.41 us
    unnamed x20, local copies, waits for them, and re-layouts  1.28 us
  transfers between devices with their start and end apart: 12, of which 6 were waited for; matrix products, arithmetic and copies ran while one was open for 4% of the time, Pallas kernels for 8%

profile of v4, /device:TPU:0, one launch (start us, length us, event | category | flops | bytes accessed | tf_op | source)
XLA Modules:
  0.0 30.5 jit_solution(3107642411315299740)
XLA Ops:
  0.0 4.0 %collective-permute-start = (bf16[48,1024]{1,0:T(8,128)(2,1)}, bf16[48,1024]{1,0:T(8,128)(2,1)S(1)}, u32[]{:S(2)}, u32[]{:S(2)}) collective-permute-start(bf16[48,1024]{1,0:T(8,128)(2,1)} %param.7), channel_id=1, source_target_pairs={{0,8},{1,9},{2,10},{3,11},{4,12},{5,13},{6,14},{7,15},{8,0},{9,1},... | collective-permute-start | bytes 294920 | tf_op jit(solution)/shard_map/ppermute | solution.py:235
  4.0 1.3 %collective-permute-start.1 = (bf16[48,1024]{1,0:T(8,128)(2,1)}, bf16[48,1024]{1,0:T(8,128)(2,1)S(1)}, u32[]{:S(2)}, u32[]{:S(2)}) collective-permute-start(bf16[48,1024]{1,0:T(8,128)(2,1)} %param.7), channel_id=1, source_target_pairs={{0,12},{1,13},{2,14},{3,15},{4,8},{5,9},{6,10},{7,11},{8,4},{9,5},... | collective-permute-start | bytes 294920 | tf_op jit(solution)/shard_map/ppermute | solution.py:235
  5.4 2.4 %collective-permute-start.6 = (bf16[48,1024]{1,0:T(8,128)(2,1)}, bf16[48,1024]{1,0:T(8,128)(2,1)S(1)}, u32[]{:S(2)}, u32[]{:S(2)}) collective-permute-start(bf16[48,1024]{1,0:T(8,128)(2,1)} %param.7), channel_id=1, source_target_pairs={{0,18},{1,19},{2,16},{3,17},{4,22},{5,23},{6,20},{7,21},{8,26},{9,... | collective-permute-start | bytes 294920 | tf_op jit(solution)/shard_map/ppermute | solution.py:235
  7.8 0.5 %collective-permute-start.7 = (bf16[48,1024]{1,0:T(8,128)(2,1)}, bf16[48,1024]{1,0:T(8,128)(2,1)S(1)}, u32[]{:S(2)}, u32[]{:S(2)}) collective-permute-start(bf16[48,1024]{1,0:T(8,128)(2,1)} %param.7), channel_id=1, source_target_pairs={{0,2},{1,3},{2,0},{3,1},{4,6},{5,7},{6,4},{7,5},{8,10},{9,11},{10,... | collective-permute-start | bytes 294920 | tf_op jit(solution)/shard_map/ppermute | solution.py:235
  8.3 0.5 %collective-permute-start.8 = (bf16[48,1024]{1,0:T(8,128)(2,1)}, bf16[48,1024]{1,0:T(8,128)(2,1)S(1)}, u32[]{:S(2)}, u32[]{:S(2)}) collective-permute-start(bf16[48,1024]{1,0:T(8,128)(2,1)} %param.7), channel_id=1, source_target_pairs={{0,16},{1,17},{2,18},{3,19},{4,20},{5,21},{6,22},{7,23},{8,24},{9,... | collective-permute-start | bytes 294920 | tf_op jit(solution)/shard_map/ppermute | solution.py:235
  8.9 0.9 %constant_dynamic-update-slice_fusion.12 = bf16[384,1024]{1,0:T(8,128)(2,1)S(1)} fusion(bf16[48,1024]{1,0:T(8,128)(2,1)} %param.7), kind=kLoop, calls=%fused_computation.13 | loop fusion | bytes 196608
  9.8 2.3 %collective-permute-done = bf16[48,1024]{1,0:T(8,128)(2,1)S(1)} collective-permute-done((bf16[48,1024]{1,0:T(8,128)(2,1)}, bf16[48,1024]{1,0:T(8,128)(2,1)S(1)}, u32[]{:S(2)}, u32[]{:S(2)}) %collective-permute-start) | collective-permute-done | bytes 98336 | tf_op jit(solution)/shard_map/ppermute | solution.py:235
  12.2 0.0 collective-permute-start.9
  12.2 2.7 %collective-permute-start.2 = (bf16[96,1024]{1,0:T(8,128)(2,1)S(1)}, bf16[96,1024]{1,0:T(8,128)(2,1)S(1)}, u32[]{:S(2)}, u32[]{:S(2)}) collective-permute-start(bf16[96,1024]{1,0:T(8,128)(2,1)S(1)} %get-tuple-element.11), channel_id=1, source_target_pairs={{0,18},{1,19},{2,16},{3,17},{4,22},{5,23},{6,20},{7,21},{8,26},{9,... | collective-permute-start | bytes 589832 | tf_op jit(solution)/shard_map/ppermute | solution.py:235
  14.9 0.5 %collective-permute-start.3 = (bf16[96,1024]{1,0:T(8,128)(2,1)S(1)}, bf16[96,1024]{1,0:T(8,128)(2,1)S(1)}, u32[]{:S(2)}, u32[]{:S(2)}) collective-permute-start(bf16[96,1024]{1,0:T(8,128)(2,1)S(1)} %get-tuple-element.11), channel_id=1, source_target_pairs={{0,2},{1,3},{2,0},{3,1},{4,6},{5,7},{6,4},{7,5},{8,10},{9,11},{10,... | collective-permute-start | bytes 589832 | tf_op jit(solution)/shard_map/ppermute | solution.py:235
  15.4 0.4 %collective-permute-start.4 = (bf16[96,1024]{1,0:T(8,128)(2,1)S(1)}, bf16[96,1024]{1,0:T(8,128)(2,1)S(1)}, u32[]{:S(2)}, u32[]{:S(2)}) collective-permute-start(bf16[96,1024]{1,0:T(8,128)(2,1)S(1)} %get-tuple-element.11), channel_id=1, source_target_pairs={{0,16},{1,17},{2,18},{3,19},{4,20},{5,21},{6,22},{7,23},{8,24},{9,... | collective-permute-start | bytes 589832 | tf_op jit(solution)/shard_map/ppermute | solution.py:235
  15.8 2.1 %collective-permute-start.10 = (bf16[144,1024]{1,0:T(8,128)(2,1)S(1)}, bf16[144,1024]{1,0:T(8,128)(2,1)S(1)}, u32[]{:S(2)}, u32[]{:S(2)}) collective-permute-start(bf16[144,1024]{1,0:T(8,128)(2,1)S(1)} %pad_maximum_fusion), channel_id=1, source_target_pairs={{0,4},{1,5},{2,6},{3,7},{4,0},{5,1},{6,2},{7,3},{8,12},{9,13},{10,... | collective-permute-start | bytes 884744 | tf_op jit(solution)/shard_map/ppermute | solution.py:235
  18.0 3.1 %collective-permute-done.2 = bf16[96,1024]{1,0:T(8,128)(2,1)S(1)} collective-permute-done((bf16[96,1024]{1,0:T(8,128)(2,1)S(1)}, bf16[96,1024]{1,0:T(8,128)(2,1)S(1)}, u32[]{:S(2)}, u32[]{:S(2)}) %collective-permute-start.2) | collective-permute-done | bytes 196640 | tf_op jit(solution)/shard_map/ppermute | solution.py:235
  21.0 0.0 copy-start.1
  21.1 2.8 %collective-permute-done.3 = bf16[96,1024]{1,0:T(8,128)(2,1)S(1)} collective-permute-done((bf16[96,1024]{1,0:T(8,128)(2,1)S(1)}, bf16[96,1024]{1,0:T(8,128)(2,1)S(1)}, u32[]{:S(2)}, u32[]{:S(2)}) %collective-permute-start.3) | collective-permute-done | bytes 196640 | tf_op jit(solution)/shard_map/ppermute | solution.py:235
  23.9 0.1 collective-permute-done.4
  24.0 0.0 copy-start
  24.0 0.1 collective-permute-start.5
  24.1 0.1 collective-permute-done.10
  24.2 0.5 %collective-permute-start.11 = (bf16[384,1024]{1,0:T(8,128)(2,1)S(1)}, bf16[384,1024]{1,0:T(8,128)(2,1)S(1)}, u32[]{:S(2)}, u32[]{:S(2)}) collective-permute-start(bf16[384,1024]{1,0:T(8,128)(2,1)S(1)} %constant_dynamic-update-slice_fusion.7.refs_0_), channel_id=1, source_target_pairs={{0,1},{1,0},{2,3},{3,2},{4,5},{5,4},{6,7},{7,6},{8,9},{9,8},{10,11... | collective-permute-start | bytes 2359304 | tf_op jit(solution)/shard_map/ppermute | solution.py:235
  24.7 0.2 copy-done
  25.0 2.4 %shard_map.64 = (f32[1152,128]{1,0:T(8,128)S(1)}, f32[1152,128]{1,0:T(8,128)S(1)}, f32[1,3072]{1,0:T(1,128)S(1)}) custom-call(s32[2]{0:T(128)S(1)} %copy-done.2, s32[2]{0:T(128)S(1)} %copy-done.3, s32[2]{0:T(128)S(1)} %copy-done.4, bf16[48,3072]{1,0:T(8,128)(2,1)S(1)} %copy-done, bf16[384,1024]{1,0:T(8,128)(2,1)S(1)} %constant_dynamic-update-slice_fusion.7.refs_0_, ...), custom_call_target="tpu_custom_call" | custom-call | flops 452984832 | bytes 1572864 | tf_op jit(solution)/shard_map/pallas_call | solution.py:127
  27.4 0.2 collective-permute-done.11.refs_1_
  27.5 3.0 %shard_map.65 = bf16[48,3072]{1,0:T(8,128)(2,1)} custom-call(s32[2]{0:T(128)S(1)} %copy-done.2, s32[2]{0:T(128)S(1)} %copy-done.3, s32[2]{0:T(128)S(1)} %copy-done.4, bf16[48,3072]{1,0:T(8,128)(2,1)S(1)} %copy-done, bf16[384,1024]{1,0:T(8,128)(2,1)S(1)} %collective-permute-done.5.refs_0_, bf16[384,1024]{1,0:T(8,128)(2,1)S(1)} %collective-permute-done.11.refs_1_, ...), custom_call_target="tpu_custom_call" | custom-call | flops 452984832 | bytes 1572864 | tf_op jit(solution)/shard_map/pallas_call | solution.py:127
  (26 shorter events, 0.2 us)
Async XLA Ops:
  0.0 12.2 %copy-start.5 = (bf16[48,1024]{1,0:T(8,128)(2,1)S(1)}, bf16[48,1024]{1,0:T(8,128)(2,1)}, u32[]{:S(2)}) copy-start(bf16[48,1024]{1,0:T(8,128)(2,1)} %param.7) | copy-start | bytes 294916
  0.0 12.2 %collective-permute-start = (bf16[48,1024]{1,0:T(8,128)(2,1)}, bf16[48,1024]{1,0:T(8,128)(2,1)S(1)}, u32[]{:S(2)}, u32[]{:S(2)}) collective-permute-start(bf16[48,1024]{1,0:T(8,128)(2,1)} %param.7), channel_id=1, source_target_pairs={{0,8},{1,9},{2,10},{3,11},{4,12},{5,13},{6,14},{7,15},{8,0},{9,1},... | collective-permute-start | bytes 294920 | tf_op jit(solution)/shard_map/ppermute | solution.py:235
  4.0 8.2 %collective-permute-start.1 = (bf16[48,1024]{1,0:T(8,128)(2,1)}, bf16[48,1024]{1,0:T(8,128)(2,1)S(1)}, u32[]{:S(2)}, u32[]{:S(2)}) collective-permute-start(bf16[48,1024]{1,0:T(8,128)(2,1)} %param.7), channel_id=1, source_target_pairs={{0,12},{1,13},{2,14},{3,15},{4,8},{5,9},{6,10},{7,11},{8,4},{9,5},... | collective-permute-start | bytes 294920 | tf_op jit(solution)/shard_map/ppermute | solution.py:235
  5.4 9.5 %collective-permute-start.6 = (bf16[48,1024]{1,0:T(8,128)(2,1)}, bf16[48,1024]{1,0:T(8,128)(2,1)S(1)}, u32[]{:S(2)}, u32[]{:S(2)}) collective-permute-start(bf16[48,1024]{1,0:T(8,128)(2,1)} %param.7), channel_id=1, source_target_pairs={{0,18},{1,19},{2,16},{3,17},{4,22},{5,23},{6,20},{7,21},{8,26},{9,... | collective-permute-start | bytes 294920 | tf_op jit(solution)/shard_map/ppermute | solution.py:235
  7.8 7.6 %collective-permute-start.7 = (bf16[48,1024]{1,0:T(8,128)(2,1)}, bf16[48,1024]{1,0:T(8,128)(2,1)S(1)}, u32[]{:S(2)}, u32[]{:S(2)}) collective-permute-start(bf16[48,1024]{1,0:T(8,128)(2,1)} %param.7), channel_id=1, source_target_pairs={{0,2},{1,3},{2,0},{3,1},{4,6},{5,7},{6,4},{7,5},{8,10},{9,11},{10,... | collective-permute-start | bytes 294920 | tf_op jit(solution)/shard_map/ppermute | solution.py:235
  8.3 7.5 %collective-permute-start.8 = (bf16[48,1024]{1,0:T(8,128)(2,1)}, bf16[48,1024]{1,0:T(8,128)(2,1)S(1)}, u32[]{:S(2)}, u32[]{:S(2)}) collective-permute-start(bf16[48,1024]{1,0:T(8,128)(2,1)} %param.7), channel_id=1, source_target_pairs={{0,16},{1,17},{2,18},{3,19},{4,20},{5,21},{6,22},{7,23},{8,24},{9,... | collective-permute-start | bytes 294920 | tf_op jit(solution)/shard_map/ppermute | solution.py:235
  12.2 5.8 %collective-permute-start.9 = (bf16[48,1024]{1,0:T(8,128)(2,1)S(1)}, bf16[48,1024]{1,0:T(8,128)(2,1)S(1)}, u32[]{:S(2)}, u32[]{:S(2)}) collective-permute-start(bf16[48,1024]{1,0:T(8,128)(2,1)S(1)} %copy-done.5), channel_id=1, source_target_pairs={{0,4},{1,5},{2,6},{3,7},{4,0},{5,1},{6,2},{7,3},{8,12},{9,13},{10,... | collective-permute-start | bytes 294920 | tf_op jit(solution)/shard_map/ppermute | solution.py:235
  12.2 8.8 %collective-permute-start.2 = (bf16[96,1024]{1,0:T(8,128)(2,1)S(1)}, bf16[96,1024]{1,0:T(8,128)(2,1)S(1)}, u32[]{:S(2)}, u32[]{:S(2)}) collective-permute-start(bf16[96,1024]{1,0:T(8,128)(2,1)S(1)} %get-tuple-element.11), channel_id=1, source_target_pairs={{0,18},{1,19},{2,16},{3,17},{4,22},{5,23},{6,20},{7,21},{8,26},{9,... | collective-permute-start | bytes 589832 | tf_op jit(solution)/shard_map/ppermute | solution.py:235
  14.9 9.0 %collective-permute-start.3 = (bf16[96,1024]{1,0:T(8,128)(2,1)S(1)}, bf16[96,1024]{1,0:T(8,128)(2,1)S(1)}, u32[]{:S(2)}, u32[]{:S(2)}) collective-permute-start(bf16[96,1024]{1,0:T(8,128)(2,1)S(1)} %get-tuple-element.11), channel_id=1, source_target_pairs={{0,2},{1,3},{2,0},{3,1},{4,6},{5,7},{6,4},{7,5},{8,10},{9,11},{10,... | collective-permute-start | bytes 589832 | tf_op jit(solution)/shard_map/ppermute | solution.py:235
  15.4 8.6 %collective-permute-start.4 = (bf16[96,1024]{1,0:T(8,128)(2,1)S(1)}, bf16[96,1024]{1,0:T(8,128)(2,1)S(1)}, u32[]{:S(2)}, u32[]{:S(2)}) collective-permute-start(bf16[96,1024]{1,0:T(8,128)(2,1)S(1)} %get-tuple-element.11), channel_id=1, source_target_pairs={{0,16},{1,17},{2,18},{3,19},{4,20},{5,21},{6,22},{7,23},{8,24},{9,... | collective-permute-start | bytes 589832 | tf_op jit(solution)/shard_map/ppermute | solution.py:235
  15.8 8.4 %collective-permute-start.10 = (bf16[144,1024]{1,0:T(8,128)(2,1)S(1)}, bf16[144,1024]{1,0:T(8,128)(2,1)S(1)}, u32[]{:S(2)}, u32[]{:S(2)}) collective-permute-start(bf16[144,1024]{1,0:T(8,128)(2,1)S(1)} %pad_maximum_fusion), channel_id=1, source_target_pairs={{0,4},{1,5},{2,6},{3,7},{4,0},{5,1},{6,2},{7,3},{8,12},{9,13},{10,... | collective-permute-start | bytes 884744 | tf_op jit(solution)/shard_map/ppermute | solution.py:235
  21.0 3.7 %copy-start.1 = (f32[64,3072]{1,0:T(8,128)S(1)}, f32[64,3072]{1,0:T(8,128)}, u32[]{:S(2)}) copy-start(f32[64,3072]{1,0:T(8,128)} %refs_2_.1) | copy-start | bytes 2359300
  24.0 1.0 %copy-start = (bf16[48,3072]{1,0:T(8,128)(2,1)S(1)}, bf16[48,3072]{1,0:T(8,128)(2,1)}, u32[]{:S(2)}) copy-start(bf16[48,3072]{1,0:T(8,128)(2,1)} %q_ref.3) | copy-start | bytes 884740
  24.0 1.0 %copy-start.2 = (s32[2]{0:T(128)S(1)}, s32[2]{0:T(128)}, u32[]{:S(2)}) copy-start(s32[2]{0:T(128)} %clip_ref.3) | copy-start | bytes 28
  24.0 0.9 %copy-start.3 = (s32[2]{0:T(128)S(1)}, s32[2]{0:T(128)}, u32[]{:S(2)}) copy-start(s32[2]{0:T(128)} %valid_ref.3) | copy-start | bytes 28
  24.0 0.9 %copy-start.4 = (s32[2]{0:T(128)S(1)}, s32[2]{0:T(128)}, u32[]{:S(2)}) copy-start(s32[2]{0:T(128)} %step_ref.3) | copy-start | bytes 28
  24.0 3.3 %collective-permute-start.5 = (bf16[384,1024]{1,0:T(8,128)(2,1)S(1)}, bf16[384,1024]{1,0:T(8,128)(2,1)S(1)}, u32[]{:S(2)}, u32[]{:S(2)}) collective-permute-start(bf16[384,1024]{1,0:T(8,128)(2,1)S(1)} %constant_dynamic-update-slice_fusion.2.refs_1_), channel_id=1, source_target_pairs={{0,1},{1,0},{2,3},{3,2},{4,5},{5,4},{6,7},{7,6},{8,9},{9,8},{10,11... | collective-permute-start | bytes 2359304 | tf_op jit(solution)/shard_map/ppermute | solution.py:235
  24.2 3.3 %collective-permute-start.11 = (bf16[384,1024]{1,0:T(8,128)(2,1)S(1)}, bf16[384,1024]{1,0:T(8,128)(2,1)S(1)}, u32[]{:S(2)}, u32[]{:S(2)}) collective-permute-start(bf16[384,1024]{1,0:T(8,128)(2,1)S(1)} %constant_dynamic-update-slice_fusion.7.refs_0_), channel_id=1, source_target_pairs={{0,1},{1,0},{2,3},{3,2},{4,5},{5,4},{6,7},{7,6},{8,9},{9,8},{10,11... | collective-permute-start | bytes 2359304 | tf_op jit(solution)/shard_map/ppermute | solution.py:235

commit v5 on v4

--- a/solution.py
+++ b/solution.py
@@ -71,12 +71,12 @@
         for i, kv_ref in enumerate(kv_refs):
             repeats = scores[h, i].shape[1] // HEAD_WIDTH
             weights = jnp.exp2(scores[h, i] - jnp.concatenate([tops[h]] * repeats, axis=1))
-            total = total + jnp.sum(weights, axis=1, keepdims=True)
             numerator = numerator + jnp.dot(
                 weights.astype(jnp.bfloat16),
-                kv_ref[:, columns[KEY_VALUE_HEADS + h]],
+                jnp.concatenate([kv_ref[:, columns[KEY_VALUE_HEADS + h]], jnp.ones((kv_ref.shape[0], HEAD_WIDTH), jnp.bfloat16)], axis=1),
                 preferred_element_type=jnp.float32,
             )
+        total, numerator = numerator[:, HEAD_WIDTH:], numerator[:, :HEAD_WIDTH]
         if not opens:
             factor = jnp.exp2(top_in[span, :] - tops[h])
             total = total + factor

time: 31.1 us -> 31 us (level)
  transfers between devices with their start and end apart: 12 -> 12, of which waited for: 6 -> 6; matrix products, arithmetic and copies ran while one was open for 4% -> 4% of each run, Pallas kernels for 8% -> 7%
where the time goes in v5:
time: 31 us; the launch traced here: 30.4 us
  starting transfers between devices  15 us (48%)
  waiting for transfers between devices  8.73 us (28%)
  Pallas kernels  5.12 us (17%)
  local copies, waits for them, and re-layouts  1.33 us (4%)
    ppermute x12, starting transfers between devices, exchange(): return lax.ppermute(block, ('span', 'seq'), pairs)  15 us
    ppermute x12, waiting for transfers between devices, exchange(): return lax.ppermute(block, ('span', 'seq'), pairs)  8.73 us
    pallas_call x2, Pallas kernels, attend(): pl.pallas_call(functools.partial(attend_kernel, orders, stage, n_seq), ou...  5.12 us
    unnamed x20, local copies, waits for them, and re-layouts  1.28 us
  transfers between devices with their start and end apart: 12, of which 6 were waited for; matrix products, arithmetic and copies ran while one was open for 4% of the time, Pallas kernels for 7%

profile of v5, /device:TPU:0, one launch (start us, length us, event | category | flops | bytes accessed | tf_op | source)
XLA Modules:
  0.0 30.4 jit_solution(8853393136102263637)
XLA Ops:
  0.0 4.0 %collective-permute-start = (bf16[48,1024]{1,0:T(8,128)(2,1)}, bf16[48,1024]{1,0:T(8,128)(2,1)S(1)}, u32[]{:S(2)}, u32[]{:S(2)}) collective-permute-start(bf16[48,1024]{1,0:T(8,128)(2,1)} %param.7), channel_id=1, source_target_pairs={{0,8},{1,9},{2,10},{3,11},{4,12},{5,13},{6,14},{7,15},{8,0},{9,1},... | collective-permute-start | bytes 294920 | tf_op jit(solution)/shard_map/ppermute | solution.py:235
  4.0 1.3 %collective-permute-start.1 = (bf16[48,1024]{1,0:T(8,128)(2,1)}, bf16[48,1024]{1,0:T(8,128)(2,1)S(1)}, u32[]{:S(2)}, u32[]{:S(2)}) collective-permute-start(bf16[48,1024]{1,0:T(8,128)(2,1)} %param.7), channel_id=1, source_target_pairs={{0,12},{1,13},{2,14},{3,15},{4,8},{5,9},{6,10},{7,11},{8,4},{9,5},... | collective-permute-start | bytes 294920 | tf_op jit(solution)/shard_map/ppermute | solution.py:235
  5.4 2.4 %collective-permute-start.6 = (bf16[48,1024]{1,0:T(8,128)(2,1)}, bf16[48,1024]{1,0:T(8,128)(2,1)S(1)}, u32[]{:S(2)}, u32[]{:S(2)}) collective-permute-start(bf16[48,1024]{1,0:T(8,128)(2,1)} %param.7), channel_id=1, source_target_pairs={{0,18},{1,19},{2,16},{3,17},{4,22},{5,23},{6,20},{7,21},{8,26},{9,... | collective-permute-start | bytes 294920 | tf_op jit(solution)/shard_map/ppermute | solution.py:235
  7.8 0.5 %collective-permute-start.7 = (bf16[48,1024]{1,0:T(8,128)(2,1)}, bf16[48,1024]{1,0:T(8,128)(2,1)S(1)}, u32[]{:S(2)}, u32[]{:S(2)}) collective-permute-start(bf16[48,1024]{1,0:T(8,128)(2,1)} %param.7), channel_id=1, source_target_pairs={{0,2},{1,3},{2,0},{3,1},{4,6},{5,7},{6,4},{7,5},{8,10},{9,11},{10,... | collective-permute-start | bytes 294920 | tf_op jit(solution)/shard_map/ppermute | solution.py:235
  8.3 0.5 %collective-permute-start.8 = (bf16[48,1024]{1,0:T(8,128)(2,1)}, bf16[48,1024]{1,0:T(8,128)(2,1)S(1)}, u32[]{:S(2)}, u32[]{:S(2)}) collective-permute-start(bf16[48,1024]{1,0:T(8,128)(2,1)} %param.7), channel_id=1, source_target_pairs={{0,16},{1,17},{2,18},{3,19},{4,20},{5,21},{6,22},{7,23},{8,24},{9,... | collective-permute-start | bytes 294920 | tf_op jit(solution)/shard_map/ppermute | solution.py:235
  8.9 0.9 %constant_dynamic-update-slice_fusion.12 = bf16[384,1024]{1,0:T(8,128)(2,1)S(1)} fusion(bf16[48,1024]{1,0:T(8,128)(2,1)} %param.7), kind=kLoop, calls=%fused_computation.13 | loop fusion | bytes 196608
  9.8 2.3 %collective-permute-done = bf16[48,1024]{1,0:T(8,128)(2,1)S(1)} collective-permute-done((bf16[48,1024]{1,0:T(8,128)(2,1)}, bf16[48,1024]{1,0:T(8,128)(2,1)S(1)}, u32[]{:S(2)}, u32[]{:S(2)}) %collective-permute-start) | collective-permute-done | bytes 98336 | tf_op jit(solution)/shard_map/ppermute | solution.py:235
  12.2 0.0 collective-permute-start.9
  12.2 2.7 %collective-permute-start.2 = (bf16[96,1024]{1,0:T(8,128)(2,1)S(1)}, bf16[96,1024]{1,0:T(8,128)(2,1)S(1)}, u32[]{:S(2)}, u32[]{:S(2)}) collective-permute-start(bf16[96,1024]{1,0:T(8,128)(2,1)S(1)} %get-tuple-element.11), channel_id=1, source_target_pairs={{0,18},{1,19},{2,16},{3,17},{4,22},{5,23},{6,20},{7,21},{8,26},{9,... | collective-permute-start | bytes 589832 | tf_op jit(solution)/shard_map/ppermute | solution.py:235
  14.9 0.5 %collective-permute-start.3 = (bf16[96,1024]{1,0:T(8,128)(2,1)S(1)}, bf16[96,1024]{1,0:T(8,128)(2,1)S(1)}, u32[]{:S(2)}, u32[]{:S(2)}) collective-permute-start(bf16[96,1024]{1,0:T(8,128)(2,1)S(1)} %get-tuple-element.11), channel_id=1, source_target_pairs={{0,2},{1,3},{2,0},{3,1},{4,6},{5,7},{6,4},{7,5},{8,10},{9,11},{10,... | collective-permute-start | bytes 589832 | tf_op jit(solution)/shard_map/ppermute | solution.py:235
  15.4 0.4 %collective-permute-start.4 = (bf16[96,1024]{1,0:T(8,128)(2,1)S(1)}, bf16[96,1024]{1,0:T(8,128)(2,1)S(1)}, u32[]{:S(2)}, u32[]{:S(2)}) collective-permute-start(bf16[96,1024]{1,0:T(8,128)(2,1)S(1)} %get-tuple-element.11), channel_id=1, source_target_pairs={{0,16},{1,17},{2,18},{3,19},{4,20},{5,21},{6,22},{7,23},{8,24},{9,... | collective-permute-start | bytes 589832 | tf_op jit(solution)/shard_map/ppermute | solution.py:235
  15.8 2.1 %collective-permute-start.10 = (bf16[144,1024]{1,0:T(8,128)(2,1)S(1)}, bf16[144,1024]{1,0:T(8,128)(2,1)S(1)}, u32[]{:S(2)}, u32[]{:S(2)}) collective-permute-start(bf16[144,1024]{1,0:T(8,128)(2,1)S(1)} %pad_maximum_fusion), channel_id=1, source_target_pairs={{0,4},{1,5},{2,6},{3,7},{4,0},{5,1},{6,2},{7,3},{8,12},{9,13},{10,... | collective-permute-start | bytes 884744 | tf_op jit(solution)/shard_map/ppermute | solution.py:235
  18.0 3.1 %collective-permute-done.2 = bf16[96,1024]{1,0:T(8,128)(2,1)S(1)} collective-permute-done((bf16[96,1024]{1,0:T(8,128)(2,1)S(1)}, bf16[96,1024]{1,0:T(8,128)(2,1)S(1)}, u32[]{:S(2)}, u32[]{:S(2)}) %collective-permute-start.2) | collective-permute-done | bytes 196640 | tf_op jit(solution)/shard_map/ppermute | solution.py:235
  21.1 2.8 %collective-permute-done.3 = bf16[96,1024]{1,0:T(8,128)(2,1)S(1)} collective-permute-done((bf16[96,1024]{1,0:T(8,128)(2,1)S(1)}, bf16[96,1024]{1,0:T(8,128)(2,1)S(1)}, u32[]{:S(2)}, u32[]{:S(2)}) %collective-permute-start.3) | collective-permute-done | bytes 196640 | tf_op jit(solution)/shard_map/ppermute | solution.py:235
  23.9 0.1 collective-permute-done.4
  24.0 0.0 copy-start
  24.0 0.0 copy-start.2
  24.0 0.1 collective-permute-start.5
  24.1 0.1 collective-permute-done.10
  24.2 0.5 %collective-permute-start.11 = (bf16[384,1024]{1,0:T(8,128)(2,1)S(1)}, bf16[384,1024]{1,0:T(8,128)(2,1)S(1)}, u32[]{:S(2)}, u32[]{:S(2)}) collective-permute-start(bf16[384,1024]{1,0:T(8,128)(2,1)S(1)} %constant_dynamic-update-slice_fusion.7.refs_0_), channel_id=1, source_target_pairs={{0,1},{1,0},{2,3},{3,2},{4,5},{5,4},{6,7},{7,6},{8,9},{9,8},{10,11... | collective-permute-start | bytes 2359304 | tf_op jit(solution)/shard_map/ppermute | solution.py:235
  24.7 0.2 copy-done
  25.0 2.2 %shard_map.64 = (f32[1152,128]{1,0:T(8,128)S(1)}, f32[1152,128]{1,0:T(8,128)S(1)}, f32[1,3072]{1,0:T(1,128)S(1)}) custom-call(s32[2]{0:T(128)S(1)} %copy-done.2, s32[2]{0:T(128)S(1)} %copy-done.3, s32[2]{0:T(128)S(1)} %copy-done.4, bf16[48,3072]{1,0:T(8,128)(2,1)S(1)} %copy-done, bf16[384,1024]{1,0:T(8,128)(2,1)S(1)} %constant_dynamic-update-slice_fusion.7.refs_0_, ...), custom_call_target="tpu_custom_call" | custom-call | flops 452984832 | bytes 1572864 | tf_op jit(solution)/shard_map/pallas_call | solution.py:127
  27.2 0.3 %collective-permute-done.11.refs_1_ = bf16[384,1024]{1,0:T(8,128)(2,1)S(1)} collective-permute-done((bf16[384,1024]{1,0:T(8,128)(2,1)S(1)}, bf16[384,1024]{1,0:T(8,128)(2,1)S(1)}, u32[]{:S(2)}, u32[]{:S(2)}) %collective-permute-start.11) | collective-permute-done | bytes 786464 | tf_op jit(solution)/shard_map/ppermute | solution.py:235
  27.5 2.9 %shard_map.65 = bf16[48,3072]{1,0:T(8,128)(2,1)} custom-call(s32[2]{0:T(128)S(1)} %copy-done.2, s32[2]{0:T(128)S(1)} %copy-done.3, s32[2]{0:T(128)S(1)} %copy-done.4, bf16[48,3072]{1,0:T(8,128)(2,1)S(1)} %copy-done, bf16[384,1024]{1,0:T(8,128)(2,1)S(1)} %collective-permute-done.5.refs_0_, bf16[384,1024]{1,0:T(8,128)(2,1)S(1)} %collective-permute-done.11.refs_1_, ...), custom_call_target="tpu_custom_call" | custom-call | flops 452984832 | bytes 1572864 | tf_op jit(solution)/shard_map/pallas_call | solution.py:127
  (26 shorter events, 0.2 us)
Async XLA Ops:
  0.0 12.2 %copy-start.5 = (bf16[48,1024]{1,0:T(8,128)(2,1)S(1)}, bf16[48,1024]{1,0:T(8,128)(2,1)}, u32[]{:S(2)}) copy-start(bf16[48,1024]{1,0:T(8,128)(2,1)} %param.7) | copy-start | bytes 294916
  0.0 12.2 %collective-permute-start = (bf16[48,1024]{1,0:T(8,128)(2,1)}, bf16[48,1024]{1,0:T(8,128)(2,1)S(1)}, u32[]{:S(2)}, u32[]{:S(2)}) collective-permute-start(bf16[48,1024]{1,0:T(8,128)(2,1)} %param.7), channel_id=1, source_target_pairs={{0,8},{1,9},{2,10},{3,11},{4,12},{5,13},{6,14},{7,15},{8,0},{9,1},... | collective-permute-start | bytes 294920 | tf_op jit(solution)/shard_map/ppermute | solution.py:235
  4.0 8.2 %collective-permute-start.1 = (bf16[48,1024]{1,0:T(8,128)(2,1)}, bf16[48,1024]{1,0:T(8,128)(2,1)S(1)}, u32[]{:S(2)}, u32[]{:S(2)}) collective-permute-start(bf16[48,1024]{1,0:T(8,128)(2,1)} %param.7), channel_id=1, source_target_pairs={{0,12},{1,13},{2,14},{3,15},{4,8},{5,9},{6,10},{7,11},{8,4},{9,5},... | collective-permute-start | bytes 294920 | tf_op jit(solution)/shard_map/ppermute | solution.py:235
  5.4 9.5 %collective-permute-start.6 = (bf16[48,1024]{1,0:T(8,128)(2,1)}, bf16[48,1024]{1,0:T(8,128)(2,1)S(1)}, u32[]{:S(2)}, u32[]{:S(2)}) collective-permute-start(bf16[48,1024]{1,0:T(8,128)(2,1)} %param.7), channel_id=1, source_target_pairs={{0,18},{1,19},{2,16},{3,17},{4,22},{5,23},{6,20},{7,21},{8,26},{9,... | collective-permute-start | bytes 294920 | tf_op jit(solution)/shard_map/ppermute | solution.py:235
  7.8 7.6 %collective-permute-start.7 = (bf16[48,1024]{1,0:T(8,128)(2,1)}, bf16[48,1024]{1,0:T(8,128)(2,1)S(1)}, u32[]{:S(2)}, u32[]{:S(2)}) collective-permute-start(bf16[48,1024]{1,0:T(8,128)(2,1)} %param.7), channel_id=1, source_target_pairs={{0,2},{1,3},{2,0},{3,1},{4,6},{5,7},{6,4},{7,5},{8,10},{9,11},{10,... | collective-permute-start | bytes 294920 | tf_op jit(solution)/shard_map/ppermute | solution.py:235
  8.3 7.5 %collective-permute-start.8 = (bf16[48,1024]{1,0:T(8,128)(2,1)}, bf16[48,1024]{1,0:T(8,128)(2,1)S(1)}, u32[]{:S(2)}, u32[]{:S(2)}) collective-permute-start(bf16[48,1024]{1,0:T(8,128)(2,1)} %param.7), channel_id=1, source_target_pairs={{0,16},{1,17},{2,18},{3,19},{4,20},{5,21},{6,22},{7,23},{8,24},{9,... | collective-permute-start | bytes 294920 | tf_op jit(solution)/shard_map/ppermute | solution.py:235
  12.2 5.8 %collective-permute-start.9 = (bf16[48,1024]{1,0:T(8,128)(2,1)S(1)}, bf16[48,1024]{1,0:T(8,128)(2,1)S(1)}, u32[]{:S(2)}, u32[]{:S(2)}) collective-permute-start(bf16[48,1024]{1,0:T(8,128)(2,1)S(1)} %copy-done.5), channel_id=1, source_target_pairs={{0,4},{1,5},{2,6},{3,7},{4,0},{5,1},{6,2},{7,3},{8,12},{9,13},{10,... | collective-permute-start | bytes 294920 | tf_op jit(solution)/shard_map/ppermute | solution.py:235
  12.2 8.8 %collective-permute-start.2 = (bf16[96,1024]{1,0:T(8,128)(2,1)S(1)}, bf16[96,1024]{1,0:T(8,128)(2,1)S(1)}, u32[]{:S(2)}, u32[]{:S(2)}) collective-permute-start(bf16[96,1024]{1,0:T(8,128)(2,1)S(1)} %get-tuple-element.11), channel_id=1, source_target_pairs={{0,18},{1,19},{2,16},{3,17},{4,22},{5,23},{6,20},{7,21},{8,26},{9,... | collective-permute-start | bytes 589832 | tf_op jit(solution)/shard_map/ppermute | solution.py:235
  14.9 9.0 %collective-permute-start.3 = (bf16[96,1024]{1,0:T(8,128)(2,1)S(1)}, bf16[96,1024]{1,0:T(8,128)(2,1)S(1)}, u32[]{:S(2)}, u32[]{:S(2)}) collective-permute-start(bf16[96,1024]{1,0:T(8,128)(2,1)S(1)} %get-tuple-element.11), channel_id=1, source_target_pairs={{0,2},{1,3},{2,0},{3,1},{4,6},{5,7},{6,4},{7,5},{8,10},{9,11},{10,... | collective-permute-start | bytes 589832 | tf_op jit(solution)/shard_map/ppermute | solution.py:235
  15.4 8.6 %collective-permute-start.4 = (bf16[96,1024]{1,0:T(8,128)(2,1)S(1)}, bf16[96,1024]{1,0:T(8,128)(2,1)S(1)}, u32[]{:S(2)}, u32[]{:S(2)}) collective-permute-start(bf16[96,1024]{1,0:T(8,128)(2,1)S(1)} %get-tuple-element.11), channel_id=1, source_target_pairs={{0,16},{1,17},{2,18},{3,19},{4,20},{5,21},{6,22},{7,23},{8,24},{9,... | collective-permute-start | bytes 589832 | tf_op jit(solution)/shard_map/ppermute | solution.py:235
  15.8 8.4 %collective-permute-start.10 = (bf16[144,1024]{1,0:T(8,128)(2,1)S(1)}, bf16[144,1024]{1,0:T(8,128)(2,1)S(1)}, u32[]{:S(2)}, u32[]{:S(2)}) collective-permute-start(bf16[144,1024]{1,0:T(8,128)(2,1)S(1)} %pad_maximum_fusion), channel_id=1, source_target_pairs={{0,4},{1,5},{2,6},{3,7},{4,0},{5,1},{6,2},{7,3},{8,12},{9,13},{10,... | collective-permute-start | bytes 884744 | tf_op jit(solution)/shard_map/ppermute | solution.py:235
  21.0 3.7 %copy-start.1 = (f32[64,3072]{1,0:T(8,128)S(1)}, f32[64,3072]{1,0:T(8,128)}, u32[]{:S(2)}) copy-start(f32[64,3072]{1,0:T(8,128)} %refs_2_.1) | copy-start | bytes 2359300
  24.0 1.0 %copy-start = (bf16[48,3072]{1,0:T(8,128)(2,1)S(1)}, bf16[48,3072]{1,0:T(8,128)(2,1)}, u32[]{:S(2)}) copy-start(bf16[48,3072]{1,0:T(8,128)(2,1)} %q_ref.3) | copy-start | bytes 884740
  24.0 1.0 %copy-start.2 = (s32[2]{0:T(128)S(1)}, s32[2]{0:T(128)}, u32[]{:S(2)}) copy-start(s32[2]{0:T(128)} %clip_ref.3) | copy-start | bytes 28
  24.0 0.9 %copy-start.3 = (s32[2]{0:T(128)S(1)}, s32[2]{0:T(128)}, u32[]{:S(2)}) copy-start(s32[2]{0:T(128)} %valid_ref.3) | copy-start | bytes 28
  24.0 0.9 %copy-start.4 = (s32[2]{0:T(128)S(1)}, s32[2]{0:T(128)}, u32[]{:S(2)}) copy-start(s32[2]{0:T(128)} %step_ref.3) | copy-start | bytes 28
  24.0 3.2 %collective-permute-start.5 = (bf16[384,1024]{1,0:T(8,128)(2,1)S(1)}, bf16[384,1024]{1,0:T(8,128)(2,1)S(1)}, u32[]{:S(2)}, u32[]{:S(2)}) collective-permute-start(bf16[384,1024]{1,0:T(8,128)(2,1)S(1)} %constant_dynamic-update-slice_fusion.2.refs_1_), channel_id=1, source_target_pairs={{0,1},{1,0},{2,3},{3,2},{4,5},{5,4},{6,7},{7,6},{8,9},{9,8},{10,11... | collective-permute-start | bytes 2359304 | tf_op jit(solution)/shard_map/ppermute | solution.py:235
  24.2 3.3 %collective-permute-start.11 = (bf16[384,1024]{1,0:T(8,128)(2,1)S(1)}, bf16[384,1024]{1,0:T(8,128)(2,1)S(1)}, u32[]{:S(2)}, u32[]{:S(2)}) collective-permute-start(bf16[384,1024]{1,0:T(8,128)(2,1)S(1)} %constant_dynamic-update-slice_fusion.7.refs_0_), channel_id=1, source_target_pairs={{0,1},{1,0},{2,3},{3,2},{4,5},{5,4},{6,7},{7,6},{8,9},{9,8},{10,11... | collective-permute-start | bytes 2359304 | tf_op jit(solution)/shard_map/ppermute | solution.py:235

commit v6 on v5

--- a/solution.py
+++ b/solution.py
@@ -34,75 +34,90 @@
     return jnp.where(lane < bound, 0.0, NEGATIVE).astype(jnp.float32)
 
 
-def attend_kernel(orders, stage, n_seq, clip_ref, valid_ref, step_ref, q_ref, *refs):
+def attend_kernel(orders, groups, stage, n_seq, clip_ref, valid_ref, step_ref, q_ref, *refs):
     kv_refs, refs = refs[: len(orders)], refs[len(orders) :]
-    opens, closes = stage == "first", stage == "last"
+    opens = stage == "first"
     tokens = q_ref.shape[0]
     rows = RATIO * tokens
     scale = LOG2E / math.sqrt(HEAD_WIDTH)
     heads = range(KEY_VALUE_HEADS)
     columns = [slice(h * HEAD_WIDTH, (h + 1) * HEAD_WIDTH) for h in range(QUERY_HEADS)]
+    span_id = lax.axis_index("span")
     if opens:
         table_ref, top_out, part_out, gate_out, gate_ref, gate_sem = refs
-        step = step_ref[lax.axis_index("span")]
+        step = step_ref[span_id]
         first = pl.multiple_of(step - step % GATE_ROWS, GATE_ROWS)
         fetch = pltpu.make_async_copy(table_ref.at[pl.ds(first, GATE_ROWS)], gate_ref, gate_sem)
         fetch.start()
     else:
         top_in, part_in, gate_ref, out_ref, staged_ref, out_sem = refs
         position = lax.axis_index("seq") * tokens + lax.broadcasted_iota(jnp.int32, (tokens, 1), 0)
-        live = (position < valid_ref[lax.axis_index("span")]).astype(jnp.float32)
-    biases = [key_bias(order, tokens, n_seq, clip_ref, valid_ref) for order in orders]
-    scores, tops, writes = {}, {}, []
-    for h in heads:
-        query = jnp.concatenate([q_ref[:, c] for c in columns[h * RATIO : (h + 1) * RATIO]], axis=0)
-        for i, kv_ref in enumerate(kv_refs):
-            products = lax.dot_general(
-                query, kv_ref[:, columns[h]], (((1,), (1,)), ((), ())), preferred_element_type=jnp.float32
+        live = (position < valid_ref[span_id]).astype(jnp.float32)
+
+    def run(groups):
+        def joined(group, c):
+            return jnp.concatenate([kv_refs[i][start:stop, c] for i, start, stop in group], axis=0)
+
+        biases = []
+        for group in groups:
+            order = [d for i, start, stop in group for d in orders[i][start // tokens : stop // tokens]]
+            biases.append(key_bias(order, tokens, n_seq, clip_ref, valid_ref))
+        scores, tops, writes = {}, {}, []
+        for h in heads:
+            query = jnp.concatenate([q_ref[:, c] for c in columns[h * RATIO : (h + 1) * RATIO]], axis=0)
+            for g, group in enumerate(groups):
+                products = lax.dot_general(
+                    query,
+                    joined(group, columns[h]),
+                    (((1,), (1,)), ((), ())),
+                    preferred_element_type=jnp.float32,
+                )
+                scores[h, g] = products * scale + biases[g]
+        for h in heads:
+            found = [jnp.max(scores[h, g], axis=1, keepdims=True) for g in range(len(groups))]
+            top = jnp.broadcast_to(functools.reduce(jnp.maximum, found), (rows, HEAD_WIDTH))
+            tops[h] = top if opens else jnp.maximum(top, top_in[h * rows : (h + 1) * rows, :])
+        for h in heads:
+            span = slice(h * rows, (h + 1) * rows)
+            sums = 0.0
+            for g, group in enumerate(groups):
+                repeats = scores[h, g].shape[1] // HEAD_WIDTH
+                weights = jnp.exp2(scores[h, g] - jnp.concatenate([tops[h]] * repeats, axis=1))
+                value = joined(group, columns[KEY_VALUE_HEADS + h])
+                value = jnp.concatenate([value, jnp.ones_like(value)], axis=1)
+                sums = sums + jnp.dot(
+                    weights.astype(jnp.bfloat16), value, preferred_element_type=jnp.float32
+                )
+            numerator, total = sums[:, :HEAD_WIDTH], sums[:, HEAD_WIDTH:]
+            if not opens:
+                factor = jnp.exp2(top_in[span, :] - tops[h])
+                total = total + factor
+                numerator = numerator + part_in[span, :] * factor
+            result = numerator * (1.0 / total)
+            if opens:
+                top_out[span, :] = tops[h] + jnp.log2(total)
+                part_out[span, :] = result
+                continue
+            for r in range(RATIO):
+                c = columns[h * RATIO + r]
+                part = result[r * tokens : (r + 1) * tokens]
+                staged_ref[:, c] = (part * gate_ref[:, c] * live).astype(out_ref.dtype)
+            group = slice(h * RATIO * HEAD_WIDTH, (h + 1) * RATIO * HEAD_WIDTH)
+            writes.append(
+                pltpu.make_async_copy(staged_ref.at[:, group], out_ref.at[:, group], out_sem.at[h])
             )
-            scores[h, i] = products * scale + biases[i]
-    for h in heads:
-        found = [jnp.max(scores[h, i], axis=1, keepdims=True) for i in range(len(orders))]
-        top = jnp.broadcast_to(functools.reduce(jnp.maximum, found), (rows, HEAD_WIDTH))
-        tops[h] = top if opens else jnp.maximum(top, top_in[h * rows : (h + 1) * rows, :])
-    for h in heads:
-        span = slice(h * rows, (h + 1) * rows)
-        total, numerator = jnp.zeros((rows, HEAD_WIDTH), jnp.float32), 0.0
-        for i, kv_ref in enumerate(kv_refs):
-            repeats = scores[h, i].shape[1] // HEAD_WIDTH
-            weights = jnp.exp2(scores[h, i] - jnp.concatenate([tops[h]] * repeats, axis=1))
-            numerator = numerator + jnp.dot(
-                weights.astype(jnp.bfloat16),
-                jnp.concatenate([kv_ref[:, columns[KEY_VALUE_HEADS + h]], jnp.ones((kv_ref.shape[0], HEAD_WIDTH), jnp.bfloat16)], axis=1),
-                preferred_element_type=jnp.float32,
-            )
-        total, numerator = numerator[:, HEAD_WIDTH:], numerator[:, :HEAD_WIDTH]
-        if not opens:
-            factor = jnp.exp2(top_in[span, :] - tops[h])
-            total = total + factor
-            numerator = numerator + part_in[span, :] * factor
-        result = numerator * (1.0 / total)
-        if not closes:
-            top_out[span, :] = tops[h] + jnp.log2(total)
-            part_out[span, :] = result
-            continue
-        for r in range(RATIO):
-            c = columns[h * RATIO + r]
-            staged_ref[:, c] = (result[r * tokens : (r + 1) * tokens] * gate_ref[:, c] * live).astype(
-                out_ref.dtype
-            )
-        group = slice(h * RATIO * HEAD_WIDTH, (h + 1) * RATIO * HEAD_WIDTH)
-        writes.append(pltpu.make_async_copy(staged_ref.at[:, group], out_ref.at[:, group], out_sem.at[h]))
-        writes[-1].start()
+            writes[-1].start()
+        for write in writes:
+            write.wait()
+
+    run(groups)
     if opens:
         fetch.wait()
         chosen = lax.broadcasted_iota(jnp.int32, (GATE_ROWS, 1), 0) == step % GATE_ROWS
         gate_out[...] = jnp.sum(jnp.where(chosen, gate_ref[...], 0.0), axis=0, keepdims=True)
-    for write in writes:
-        write.wait()
-
-
-def attend(scalars, queries, keyvals, orders, n_seq, stage, *carried):
+
+
+def attend(scalars, queries, keyvals, orders, groups, n_seq, stage, *carried):
     rows = QUERY_HEADS * queries.shape[0]
     keys = sum(kv.shape[0] for kv in keyvals)
     smem, vmem = pl.BlockSpec(memory_space=pltpu.SMEM), pl.BlockSpec(memory_space=pltpu.VMEM)
@@ -125,7 +140,7 @@
         out_specs.append(vmem)
         scratch = [pltpu.VMEM((GATE_ROWS, queries.shape[1]), jnp.float32), pltpu.SemaphoreType.DMA]
     return pl.pallas_call(
-        functools.partial(attend_kernel, orders, stage, n_seq),
+        functools.partial(attend_kernel, orders, groups, stage, n_seq),
         out_shape=out_shape,
         in_specs=in_specs,
         out_specs=out_specs,
@@ -237,20 +252,22 @@
     plane = [n_seq + 2, 2, n_seq]
     away = jnp.concatenate([exchange(keyvals, d) for d in far[2:]], axis=0)
     column = exchange(keyvals, far[1])
-    home = jnp.concatenate([keyvals] + [exchange(keyvals, d) for d in plane], axis=0)
-    near = jnp.concatenate([home, column, exchange(home[tokens:], far[1])], axis=0)
-    away = jnp.concatenate([away] + [exchange(away, d) for d in plane], axis=0)
-    near_order = [z ^ p for z in far[:2] for p in [0] + plane]
+    received = [exchange(keyvals, d) for d in plane]
+    passed = exchange(jnp.concatenate(received, axis=0), far[1])
+    spread = [away] + [exchange(away, d) for d in plane]
     away_order = [p ^ z for p in [0] + plane for z in far[2:]]
+    home_order = [0] + plane + [far[1]]
+    passed_order = [far[1] ^ p for p in plane]
     twin = lambda order: [d ^ 1 for d in order]
-    near_twin, away_twin = exchange(near, 1), exchange(away, 1)
     scalars = (clip_index, valid_count, noise_step)
-    *state, gate = attend(
-        scalars, queries, [near, away], [near_order, away_order], n_seq, "first", gate_table
-    )
-    return attend(
-        scalars, queries, [away_twin, near_twin], [twin(away_order), twin(near_order)], n_seq, "last", *state, gate
-    )
+    n_away, n_home, n_passed = (len(o) * tokens for o in (away_order, home_order, passed_order))
+    pieces = [jnp.concatenate(spread, axis=0), jnp.concatenate([keyvals] + received + [column], axis=0), passed]
+    orders = [away_order, home_order, passed_order]
+    groups = [[(0, 0, n_away)], [(1, 0, n_home), (2, 0, n_passed)]]
+    twins = [exchange(x, 1) for x in pieces]
+    *state, gate = attend(scalars, queries, pieces, orders, groups, n_seq, "first", gate_table)
+    orders = [twin(o) for o in orders]
+    return attend(scalars, queries, twins, orders, groups, n_seq, "last", *state, gate)
 
 
 def solution(mesh):

time: 31 us -> 30.9 us (level)
    ppermute x12 -> x13, starting transfers between devices: 15 us -> 15.2 us  [exchange(): return lax.ppermute(block, ('span', 'seq'), pairs)]
    unnamed x20 -> x19, local copies, waits for them, and re-layouts: 1.28 us -> 1.17 us
    ppermute x12 -> x13, waiting for transfers between devices: 8.73 us -> 8.65 us  [exchange(): return lax.ppermute(block, ('span', 'seq'), pairs)]
  transfers between devices with their start and end apart: 12 -> 13, of which waited for: 6 -> 5; matrix products, arithmetic and copies ran while one was open for 4% -> 3% of each run, Pallas kernels for 7% -> 7%
where the time goes in v6:
time: 30.9 us; the launch traced here: 30.4 us
  starting transfers between devices  15.2 us (49%)
  waiting for transfers between devices  8.65 us (28%)
  Pallas kernels  5.12 us (17%)
  local copies, waits for them, and re-layouts  1.21 us (4%)
    ppermute x13, starting transfers between devices, exchange(): return lax.ppermute(block, ('span', 'seq'), pairs)  15.2 us
    ppermute x13, waiting for transfers between devices, exchange(): return lax.ppermute(block, ('span', 'seq'), pairs)  8.65 us
    pallas_call x2, Pallas kernels, attend(): pl.pallas_call(functools.partial(attend_kernel, orders, groups, stage, n_...  5.12 us
    unnamed x19, local copies, waits for them, and re-layouts  1.17 us
  transfers between devices with their start and end apart: 13, of which 5 were waited for; matrix products, arithmetic and copies ran while one was open for 3% of the time, Pallas kernels for 7%

profile of v6, /device:TPU:0, one launch (start us, length us, event | category | flops | bytes accessed | tf_op | source)
XLA Modules:
  0.0 30.4 jit_solution(11544512680432230560)
XLA Ops:
  0.0 4.0 %collective-permute-start = (bf16[48,1024]{1,0:T(8,128)(2,1)}, bf16[48,1024]{1,0:T(8,128)(2,1)S(1)}, u32[]{:S(2)}, u32[]{:S(2)}) collective-permute-start(bf16[48,1024]{1,0:T(8,128)(2,1)} %param.7), channel_id=1, source_target_pairs={{0,8},{1,9},{2,10},{3,11},{4,12},{5,13},{6,14},{7,15},{8,0},{9,1},... | collective-permute-start | bytes 294920 | tf_op jit(solution)/shard_map/ppermute | solution.py:250
  4.0 1.3 %collective-permute-start.1 = (bf16[48,1024]{1,0:T(8,128)(2,1)}, bf16[48,1024]{1,0:T(8,128)(2,1)S(1)}, u32[]{:S(2)}, u32[]{:S(2)}) collective-permute-start(bf16[48,1024]{1,0:T(8,128)(2,1)} %param.7), channel_id=1, source_target_pairs={{0,12},{1,13},{2,14},{3,15},{4,8},{5,9},{6,10},{7,11},{8,4},{9,5},... | collective-permute-start | bytes 294920 | tf_op jit(solution)/shard_map/ppermute | solution.py:250
  5.4 2.4 %collective-permute-start.6 = (bf16[48,1024]{1,0:T(8,128)(2,1)}, bf16[48,1024]{1,0:T(8,128)(2,1)S(1)}, u32[]{:S(2)}, u32[]{:S(2)}) collective-permute-start(bf16[48,1024]{1,0:T(8,128)(2,1)} %param.7), channel_id=1, source_target_pairs={{0,18},{1,19},{2,16},{3,17},{4,22},{5,23},{6,20},{7,21},{8,26},{9,... | collective-permute-start | bytes 294920 | tf_op jit(solution)/shard_map/ppermute | solution.py:250
  7.8 0.5 %collective-permute-start.7 = (bf16[48,1024]{1,0:T(8,128)(2,1)}, bf16[48,1024]{1,0:T(8,128)(2,1)S(1)}, u32[]{:S(2)}, u32[]{:S(2)}) collective-permute-start(bf16[48,1024]{1,0:T(8,128)(2,1)} %param.7), channel_id=1, source_target_pairs={{0,2},{1,3},{2,0},{3,1},{4,6},{5,7},{6,4},{7,5},{8,10},{9,11},{10,... | collective-permute-start | bytes 294920 | tf_op jit(solution)/shard_map/ppermute | solution.py:250
  8.3 0.5 %collective-permute-start.8 = (bf16[48,1024]{1,0:T(8,128)(2,1)}, bf16[48,1024]{1,0:T(8,128)(2,1)S(1)}, u32[]{:S(2)}, u32[]{:S(2)}) collective-permute-start(bf16[48,1024]{1,0:T(8,128)(2,1)} %param.7), channel_id=1, source_target_pairs={{0,16},{1,17},{2,18},{3,19},{4,20},{5,21},{6,22},{7,23},{8,24},{9,... | collective-permute-start | bytes 294920 | tf_op jit(solution)/shard_map/ppermute | solution.py:250
  8.9 0.9 %constant_dynamic-update-slice_fusion.11 = bf16[240,1024]{1,0:T(8,128)(2,1)S(1)} fusion(bf16[48,1024]{1,0:T(8,128)(2,1)} %param.7), kind=kLoop, calls=%fused_computation.12 | loop fusion | bytes 196608
  9.8 2.3 %collective-permute-done = bf16[48,1024]{1,0:T(8,128)(2,1)S(1)} collective-permute-done((bf16[48,1024]{1,0:T(8,128)(2,1)}, bf16[48,1024]{1,0:T(8,128)(2,1)S(1)}, u32[]{:S(2)}, u32[]{:S(2)}) %collective-permute-start) | collective-permute-done | bytes 98336 | tf_op jit(solution)/shard_map/ppermute | solution.py:250
  12.2 0.0 collective-permute-start.9
  12.2 2.7 %collective-permute-start.2 = (bf16[96,1024]{1,0:T(8,128)(2,1)S(1)}, bf16[96,1024]{1,0:T(8,128)(2,1)S(1)}, u32[]{:S(2)}, u32[]{:S(2)}) collective-permute-start(bf16[96,1024]{1,0:T(8,128)(2,1)S(1)} %get-tuple-element.11), channel_id=1, source_target_pairs={{0,18},{1,19},{2,16},{3,17},{4,22},{5,23},{6,20},{7,21},{8,26},{9,... | collective-permute-start | bytes 589832 | tf_op jit(solution)/shard_map/ppermute | solution.py:250
  14.9 0.5 %collective-permute-start.3 = (bf16[96,1024]{1,0:T(8,128)(2,1)S(1)}, bf16[96,1024]{1,0:T(8,128)(2,1)S(1)}, u32[]{:S(2)}, u32[]{:S(2)}) collective-permute-start(bf16[96,1024]{1,0:T(8,128)(2,1)S(1)} %get-tuple-element.11), channel_id=1, source_target_pairs={{0,2},{1,3},{2,0},{3,1},{4,6},{5,7},{6,4},{7,5},{8,10},{9,11},{10,... | collective-permute-start | bytes 589832 | tf_op jit(solution)/shard_map/ppermute | solution.py:250
  15.4 0.4 %collective-permute-start.4 = (bf16[96,1024]{1,0:T(8,128)(2,1)S(1)}, bf16[96,1024]{1,0:T(8,128)(2,1)S(1)}, u32[]{:S(2)}, u32[]{:S(2)}) collective-permute-start(bf16[96,1024]{1,0:T(8,128)(2,1)S(1)} %get-tuple-element.11), channel_id=1, source_target_pairs={{0,16},{1,17},{2,18},{3,19},{4,20},{5,21},{6,22},{7,23},{8,24},{9,... | collective-permute-start | bytes 589832 | tf_op jit(solution)/shard_map/ppermute | solution.py:250
  15.8 2.1 %collective-permute-start.11 = (bf16[144,1024]{1,0:T(8,128)(2,1)S(1)}, bf16[144,1024]{1,0:T(8,128)(2,1)S(1)}, u32[]{:S(2)}, u32[]{:S(2)}) collective-permute-start(bf16[144,1024]{1,0:T(8,128)(2,1)S(1)} %pad_maximum_fusion), channel_id=1, source_target_pairs={{0,4},{1,5},{2,6},{3,7},{4,0},{5,1},{6,2},{7,3},{8,12},{9,13},{10,... | collective-permute-start | bytes 884744 | tf_op jit(solution)/shard_map/ppermute | solution.py:250
  17.9 3.1 %collective-permute-done.2 = bf16[96,1024]{1,0:T(8,128)(2,1)S(1)} collective-permute-done((bf16[96,1024]{1,0:T(8,128)(2,1)S(1)}, bf16[96,1024]{1,0:T(8,128)(2,1)S(1)}, u32[]{:S(2)}, u32[]{:S(2)}) %collective-permute-start.2) | collective-permute-done | bytes 196640 | tf_op jit(solution)/shard_map/ppermute | solution.py:250
  21.0 0.0 copy-start.1
  21.1 2.8 %collective-permute-done.3 = bf16[96,1024]{1,0:T(8,128)(2,1)S(1)} collective-permute-done((bf16[96,1024]{1,0:T(8,128)(2,1)S(1)}, bf16[96,1024]{1,0:T(8,128)(2,1)S(1)}, u32[]{:S(2)}, u32[]{:S(2)}) %collective-permute-start.3) | collective-permute-done | bytes 196640 | tf_op jit(solution)/shard_map/ppermute | solution.py:250
  23.9 0.1 collective-permute-done.4
  24.0 0.0 copy-start
  24.0 0.1 collective-permute-start.5
  24.2 0.5 %collective-permute-start.10 = (bf16[240,1024]{1,0:T(8,128)(2,1)S(1)}, bf16[240,1024]{1,0:T(8,128)(2,1)S(1)}, u32[]{:S(2)}, u32[]{:S(2)}) collective-permute-start(bf16[240,1024]{1,0:T(8,128)(2,1)S(1)} %constant_dynamic-update-slice_fusion.7.refs_1_), channel_id=1, source_target_pairs={{0,1},{1,0},{2,3},{3,2},{4,5},{5,4},{6,7},{7,6},{8,9},{9,8},{10,11... | collective-permute-start | bytes 1474568 | tf_op jit(solution)/shard_map/ppermute | solution.py:250
  24.7 0.1 collective-permute-start.12
  24.8 0.1 copy-done
  25.0 2.2 %shard_map.64 = (f32[1152,128]{1,0:T(8,128)S(1)}, f32[1152,128]{1,0:T(8,128)S(1)}, f32[1,3072]{1,0:T(1,128)S(1)}) custom-call(s32[2]{0:T(128)S(1)} %copy-done.2, s32[2]{0:T(128)S(1)} %copy-done.3, s32[2]{0:T(128)S(1)} %copy-done.4, bf16[48,3072]{1,0:T(8,128)(2,1)S(1)} %copy-done, bf16[384,1024]{1,0:T(8,128)(2,1)S(1)} %constant_dynamic-update-slice_fusion.2.refs_0_, ...), custom_call_target="tpu_custom_call" | custom-call | flops 452984832 | bytes 1572864 | tf_op jit(solution)/shard_map/pallas_call | solution.py:142
  27.2 0.3 collective-permute-done.12.refs_2_
  27.5 2.9 %shard_map.65 = bf16[48,3072]{1,0:T(8,128)(2,1)} custom-call(s32[2]{0:T(128)S(1)} %copy-done.2, s32[2]{0:T(128)S(1)} %copy-done.3, s32[2]{0:T(128)S(1)} %copy-done.4, bf16[48,3072]{1,0:T(8,128)(2,1)S(1)} %copy-done, bf16[384,1024]{1,0:T(8,128)(2,1)S(1)} %collective-permute-done.5.refs_0_, bf16[240,1024]{1,0:T(8,128)(2,1)S(1)} %collective-permute-done.10.refs_1_, ...), custom_call_target="tpu_custom_call" | custom-call | flops 452984832 | bytes 1572864 | tf_op jit(solution)/shard_map/pallas_call | solution.py:142
  (27 shorter events, 0.2 us)
Async XLA Ops:
  0.0 12.2 %copy-start.5 = (bf16[48,1024]{1,0:T(8,128)(2,1)S(1)}, bf16[48,1024]{1,0:T(8,128)(2,1)}, u32[]{:S(2)}) copy-start(bf16[48,1024]{1,0:T(8,128)(2,1)} %param.7) | copy-start | bytes 294916
  0.0 12.2 %collective-permute-start = (bf16[48,1024]{1,0:T(8,128)(2,1)}, bf16[48,1024]{1,0:T(8,128)(2,1)S(1)}, u32[]{:S(2)}, u32[]{:S(2)}) collective-permute-start(bf16[48,1024]{1,0:T(8,128)(2,1)} %param.7), channel_id=1, source_target_pairs={{0,8},{1,9},{2,10},{3,11},{4,12},{5,13},{6,14},{7,15},{8,0},{9,1},... | collective-permute-start | bytes 294920 | tf_op jit(solution)/shard_map/ppermute | solution.py:250
  4.0 8.2 %collective-permute-start.1 = (bf16[48,1024]{1,0:T(8,128)(2,1)}, bf16[48,1024]{1,0:T(8,128)(2,1)S(1)}, u32[]{:S(2)}, u32[]{:S(2)}) collective-permute-start(bf16[48,1024]{1,0:T(8,128)(2,1)} %param.7), channel_id=1, source_target_pairs={{0,12},{1,13},{2,14},{3,15},{4,8},{5,9},{6,10},{7,11},{8,4},{9,5},... | collective-permute-start | bytes 294920 | tf_op jit(solution)/shard_map/ppermute | solution.py:250
  5.4 9.5 %collective-permute-start.6 = (bf16[48,1024]{1,0:T(8,128)(2,1)}, bf16[48,1024]{1,0:T(8,128)(2,1)S(1)}, u32[]{:S(2)}, u32[]{:S(2)}) collective-permute-start(bf16[48,1024]{1,0:T(8,128)(2,1)} %param.7), channel_id=1, source_target_pairs={{0,18},{1,19},{2,16},{3,17},{4,22},{5,23},{6,20},{7,21},{8,26},{9,... | collective-permute-start | bytes 294920 | tf_op jit(solution)/shard_map/ppermute | solution.py:250
  7.8 7.6 %collective-permute-start.7 = (bf16[48,1024]{1,0:T(8,128)(2,1)}, bf16[48,1024]{1,0:T(8,128)(2,1)S(1)}, u32[]{:S(2)}, u32[]{:S(2)}) collective-permute-start(bf16[48,1024]{1,0:T(8,128)(2,1)} %param.7), channel_id=1, source_target_pairs={{0,2},{1,3},{2,0},{3,1},{4,6},{5,7},{6,4},{7,5},{8,10},{9,11},{10,... | collective-permute-start | bytes 294920 | tf_op jit(solution)/shard_map/ppermute | solution.py:250
  8.3 7.5 %collective-permute-start.8 = (bf16[48,1024]{1,0:T(8,128)(2,1)}, bf16[48,1024]{1,0:T(8,128)(2,1)S(1)}, u32[]{:S(2)}, u32[]{:S(2)}) collective-permute-start(bf16[48,1024]{1,0:T(8,128)(2,1)} %param.7), channel_id=1, source_target_pairs={{0,16},{1,17},{2,18},{3,19},{4,20},{5,21},{6,22},{7,23},{8,24},{9,... | collective-permute-start | bytes 294920 | tf_op jit(solution)/shard_map/ppermute | solution.py:250
  12.2 12.0 %collective-permute-start.9 = (bf16[48,1024]{1,0:T(8,128)(2,1)S(1)}, bf16[48,1024]{1,0:T(8,128)(2,1)S(1)}, u32[]{:S(2)}, u32[]{:S(2)}) collective-permute-start(bf16[48,1024]{1,0:T(8,128)(2,1)S(1)} %copy-done.5), channel_id=1, source_target_pairs={{0,4},{1,5},{2,6},{3,7},{4,0},{5,1},{6,2},{7,3},{8,12},{9,13},{10,... | collective-permute-start | bytes 294920 | tf_op jit(solution)/shard_map/ppermute | solution.py:250
  12.2 8.8 %collective-permute-start.2 = (bf16[96,1024]{1,0:T(8,128)(2,1)S(1)}, bf16[96,1024]{1,0:T(8,128)(2,1)S(1)}, u32[]{:S(2)}, u32[]{:S(2)}) collective-permute-start(bf16[96,1024]{1,0:T(8,128)(2,1)S(1)} %get-tuple-element.11), channel_id=1, source_target_pairs={{0,18},{1,19},{2,16},{3,17},{4,22},{5,23},{6,20},{7,21},{8,26},{9,... | collective-permute-start | bytes 589832 | tf_op jit(solution)/shard_map/ppermute | solution.py:250
  14.9 9.0 %collective-permute-start.3 = (bf16[96,1024]{1,0:T(8,128)(2,1)S(1)}, bf16[96,1024]{1,0:T(8,128)(2,1)S(1)}, u32[]{:S(2)}, u32[]{:S(2)}) collective-permute-start(bf16[96,1024]{1,0:T(8,128)(2,1)S(1)} %get-tuple-element.11), channel_id=1, source_target_pairs={{0,2},{1,3},{2,0},{3,1},{4,6},{5,7},{6,4},{7,5},{8,10},{9,11},{10,... | collective-permute-start | bytes 589832 | tf_op jit(solution)/shard_map/ppermute | solution.py:250
  15.4 8.6 %collective-permute-start.4 = (bf16[96,1024]{1,0:T(8,128)(2,1)S(1)}, bf16[96,1024]{1,0:T(8,128)(2,1)S(1)}, u32[]{:S(2)}, u32[]{:S(2)}) collective-permute-start(bf16[96,1024]{1,0:T(8,128)(2,1)S(1)} %get-tuple-element.11), channel_id=1, source_target_pairs={{0,16},{1,17},{2,18},{3,19},{4,20},{5,21},{6,22},{7,23},{8,24},{9,... | collective-permute-start | bytes 589832 | tf_op jit(solution)/shard_map/ppermute | solution.py:250
  15.8 8.9 %collective-permute-start.11 = (bf16[144,1024]{1,0:T(8,128)(2,1)S(1)}, bf16[144,1024]{1,0:T(8,128)(2,1)S(1)}, u32[]{:S(2)}, u32[]{:S(2)}) collective-permute-start(bf16[144,1024]{1,0:T(8,128)(2,1)S(1)} %pad_maximum_fusion), channel_id=1, source_target_pairs={{0,4},{1,5},{2,6},{3,7},{4,0},{5,1},{6,2},{7,3},{8,12},{9,13},{10,... | collective-permute-start | bytes 884744 | tf_op jit(solution)/shard_map/ppermute | solution.py:250
  21.0 3.8 %copy-start.1 = (f32[64,3072]{1,0:T(8,128)S(1)}, f32[64,3072]{1,0:T(8,128)}, u32[]{:S(2)}) copy-start(f32[64,3072]{1,0:T(8,128)} %refs_3_.1) | copy-start | bytes 2359300
  24.0 1.0 %copy-start = (bf16[48,3072]{1,0:T(8,128)(2,1)S(1)}, bf16[48,3072]{1,0:T(8,128)(2,1)}, u32[]{:S(2)}) copy-start(bf16[48,3072]{1,0:T(8,128)(2,1)} %q_ref.3) | copy-start | bytes 884740
  24.0 3.5 %collective-permute-start.5 = (bf16[384,1024]{1,0:T(8,128)(2,1)S(1)}, bf16[384,1024]{1,0:T(8,128)(2,1)S(1)}, u32[]{:S(2)}, u32[]{:S(2)}) collective-permute-start(bf16[384,1024]{1,0:T(8,128)(2,1)S(1)} %constant_dynamic-update-slice_fusion.2.refs_0_), channel_id=1, source_target_pairs={{0,1},{1,0},{2,3},{3,2},{4,5},{5,4},{6,7},{7,6},{8,9},{9,8},{10,11... | collective-permute-start | bytes 2359304 | tf_op jit(solution)/shard_map/ppermute | solution.py:250
  24.1 0.8 %copy-start.2 = (s32[2]{0:T(128)S(1)}, s32[2]{0:T(128)}, u32[]{:S(2)}) copy-start(s32[2]{0:T(128)} %clip_ref.3) | copy-start | bytes 28
  24.1 0.8 %copy-start.3 = (s32[2]{0:T(128)S(1)}, s32[2]{0:T(128)}, u32[]{:S(2)}) copy-start(s32[2]{0:T(128)} %valid_ref.3) | copy-start | bytes 28
  24.1 0.8 %copy-start.4 = (s32[2]{0:T(128)S(1)}, s32[2]{0:T(128)}, u32[]{:S(2)}) copy-start(s32[2]{0:T(128)} %step_ref.3) | copy-start | bytes 28
  24.2 3.0 %collective-permute-start.10 = (bf16[240,1024]{1,0:T(8,128)(2,1)S(1)}, bf16[240,1024]{1,0:T(8,128)(2,1)S(1)}, u32[]{:S(2)}, u32[]{:S(2)}) collective-permute-start(bf16[240,1024]{1,0:T(8,128)(2,1)S(1)} %constant_dynamic-update-slice_fusion.7.refs_1_), channel_id=1, source_target_pairs={{0,1},{1,0},{2,3},{3,2},{4,5},{5,4},{6,7},{7,6},{8,9},{9,8},{10,11... | collective-permute-start | bytes 1474568 | tf_op jit(solution)/shard_map/ppermute | solution.py:250
  24.7 2.7 %collective-permute-start.12 = (bf16[144,1024]{1,0:T(8,128)(2,1)S(1)}, bf16[144,1024]{1,0:T(8,128)(2,1)S(1)}, u32[]{:S(2)}, u32[]{:S(2)}) collective-permute-start(bf16[144,1024]{1,0:T(8,128)(2,1)S(1)} %collective-permute-done.11.refs_2_), channel_id=1, source_target_pairs={{0,1},{1,0},{2,3},{3,2},{4,5},{5,4},{6,7},{7,6},{8,9},{9,8},{10,11... | collective-permute-start | bytes 884744 | tf_op jit(solution)/shard_map/ppermute | solution.py:250

commit v7 on v6

--- a/solution.py
+++ b/solution.py
@@ -26,7 +26,11 @@
     lane = lax.broadcasted_iota(jnp.int32, (1, len(distances) * tokens), 1)
     bound = jnp.zeros_like(lane)
     for i, distance in enumerate(distances):
-        source = me ^ distance
+        base = me
+        if isinstance(distance, tuple):
+            core, distance = distance
+            base = me - me % 2 + core
+        source = base ^ distance
         group = source // n_seq
         limit = jnp.where(clip_ref[group] <= clip_ref[span_id], valid_ref[group], 0)
         usable = jnp.minimum(limit - (source % n_seq) * tokens, tokens)
@@ -36,7 +40,7 @@
 
 def attend_kernel(orders, groups, stage, n_seq, clip_ref, valid_ref, step_ref, q_ref, *refs):
     kv_refs, refs = refs[: len(orders)], refs[len(orders) :]
-    opens = stage == "first"
+    opens, closes = stage == "first", stage == "last"
     tokens = q_ref.shape[0]
     rows = RATIO * tokens
     scale = LOG2E / math.sqrt(HEAD_WIDTH)
@@ -49,10 +53,12 @@
         first = pl.multiple_of(step - step % GATE_ROWS, GATE_ROWS)
         fetch = pltpu.make_async_copy(table_ref.at[pl.ds(first, GATE_ROWS)], gate_ref, gate_sem)
         fetch.start()
-    else:
+    elif closes:
         top_in, part_in, gate_ref, out_ref, staged_ref, out_sem = refs
         position = lax.axis_index("seq") * tokens + lax.broadcasted_iota(jnp.int32, (tokens, 1), 0)
         live = (position < valid_ref[span_id]).astype(jnp.float32)
+    else:
+        top_in, part_in, top_out, part_out = refs
 
     def run(groups):
         def joined(group, c):
@@ -81,8 +87,9 @@
             span = slice(h * rows, (h + 1) * rows)
             sums = 0.0
             for g, group in enumerate(groups):
-                repeats = scores[h, g].shape[1] // HEAD_WIDTH
-                weights = jnp.exp2(scores[h, g] - jnp.concatenate([tops[h]] * repeats, axis=1))
+                size = scores[h, g].shape[1]
+                shift = jnp.concatenate([tops[h]] * pl.cdiv(size, HEAD_WIDTH), axis=1)[:, :size]
+                weights = jnp.exp2(scores[h, g] - shift)
                 value = joined(group, columns[KEY_VALUE_HEADS + h])
                 value = jnp.concatenate([value, jnp.ones_like(value)], axis=1)
                 sums = sums + jnp.dot(
@@ -94,7 +101,7 @@
                 total = total + factor
                 numerator = numerator + part_in[span, :] * factor
             result = numerator * (1.0 / total)
-            if opens:
+            if not closes:
                 top_out[span, :] = tops[h] + jnp.log2(total)
                 part_out[span, :] = result
                 continue
@@ -252,21 +259,25 @@
     plane = [n_seq + 2, 2, n_seq]
     away = jnp.concatenate([exchange(keyvals, d) for d in far[2:]], axis=0)
     column = exchange(keyvals, far[1])
-    received = [exchange(keyvals, d) for d in plane]
-    passed = exchange(jnp.concatenate(received, axis=0), far[1])
-    spread = [away] + [exchange(away, d) for d in plane]
-    away_order = [p ^ z for p in [0] + plane for z in far[2:]]
-    home_order = [0] + plane + [far[1]]
-    passed_order = [far[1] ^ p for p in plane]
+    home = jnp.concatenate([keyvals] + [exchange(keyvals, d) for d in plane], axis=0)
+    near = jnp.concatenate([column, exchange(home[tokens:], far[1])], axis=0)
+    away = jnp.concatenate([away] + [exchange(away, d) for d in plane], axis=0)
+    home_order = [0] + plane
+    near_order = [far[1] ^ p for p in home_order]
+    away_order = [p ^ z for p in home_order for z in far[2:]]
     twin = lambda order: [d ^ 1 for d in order]
     scalars = (clip_index, valid_count, noise_step)
-    n_away, n_home, n_passed = (len(o) * tokens for o in (away_order, home_order, passed_order))
-    pieces = [jnp.concatenate(spread, axis=0), jnp.concatenate([keyvals] + received + [column], axis=0), passed]
-    orders = [away_order, home_order, passed_order]
-    groups = [[(0, 0, n_away)], [(1, 0, n_home), (2, 0, n_passed)]]
-    twins = [exchange(x, 1) for x in pieces]
-    *state, gate = attend(scalars, queries, pieces, orders, groups, n_seq, "first", gate_table)
-    orders = [twin(o) for o in orders]
+    whole = lambda *parts: [(i, 0, part.shape[0]) for i, part in enumerate(parts)]
+    *state, gate = attend(
+        scalars, queries, [home], [home_order], [whole(home)], n_seq, "first", gate_table
+    )
+    near, _ = lax.optimization_barrier((near, state[0]))
+    both = exchange(jnp.concatenate([home, near], axis=0), 1)
+    twins = [exchange(away, 1), both]
+    orders, groups = [away_order, near_order], [whole(away), [(1, 0, near.shape[0])]]
+    state = attend(scalars, queries, [away, near], orders, groups, n_seq, "middle", *state)
+    orders = [twin(away_order), twin(home_order + near_order)]
+    groups = [whole(away), [(1, 0, both.shape[0])]]
     return attend(scalars, queries, twins, orders, groups, n_seq, "last", *state, gate)
 
 

time: 30.9 us -> 30.9 us (level)
  Pallas kernels: 5.12 us -> 6.14 us
  waiting for transfers between devices: 8.65 us -> 7.87 us
    pallas_call x2 -> x3, Pallas kernels: 5.12 us -> 6.14 us  [attend(): pl.pallas_call(functools.partial(attend_kernel, orders, groups, stage, n_...]
    ppermute x13 -> x12, waiting for transfers between devices: 8.65 us -> 7.87 us  [exchange(): return lax.ppermute(block, ('span', 'seq'), pairs)]
    ppermute x13 -> x12, starting transfers between devices: 15.2 us -> 15 us  [exchange(): return lax.ppermute(block, ('span', 'seq'), pairs)]
  transfers between devices with their start and end apart: 13 -> 12, of which waited for: 5 -> 6; matrix products, arithmetic and copies ran while one was open for 3% -> 4% of each run, Pallas kernels for 7% -> 11%
where the time goes in v7:
time: 30.9 us; the launch traced here: 30.4 us
  starting transfers between devices  15 us (49%)
  waiting for transfers between devices  7.87 us (25%)
  Pallas kernels  6.14 us (20%)
  local copies, waits for them, and re-layouts  1.09 us (4%)
    ppermute x12, starting transfers between devices, exchange(): return lax.ppermute(block, ('span', 'seq'), pairs)  15 us
    ppermute x12, waiting for transfers between devices, exchange(): return lax.ppermute(block, ('span', 'seq'), pairs)  7.87 us
    pallas_call x3, Pallas kernels, attend(): pl.pallas_call(functools.partial(attend_kernel, orders, groups, stage, n_...  6.14 us
    unnamed x19, local copies, waits for them, and re-layouts  1.04 us
  transfers between devices with their start and end apart: 12, of which 6 were waited for; matrix products, arithmetic and copies ran while one was open for 4% of the time, Pallas kernels for 11%

profile of v7, /device:TPU:0, one launch (start us, length us, event | category | flops | bytes accessed | tf_op | source)
XLA Modules:
  0.0 30.4 jit_solution(12070341847340920926)
XLA Ops:
  0.0 4.0 %collective-permute-start = (bf16[48,1024]{1,0:T(8,128)(2,1)}, bf16[48,1024]{1,0:T(8,128)(2,1)S(1)}, u32[]{:S(2)}, u32[]{:S(2)}) collective-permute-start(bf16[48,1024]{1,0:T(8,128)(2,1)} %param.7), channel_id=1, source_target_pairs={{0,8},{1,9},{2,10},{3,11},{4,12},{5,13},{6,14},{7,15},{8,0},{9,1},... | collective-permute-start | bytes 294920 | tf_op jit(solution)/shard_map/ppermute | solution.py:257
  4.0 1.3 %collective-permute-start.1 = (bf16[48,1024]{1,0:T(8,128)(2,1)}, bf16[48,1024]{1,0:T(8,128)(2,1)S(1)}, u32[]{:S(2)}, u32[]{:S(2)}) collective-permute-start(bf16[48,1024]{1,0:T(8,128)(2,1)} %param.7), channel_id=1, source_target_pairs={{0,12},{1,13},{2,14},{3,15},{4,8},{5,9},{6,10},{7,11},{8,4},{9,5},... | collective-permute-start | bytes 294920 | tf_op jit(solution)/shard_map/ppermute | solution.py:257
  5.4 2.4 %collective-permute-start.6 = (bf16[48,1024]{1,0:T(8,128)(2,1)}, bf16[48,1024]{1,0:T(8,128)(2,1)S(1)}, u32[]{:S(2)}, u32[]{:S(2)}) collective-permute-start(bf16[48,1024]{1,0:T(8,128)(2,1)} %param.7), channel_id=1, source_target_pairs={{0,18},{1,19},{2,16},{3,17},{4,22},{5,23},{6,20},{7,21},{8,26},{9,... | collective-permute-start | bytes 294920 | tf_op jit(solution)/shard_map/ppermute | solution.py:257
  7.8 0.5 %collective-permute-start.7 = (bf16[48,1024]{1,0:T(8,128)(2,1)}, bf16[48,1024]{1,0:T(8,128)(2,1)S(1)}, u32[]{:S(2)}, u32[]{:S(2)}) collective-permute-start(bf16[48,1024]{1,0:T(8,128)(2,1)} %param.7), channel_id=1, source_target_pairs={{0,2},{1,3},{2,0},{3,1},{4,6},{5,7},{6,4},{7,5},{8,10},{9,11},{10,... | collective-permute-start | bytes 294920 | tf_op jit(solution)/shard_map/ppermute | solution.py:257
  8.3 0.5 %collective-permute-start.8 = (bf16[48,1024]{1,0:T(8,128)(2,1)}, bf16[48,1024]{1,0:T(8,128)(2,1)S(1)}, u32[]{:S(2)}, u32[]{:S(2)}) collective-permute-start(bf16[48,1024]{1,0:T(8,128)(2,1)} %param.7), channel_id=1, source_target_pairs={{0,16},{1,17},{2,18},{3,19},{4,20},{5,21},{6,22},{7,23},{8,24},{9,... | collective-permute-start | bytes 294920 | tf_op jit(solution)/shard_map/ppermute | solution.py:257
  8.9 0.9 %constant_dynamic-update-slice_fusion.11 = bf16[384,1024]{1,0:T(8,128)(2,1)S(1)} fusion(bf16[48,1024]{1,0:T(8,128)(2,1)} %param.7), kind=kLoop, calls=%fused_computation.14 | loop fusion | bytes 196608
  9.8 2.3 %collective-permute-done = bf16[48,1024]{1,0:T(8,128)(2,1)S(1)} collective-permute-done((bf16[48,1024]{1,0:T(8,128)(2,1)}, bf16[48,1024]{1,0:T(8,128)(2,1)S(1)}, u32[]{:S(2)}, u32[]{:S(2)}) %collective-permute-start) | collective-permute-done | bytes 98336 | tf_op jit(solution)/shard_map/ppermute | solution.py:257
  12.2 0.0 collective-permute-start.9
  12.2 0.0 copy-start.1
  12.2 2.7 %collective-permute-start.2 = (bf16[96,1024]{1,0:T(8,128)(2,1)S(1)}, bf16[96,1024]{1,0:T(8,128)(2,1)S(1)}, u32[]{:S(2)}, u32[]{:S(2)}) collective-permute-start(bf16[96,1024]{1,0:T(8,128)(2,1)S(1)} %get-tuple-element.17), channel_id=1, source_target_pairs={{0,18},{1,19},{2,16},{3,17},{4,22},{5,23},{6,20},{7,21},{8,26},{9,... | collective-permute-start | bytes 589832 | tf_op jit(solution)/shard_map/ppermute | solution.py:257
  14.9 0.5 %collective-permute-start.3 = (bf16[96,1024]{1,0:T(8,128)(2,1)S(1)}, bf16[96,1024]{1,0:T(8,128)(2,1)S(1)}, u32[]{:S(2)}, u32[]{:S(2)}) collective-permute-start(bf16[96,1024]{1,0:T(8,128)(2,1)S(1)} %get-tuple-element.17), channel_id=1, source_target_pairs={{0,2},{1,3},{2,0},{3,1},{4,6},{5,7},{6,4},{7,5},{8,10},{9,11},{10,... | collective-permute-start | bytes 589832 | tf_op jit(solution)/shard_map/ppermute | solution.py:257
  15.4 0.4 %collective-permute-start.4 = (bf16[96,1024]{1,0:T(8,128)(2,1)S(1)}, bf16[96,1024]{1,0:T(8,128)(2,1)S(1)}, u32[]{:S(2)}, u32[]{:S(2)}) collective-permute-start(bf16[96,1024]{1,0:T(8,128)(2,1)S(1)} %get-tuple-element.17), channel_id=1, source_target_pairs={{0,16},{1,17},{2,18},{3,19},{4,20},{5,21},{6,22},{7,23},{8,24},{9,... | collective-permute-start | bytes 589832 | tf_op jit(solution)/shard_map/ppermute | solution.py:257
  15.9 0.0 copy-start.3
  15.9 2.1 %collective-permute-start.10 = (bf16[144,1024]{1,0:T(8,128)(2,1)S(1)}, bf16[144,1024]{1,0:T(8,128)(2,1)S(1)}, u32[]{:S(2)}, u32[]{:S(2)}) collective-permute-start(bf16[144,1024]{1,0:T(8,128)(2,1)S(1)} %pad_maximum_fusion.2), channel_id=1, source_target_pairs={{0,4},{1,5},{2,6},{3,7},{4,0},{5,1},{6,2},{7,3},{8,12},{9,13},{10,... | collective-permute-start | bytes 884744 | tf_op jit(solution)/shard_map/ppermute | solution.py:257
  18.0 1.4 %shard_map.64 = (f32[1152,128]{1,0:T(8,128)S(1)}, f32[1152,128]{1,0:T(8,128)S(1)}, f32[1,3072]{1,0:T(1,128)S(1)}) custom-call(s32[2]{0:T(128)S(1)} %copy-done.2, s32[2]{0:T(128)S(1)} %copy-done.3, s32[2]{0:T(128)S(1)} %copy-done.4, bf16[48,3072]{1,0:T(8,128)(2,1)S(1)} %copy-done, bf16[192,1024]{1,0:T(8,128)(2,1)S(1)} %pad_maximum_fusion.1.refs_0_, ...), custom_call_target="tpu_custom_call" | custom-call | flops 113246208 | bytes 393216 | tf_op jit(solution)/shard_map/pallas_call | solution.py:149
  19.5 1.6 %collective-permute-done.2 = bf16[96,1024]{1,0:T(8,128)(2,1)S(1)} collective-permute-done((bf16[96,1024]{1,0:T(8,128)(2,1)S(1)}, bf16[96,1024]{1,0:T(8,128)(2,1)S(1)}, u32[]{:S(2)}, u32[]{:S(2)}) %collective-permute-start.2) | collective-permute-done | bytes 196640 | tf_op jit(solution)/shard_map/ppermute | solution.py:257
  21.1 2.8 %collective-permute-done.3 = bf16[96,1024]{1,0:T(8,128)(2,1)S(1)} collective-permute-done((bf16[96,1024]{1,0:T(8,128)(2,1)S(1)}, bf16[96,1024]{1,0:T(8,128)(2,1)S(1)}, u32[]{:S(2)}, u32[]{:S(2)}) %collective-permute-start.3) | collective-permute-done | bytes 196640 | tf_op jit(solution)/shard_map/ppermute | solution.py:257
  23.9 0.1 collective-permute-done.4
  24.0 0.1 collective-permute-start.5
  24.1 0.2 collective-permute-done.10
  24.3 0.4 %collective-permute-start.11 = (bf16[384,1024]{1,0:T(8,128)(2,1)S(1)}, bf16[384,1024]{1,0:T(8,128)(2,1)S(1)}, u32[]{:S(2)}, u32[]{:S(2)}) collective-permute-start(bf16[384,1024]{1,0:T(8,128)(2,1)S(1)} %constant_dynamic-update-slice_fusion.7), channel_id=1, source_target_pairs={{0,1},{1,0},{2,3},{3,2},{4,5},{5,4},{6,7},{7,6},{8,9},{9,8},{10,11... | collective-permute-start | bytes 2359304 | tf_op jit(solution)/shard_map/ppermute | solution.py:257
  24.7 1.9 %shard_map.65 = (f32[1152,128]{1,0:T(8,128)S(1)}, f32[1152,128]{1,0:T(8,128)S(1)}) custom-call(s32[2]{0:T(128)S(1)} %copy-done.2, s32[2]{0:T(128)S(1)} %copy-done.3, s32[2]{0:T(128)S(1)} %copy-done.4, bf16[48,3072]{1,0:T(8,128)(2,1)S(1)} %copy-done, bf16[384,1024]{1,0:T(8,128)(2,1)S(1)} %constant_dynamic-update-slice_fusion.2.refs_0_, ...), custom_call_target="tpu_custom_call" | custom-call | flops 339738624 | bytes 1179648 | tf_op jit(solution)/shard_map/pallas_call | solution.py:149
  26.6 0.9 %collective-permute-done.11.refs_1_ = bf16[384,1024]{1,0:T(8,128)(2,1)S(1)} collective-permute-done((bf16[384,1024]{1,0:T(8,128)(2,1)S(1)}, bf16[384,1024]{1,0:T(8,128)(2,1)S(1)}, u32[]{:S(2)}, u32[]{:S(2)}) %collective-permute-start.11) | collective-permute-done | bytes 786464 | tf_op jit(solution)/shard_map/ppermute | solution.py:257
  27.5 2.9 %shard_map.66 = bf16[48,3072]{1,0:T(8,128)(2,1)} custom-call(s32[2]{0:T(128)S(1)} %copy-done.2, s32[2]{0:T(128)S(1)} %copy-done.3, s32[2]{0:T(128)S(1)} %copy-done.4, bf16[48,3072]{1,0:T(8,128)(2,1)S(1)} %copy-done, bf16[384,1024]{1,0:T(8,128)(2,1)S(1)} %collective-permute-done.5.refs_0_, bf16[384,1024]{1,0:T(8,128)(2,1)S(1)} %collective-permute-done.11.refs_1_, ...), custom_call_target="tpu_custom_call" | custom-call | flops 452984832 | bytes 1572864 | tf_op jit(solution)/shard_map/pallas_call | solution.py:149
  (28 shorter events, 0.2 us)
Async XLA Ops:
  0.0 12.2 %copy-start.5 = (bf16[48,1024]{1,0:T(8,128)(2,1)S(1)}, bf16[48,1024]{1,0:T(8,128)(2,1)}, u32[]{:S(2)}) copy-start(bf16[48,1024]{1,0:T(8,128)(2,1)} %param.7) | copy-start | bytes 294916
  0.0 12.2 %collective-permute-start = (bf16[48,1024]{1,0:T(8,128)(2,1)}, bf16[48,1024]{1,0:T(8,128)(2,1)S(1)}, u32[]{:S(2)}, u32[]{:S(2)}) collective-permute-start(bf16[48,1024]{1,0:T(8,128)(2,1)} %param.7), channel_id=1, source_target_pairs={{0,8},{1,9},{2,10},{3,11},{4,12},{5,13},{6,14},{7,15},{8,0},{9,1},... | collective-permute-start | bytes 294920 | tf_op jit(solution)/shard_map/ppermute | solution.py:257
  4.0 8.2 %collective-permute-start.1 = (bf16[48,1024]{1,0:T(8,128)(2,1)}, bf16[48,1024]{1,0:T(8,128)(2,1)S(1)}, u32[]{:S(2)}, u32[]{:S(2)}) collective-permute-start(bf16[48,1024]{1,0:T(8,128)(2,1)} %param.7), channel_id=1, source_target_pairs={{0,12},{1,13},{2,14},{3,15},{4,8},{5,9},{6,10},{7,11},{8,4},{9,5},... | collective-permute-start | bytes 294920 | tf_op jit(solution)/shard_map/ppermute | solution.py:257
  5.4 9.5 %collective-permute-start.6 = (bf16[48,1024]{1,0:T(8,128)(2,1)}, bf16[48,1024]{1,0:T(8,128)(2,1)S(1)}, u32[]{:S(2)}, u32[]{:S(2)}) collective-permute-start(bf16[48,1024]{1,0:T(8,128)(2,1)} %param.7), channel_id=1, source_target_pairs={{0,18},{1,19},{2,16},{3,17},{4,22},{5,23},{6,20},{7,21},{8,26},{9,... | collective-permute-start | bytes 294920 | tf_op jit(solution)/shard_map/ppermute | solution.py:257
  7.8 7.6 %collective-permute-start.7 = (bf16[48,1024]{1,0:T(8,128)(2,1)}, bf16[48,1024]{1,0:T(8,128)(2,1)S(1)}, u32[]{:S(2)}, u32[]{:S(2)}) collective-permute-start(bf16[48,1024]{1,0:T(8,128)(2,1)} %param.7), channel_id=1, source_target_pairs={{0,2},{1,3},{2,0},{3,1},{4,6},{5,7},{6,4},{7,5},{8,10},{9,11},{10,... | collective-permute-start | bytes 294920 | tf_op jit(solution)/shard_map/ppermute | solution.py:257
  8.3 7.5 %collective-permute-start.8 = (bf16[48,1024]{1,0:T(8,128)(2,1)}, bf16[48,1024]{1,0:T(8,128)(2,1)S(1)}, u32[]{:S(2)}, u32[]{:S(2)}) collective-permute-start(bf16[48,1024]{1,0:T(8,128)(2,1)} %param.7), channel_id=1, source_target_pairs={{0,16},{1,17},{2,18},{3,19},{4,20},{5,21},{6,22},{7,23},{8,24},{9,... | collective-permute-start | bytes 294920 | tf_op jit(solution)/shard_map/ppermute | solution.py:257
  12.2 11.9 %collective-permute-start.9 = (bf16[48,1024]{1,0:T(8,128)(2,1)S(1)}, bf16[48,1024]{1,0:T(8,128)(2,1)S(1)}, u32[]{:S(2)}, u32[]{:S(2)}) collective-permute-start(bf16[48,1024]{1,0:T(8,128)(2,1)S(1)} %copy-done.5), channel_id=1, source_target_pairs={{0,4},{1,5},{2,6},{3,7},{4,0},{5,1},{6,2},{7,3},{8,12},{9,13},{10,... | collective-permute-start | bytes 294920 | tf_op jit(solution)/shard_map/ppermute | solution.py:257
  12.2 5.8 %copy-start.1 = (f32[64,3072]{1,0:T(8,128)S(1)}, f32[64,3072]{1,0:T(8,128)}, u32[]{:S(2)}) copy-start(f32[64,3072]{1,0:T(8,128)} %refs_1_.1) | copy-start | bytes 2359300
  12.2 8.8 %collective-permute-start.2 = (bf16[96,1024]{1,0:T(8,128)(2,1)S(1)}, bf16[96,1024]{1,0:T(8,128)(2,1)S(1)}, u32[]{:S(2)}, u32[]{:S(2)}) collective-permute-start(bf16[96,1024]{1,0:T(8,128)(2,1)S(1)} %get-tuple-element.17), channel_id=1, source_target_pairs={{0,18},{1,19},{2,16},{3,17},{4,22},{5,23},{6,20},{7,21},{8,26},{9,... | collective-permute-start | bytes 589832 | tf_op jit(solution)/shard_map/ppermute | solution.py:257
  14.9 9.0 %collective-permute-start.3 = (bf16[96,1024]{1,0:T(8,128)(2,1)S(1)}, bf16[96,1024]{1,0:T(8,128)(2,1)S(1)}, u32[]{:S(2)}, u32[]{:S(2)}) collective-permute-start(bf16[96,1024]{1,0:T(8,128)(2,1)S(1)} %get-tuple-element.17), channel_id=1, source_target_pairs={{0,2},{1,3},{2,0},{3,1},{4,6},{5,7},{6,4},{7,5},{8,10},{9,11},{10,... | collective-permute-start | bytes 589832 | tf_op jit(solution)/shard_map/ppermute | solution.py:257
  15.4 8.6 %collective-permute-start.4 = (bf16[96,1024]{1,0:T(8,128)(2,1)S(1)}, bf16[96,1024]{1,0:T(8,128)(2,1)S(1)}, u32[]{:S(2)}, u32[]{:S(2)}) collective-permute-start(bf16[96,1024]{1,0:T(8,128)(2,1)S(1)} %get-tuple-element.17), channel_id=1, source_target_pairs={{0,16},{1,17},{2,18},{3,19},{4,20},{5,21},{6,22},{7,23},{8,24},{9,... | collective-permute-start | bytes 589832 | tf_op jit(solution)/shard_map/ppermute | solution.py:257
  15.8 2.2 %copy-start = (bf16[48,3072]{1,0:T(8,128)(2,1)S(1)}, bf16[48,3072]{1,0:T(8,128)(2,1)}, u32[]{:S(2)}) copy-start(bf16[48,3072]{1,0:T(8,128)(2,1)} %q_ref.5) | copy-start | bytes 884740
  15.8 2.2 %copy-start.2 = (s32[2]{0:T(128)S(1)}, s32[2]{0:T(128)}, u32[]{:S(2)}) copy-start(s32[2]{0:T(128)} %clip_ref.5) | copy-start | bytes 28
  15.9 2.2 %copy-start.3 = (s32[2]{0:T(128)S(1)}, s32[2]{0:T(128)}, u32[]{:S(2)}) copy-start(s32[2]{0:T(128)} %valid_ref.5) | copy-start | bytes 28
  15.9 2.2 %copy-start.4 = (s32[2]{0:T(128)S(1)}, s32[2]{0:T(128)}, u32[]{:S(2)}) copy-start(s32[2]{0:T(128)} %step_ref.5) | copy-start | bytes 28
  15.9 8.4 %collective-permute-start.10 = (bf16[144,1024]{1,0:T(8,128)(2,1)S(1)}, bf16[144,1024]{1,0:T(8,128)(2,1)S(1)}, u32[]{:S(2)}, u32[]{:S(2)}) collective-permute-start(bf16[144,1024]{1,0:T(8,128)(2,1)S(1)} %pad_maximum_fusion.2), channel_id=1, source_target_pairs={{0,4},{1,5},{2,6},{3,7},{4,0},{5,1},{6,2},{7,3},{8,12},{9,13},{10,... | collective-permute-start | bytes 884744 | tf_op jit(solution)/shard_map/ppermute | solution.py:257
  24.0 2.6 %collective-permute-start.5 = (bf16[384,1024]{1,0:T(8,128)(2,1)S(1)}, bf16[384,1024]{1,0:T(8,128)(2,1)S(1)}, u32[]{:S(2)}, u32[]{:S(2)}) collective-permute-start(bf16[384,1024]{1,0:T(8,128)(2,1)S(1)} %constant_dynamic-update-slice_fusion.2.refs_0_), channel_id=1, source_target_pairs={{0,1},{1,0},{2,3},{3,2},{4,5},{5,4},{6,7},{7,6},{8,9},{9,8},{10,11... | collective-permute-start | bytes 2359304 | tf_op jit(solution)/shard_map/ppermute | solution.py:257
  24.3 3.1 %collective-permute-start.11 = (bf16[384,1024]{1,0:T(8,128)(2,1)S(1)}, bf16[384,1024]{1,0:T(8,128)(2,1)S(1)}, u32[]{:S(2)}, u32[]{:S(2)}) collective-permute-start(bf16[384,1024]{1,0:T(8,128)(2,1)S(1)} %constant_dynamic-update-slice_fusion.7), channel_id=1, source_target_pairs={{0,1},{1,0},{2,3},{3,2},{4,5},{5,4},{6,7},{7,6},{8,9},{9,8},{10,11... | collective-permute-start | bytes 2359304 | tf_op jit(solution)/shard_map/ppermute | solution.py:257

commit v8 on v7

--- a/solution.py
+++ b/solution.py
@@ -109,7 +109,9 @@
                 c = columns[h * RATIO + r]
                 part = result[r * tokens : (r + 1) * tokens]
                 staged_ref[:, c] = (part * gate_ref[:, c] * live).astype(out_ref.dtype)
-            group = slice(h * RATIO * HEAD_WIDTH, (h + 1) * RATIO * HEAD_WIDTH)
+            if h % 2 == 0:
+                continue
+            group = slice((h - 1) * RATIO * HEAD_WIDTH, (h + 1) * RATIO * HEAD_WIDTH)
             writes.append(
                 pltpu.make_async_copy(staged_ref.at[:, group], out_ref.at[:, group], out_sem.at[h])
             )

time: 30.9 us -> 30.9 us (level)
  no operation moved by 1% of the time
where the time goes in v8:
time: 30.9 us; the launch traced here: 30.4 us
  starting transfers between devices  15 us (49%)
  waiting for transfers between devices  7.87 us (25%)
  Pallas kernels  6.14 us (20%)
  local copies, waits for them, and re-layouts  1.09 us (4%)
    ppermute x12, starting transfers between devices, exchange(): return lax.ppermute(block, ('span', 'seq'), pairs)  15 us
    ppermute x12, waiting for transfers between devices, exchange(): return lax.ppermute(block, ('span', 'seq'), pairs)  7.87 us
    pallas_call x3, Pallas kernels, attend(): pl.pallas_call(functools.partial(attend_kernel, orders, groups, stage, n_...  6.14 us
    unnamed x19, local copies, waits for them, and re-layouts  1.04 us
  transfers between devices with their start and end apart: 12, of which 6 were waited for; matrix products, arithmetic and copies ran while one was open for 4% of the time, Pallas kernels for 11%

profile of v8, /device:TPU:0, one launch (start us, length us, event | category | flops | bytes accessed | tf_op | source)
XLA Modules:
  0.0 30.4 jit_solution(2370628251876970112)
XLA Ops:
  0.0 4.0 %collective-permute-start = (bf16[48,1024]{1,0:T(8,128)(2,1)}, bf16[48,1024]{1,0:T(8,128)(2,1)S(1)}, u32[]{:S(2)}, u32[]{:S(2)}) collective-permute-start(bf16[48,1024]{1,0:T(8,128)(2,1)} %param.7), channel_id=1, source_target_pairs={{0,8},{1,9},{2,10},{3,11},{4,12},{5,13},{6,14},{7,15},{8,0},{9,1},... | collective-permute-start | bytes 294920 | tf_op jit(solution)/shard_map/ppermute | solution.py:259
  4.0 1.3 %collective-permute-start.1 = (bf16[48,1024]{1,0:T(8,128)(2,1)}, bf16[48,1024]{1,0:T(8,128)(2,1)S(1)}, u32[]{:S(2)}, u32[]{:S(2)}) collective-permute-start(bf16[48,1024]{1,0:T(8,128)(2,1)} %param.7), channel_id=1, source_target_pairs={{0,12},{1,13},{2,14},{3,15},{4,8},{5,9},{6,10},{7,11},{8,4},{9,5},... | collective-permute-start | bytes 294920 | tf_op jit(solution)/shard_map/ppermute | solution.py:259
  5.4 2.4 %collective-permute-start.6 = (bf16[48,1024]{1,0:T(8,128)(2,1)}, bf16[48,1024]{1,0:T(8,128)(2,1)S(1)}, u32[]{:S(2)}, u32[]{:S(2)}) collective-permute-start(bf16[48,1024]{1,0:T(8,128)(2,1)} %param.7), channel_id=1, source_target_pairs={{0,18},{1,19},{2,16},{3,17},{4,22},{5,23},{6,20},{7,21},{8,26},{9,... | collective-permute-start | bytes 294920 | tf_op jit(solution)/shard_map/ppermute | solution.py:259
  7.8 0.5 %collective-permute-start.7 = (bf16[48,1024]{1,0:T(8,128)(2,1)}, bf16[48,1024]{1,0:T(8,128)(2,1)S(1)}, u32[]{:S(2)}, u32[]{:S(2)}) collective-permute-start(bf16[48,1024]{1,0:T(8,128)(2,1)} %param.7), channel_id=1, source_target_pairs={{0,2},{1,3},{2,0},{3,1},{4,6},{5,7},{6,4},{7,5},{8,10},{9,11},{10,... | collective-permute-start | bytes 294920 | tf_op jit(solution)/shard_map/ppermute | solution.py:259
  8.3 0.5 %collective-permute-start.8 = (bf16[48,1024]{1,0:T(8,128)(2,1)}, bf16[48,1024]{1,0:T(8,128)(2,1)S(1)}, u32[]{:S(2)}, u32[]{:S(2)}) collective-permute-start(bf16[48,1024]{1,0:T(8,128)(2,1)} %param.7), channel_id=1, source_target_pairs={{0,16},{1,17},{2,18},{3,19},{4,20},{5,21},{6,22},{7,23},{8,24},{9,... | collective-permute-start | bytes 294920 | tf_op jit(solution)/shard_map/ppermute | solution.py:259
  8.9 0.9 %constant_dynamic-update-slice_fusion.11 = bf16[384,1024]{1,0:T(8,128)(2,1)S(1)} fusion(bf16[48,1024]{1,0:T(8,128)(2,1)} %param.7), kind=kLoop, calls=%fused_computation.14 | loop fusion | bytes 196608
  9.8 2.3 %collective-permute-done = bf16[48,1024]{1,0:T(8,128)(2,1)S(1)} collective-permute-done((bf16[48,1024]{1,0:T(8,128)(2,1)}, bf16[48,1024]{1,0:T(8,128)(2,1)S(1)}, u32[]{:S(2)}, u32[]{:S(2)}) %collective-permute-start) | collective-permute-done | bytes 98336 | tf_op jit(solution)/shard_map/ppermute | solution.py:259
  12.2 0.0 collective-permute-start.9
  12.2 0.0 copy-start.1
  12.2 2.7 %collective-permute-start.2 = (bf16[96,1024]{1,0:T(8,128)(2,1)S(1)}, bf16[96,1024]{1,0:T(8,128)(2,1)S(1)}, u32[]{:S(2)}, u32[]{:S(2)}) collective-permute-start(bf16[96,1024]{1,0:T(8,128)(2,1)S(1)} %get-tuple-element.17), channel_id=1, source_target_pairs={{0,18},{1,19},{2,16},{3,17},{4,22},{5,23},{6,20},{7,21},{8,26},{9,... | collective-permute-start | bytes 589832 | tf_op jit(solution)/shard_map/ppermute | solution.py:259
  14.9 0.5 %collective-permute-start.3 = (bf16[96,1024]{1,0:T(8,128)(2,1)S(1)}, bf16[96,1024]{1,0:T(8,128)(2,1)S(1)}, u32[]{:S(2)}, u32[]{:S(2)}) collective-permute-start(bf16[96,1024]{1,0:T(8,128)(2,1)S(1)} %get-tuple-element.17), channel_id=1, source_target_pairs={{0,2},{1,3},{2,0},{3,1},{4,6},{5,7},{6,4},{7,5},{8,10},{9,11},{10,... | collective-permute-start | bytes 589832 | tf_op jit(solution)/shard_map/ppermute | solution.py:259
  15.4 0.4 %collective-permute-start.4 = (bf16[96,1024]{1,0:T(8,128)(2,1)S(1)}, bf16[96,1024]{1,0:T(8,128)(2,1)S(1)}, u32[]{:S(2)}, u32[]{:S(2)}) collective-permute-start(bf16[96,1024]{1,0:T(8,128)(2,1)S(1)} %get-tuple-element.17), channel_id=1, source_target_pairs={{0,16},{1,17},{2,18},{3,19},{4,20},{5,21},{6,22},{7,23},{8,24},{9,... | collective-permute-start | bytes 589832 | tf_op jit(solution)/shard_map/ppermute | solution.py:259
  15.9 0.0 copy-start.3
  15.9 2.1 %collective-permute-start.10 = (bf16[144,1024]{1,0:T(8,128)(2,1)S(1)}, bf16[144,1024]{1,0:T(8,128)(2,1)S(1)}, u32[]{:S(2)}, u32[]{:S(2)}) collective-permute-start(bf16[144,1024]{1,0:T(8,128)(2,1)S(1)} %pad_maximum_fusion.2), channel_id=1, source_target_pairs={{0,4},{1,5},{2,6},{3,7},{4,0},{5,1},{6,2},{7,3},{8,12},{9,13},{10,... | collective-permute-start | bytes 884744 | tf_op jit(solution)/shard_map/ppermute | solution.py:259
  18.0 1.4 %shard_map.64 = (f32[1152,128]{1,0:T(8,128)S(1)}, f32[1152,128]{1,0:T(8,128)S(1)}, f32[1,3072]{1,0:T(1,128)S(1)}) custom-call(s32[2]{0:T(128)S(1)} %copy-done.2, s32[2]{0:T(128)S(1)} %copy-done.3, s32[2]{0:T(128)S(1)} %copy-done.4, bf16[48,3072]{1,0:T(8,128)(2,1)S(1)} %copy-done, bf16[192,1024]{1,0:T(8,128)(2,1)S(1)} %pad_maximum_fusion.1.refs_0_, ...), custom_call_target="tpu_custom_call" | custom-call | flops 113246208 | bytes 393216 | tf_op jit(solution)/shard_map/pallas_call | solution.py:151
  19.5 1.6 %collective-permute-done.2 = bf16[96,1024]{1,0:T(8,128)(2,1)S(1)} collective-permute-done((bf16[96,1024]{1,0:T(8,128)(2,1)S(1)}, bf16[96,1024]{1,0:T(8,128)(2,1)S(1)}, u32[]{:S(2)}, u32[]{:S(2)}) %collective-permute-start.2) | collective-permute-done | bytes 196640 | tf_op jit(solution)/shard_map/ppermute | solution.py:259
  21.1 2.8 %collective-permute-done.3 = bf16[96,1024]{1,0:T(8,128)(2,1)S(1)} collective-permute-done((bf16[96,1024]{1,0:T(8,128)(2,1)S(1)}, bf16[96,1024]{1,0:T(8,128)(2,1)S(1)}, u32[]{:S(2)}, u32[]{:S(2)}) %collective-permute-start.3) | collective-permute-done | bytes 196640 | tf_op jit(solution)/shard_map/ppermute | solution.py:259
  23.9 0.1 collective-permute-done.4
  24.0 0.1 collective-permute-start.5
  24.1 0.2 collective-permute-done.10
  24.3 0.4 %collective-permute-start.11 = (bf16[384,1024]{1,0:T(8,128)(2,1)S(1)}, bf16[384,1024]{1,0:T(8,128)(2,1)S(1)}, u32[]{:S(2)}, u32[]{:S(2)}) collective-permute-start(bf16[384,1024]{1,0:T(8,128)(2,1)S(1)} %constant_dynamic-update-slice_fusion.7), channel_id=1, source_target_pairs={{0,1},{1,0},{2,3},{3,2},{4,5},{5,4},{6,7},{7,6},{8,9},{9,8},{10,11... | collective-permute-start | bytes 2359304 | tf_op jit(solution)/shard_map/ppermute | solution.py:259
  24.7 1.9 %shard_map.65 = (f32[1152,128]{1,0:T(8,128)S(1)}, f32[1152,128]{1,0:T(8,128)S(1)}) custom-call(s32[2]{0:T(128)S(1)} %copy-done.2, s32[2]{0:T(128)S(1)} %copy-done.3, s32[2]{0:T(128)S(1)} %copy-done.4, bf16[48,3072]{1,0:T(8,128)(2,1)S(1)} %copy-done, bf16[384,1024]{1,0:T(8,128)(2,1)S(1)} %constant_dynamic-update-slice_fusion.2.refs_0_, ...), custom_call_target="tpu_custom_call" | custom-call | flops 339738624 | bytes 1179648 | tf_op jit(solution)/shard_map/pallas_call | solution.py:151
  26.6 0.9 %collective-permute-done.11.refs_1_ = bf16[384,1024]{1,0:T(8,128)(2,1)S(1)} collective-permute-done((bf16[384,1024]{1,0:T(8,128)(2,1)S(1)}, bf16[384,1024]{1,0:T(8,128)(2,1)S(1)}, u32[]{:S(2)}, u32[]{:S(2)}) %collective-permute-start.11) | collective-permute-done | bytes 786464 | tf_op jit(solution)/shard_map/ppermute | solution.py:259
  27.5 2.9 %shard_map.66 = bf16[48,3072]{1,0:T(8,128)(2,1)} custom-call(s32[2]{0:T(128)S(1)} %copy-done.2, s32[2]{0:T(128)S(1)} %copy-done.3, s32[2]{0:T(128)S(1)} %copy-done.4, bf16[48,3072]{1,0:T(8,128)(2,1)S(1)} %copy-done, bf16[384,1024]{1,0:T(8,128)(2,1)S(1)} %collective-permute-done.5.refs_0_, bf16[384,1024]{1,0:T(8,128)(2,1)S(1)} %collective-permute-done.11.refs_1_, ...), custom_call_target="tpu_custom_call" | custom-call | flops 452984832 | bytes 1572864 | tf_op jit(solution)/shard_map/pallas_call | solution.py:151
  (28 shorter events, 0.2 us)
Async XLA Ops:
  0.0 12.2 %copy-start.5 = (bf16[48,1024]{1,0:T(8,128)(2,1)S(1)}, bf16[48,1024]{1,0:T(8,128)(2,1)}, u32[]{:S(2)}) copy-start(bf16[48,1024]{1,0:T(8,128)(2,1)} %param.7) | copy-start | bytes 294916
  0.0 12.2 %collective-permute-start = (bf16[48,1024]{1,0:T(8,128)(2,1)}, bf16[48,1024]{1,0:T(8,128)(2,1)S(1)}, u32[]{:S(2)}, u32[]{:S(2)}) collective-permute-start(bf16[48,1024]{1,0:T(8,128)(2,1)} %param.7), channel_id=1, source_target_pairs={{0,8},{1,9},{2,10},{3,11},{4,12},{5,13},{6,14},{7,15},{8,0},{9,1},... | collective-permute-start | bytes 294920 | tf_op jit(solution)/shard_map/ppermute | solution.py:259
  4.0 8.2 %collective-permute-start.1 = (bf16[48,1024]{1,0:T(8,128)(2,1)}, bf16[48,1024]{1,0:T(8,128)(2,1)S(1)}, u32[]{:S(2)}, u32[]{:S(2)}) collective-permute-start(bf16[48,1024]{1,0:T(8,128)(2,1)} %param.7), channel_id=1, source_target_pairs={{0,12},{1,13},{2,14},{3,15},{4,8},{5,9},{6,10},{7,11},{8,4},{9,5},... | collective-permute-start | bytes 294920 | tf_op jit(solution)/shard_map/ppermute | solution.py:259
  5.4 9.5 %collective-permute-start.6 = (bf16[48,1024]{1,0:T(8,128)(2,1)}, bf16[48,1024]{1,0:T(8,128)(2,1)S(1)}, u32[]{:S(2)}, u32[]{:S(2)}) collective-permute-start(bf16[48,1024]{1,0:T(8,128)(2,1)} %param.7), channel_id=1, source_target_pairs={{0,18},{1,19},{2,16},{3,17},{4,22},{5,23},{6,20},{7,21},{8,26},{9,... | collective-permute-start | bytes 294920 | tf_op jit(solution)/shard_map/ppermute | solution.py:259
  7.8 7.6 %collective-permute-start.7 = (bf16[48,1024]{1,0:T(8,128)(2,1)}, bf16[48,1024]{1,0:T(8,128)(2,1)S(1)}, u32[]{:S(2)}, u32[]{:S(2)}) collective-permute-start(bf16[48,1024]{1,0:T(8,128)(2,1)} %param.7), channel_id=1, source_target_pairs={{0,2},{1,3},{2,0},{3,1},{4,6},{5,7},{6,4},{7,5},{8,10},{9,11},{10,... | collective-permute-start | bytes 294920 | tf_op jit(solution)/shard_map/ppermute | solution.py:259
  8.3 7.5 %collective-permute-start.8 = (bf16[48,1024]{1,0:T(8,128)(2,1)}, bf16[48,1024]{1,0:T(8,128)(2,1)S(1)}, u32[]{:S(2)}, u32[]{:S(2)}) collective-permute-start(bf16[48,1024]{1,0:T(8,128)(2,1)} %param.7), channel_id=1, source_target_pairs={{0,16},{1,17},{2,18},{3,19},{4,20},{5,21},{6,22},{7,23},{8,24},{9,... | collective-permute-start | bytes 294920 | tf_op jit(solution)/shard_map/ppermute | solution.py:259
  12.2 11.9 %collective-permute-start.9 = (bf16[48,1024]{1,0:T(8,128)(2,1)S(1)}, bf16[48,1024]{1,0:T(8,128)(2,1)S(1)}, u32[]{:S(2)}, u32[]{:S(2)}) collective-permute-start(bf16[48,1024]{1,0:T(8,128)(2,1)S(1)} %copy-done.5), channel_id=1, source_target_pairs={{0,4},{1,5},{2,6},{3,7},{4,0},{5,1},{6,2},{7,3},{8,12},{9,13},{10,... | collective-permute-start | bytes 294920 | tf_op jit(solution)/shard_map/ppermute | solution.py:259
  12.2 5.8 %copy-start.1 = (f32[64,3072]{1,0:T(8,128)S(1)}, f32[64,3072]{1,0:T(8,128)}, u32[]{:S(2)}) copy-start(f32[64,3072]{1,0:T(8,128)} %refs_1_.1) | copy-start | bytes 2359300
  12.2 8.8 %collective-permute-start.2 = (bf16[96,1024]{1,0:T(8,128)(2,1)S(1)}, bf16[96,1024]{1,0:T(8,128)(2,1)S(1)}, u32[]{:S(2)}, u32[]{:S(2)}) collective-permute-start(bf16[96,1024]{1,0:T(8,128)(2,1)S(1)} %get-tuple-element.17), channel_id=1, source_target_pairs={{0,18},{1,19},{2,16},{3,17},{4,22},{5,23},{6,20},{7,21},{8,26},{9,... | collective-permute-start | bytes 589832 | tf_op jit(solution)/shard_map/ppermute | solution.py:259
  14.9 9.0 %collective-permute-start.3 = (bf16[96,1024]{1,0:T(8,128)(2,1)S(1)}, bf16[96,1024]{1,0:T(8,128)(2,1)S(1)}, u32[]{:S(2)}, u32[]{:S(2)}) collective-permute-start(bf16[96,1024]{1,0:T(8,128)(2,1)S(1)} %get-tuple-element.17), channel_id=1, source_target_pairs={{0,2},{1,3},{2,0},{3,1},{4,6},{5,7},{6,4},{7,5},{8,10},{9,11},{10,... | collective-permute-start | bytes 589832 | tf_op jit(solution)/shard_map/ppermute | solution.py:259
  15.4 8.6 %collective-permute-start.4 = (bf16[96,1024]{1,0:T(8,128)(2,1)S(1)}, bf16[96,1024]{1,0:T(8,128)(2,1)S(1)}, u32[]{:S(2)}, u32[]{:S(2)}) collective-permute-start(bf16[96,1024]{1,0:T(8,128)(2,1)S(1)} %get-tuple-element.17), channel_id=1, source_target_pairs={{0,16},{1,17},{2,18},{3,19},{4,20},{5,21},{6,22},{7,23},{8,24},{9,... | collective-permute-start | bytes 589832 | tf_op jit(solution)/shard_map/ppermute | solution.py:259
  15.8 2.2 %copy-start = (bf16[48,3072]{1,0:T(8,128)(2,1)S(1)}, bf16[48,3072]{1,0:T(8,128)(2,1)}, u32[]{:S(2)}) copy-start(bf16[48,3072]{1,0:T(8,128)(2,1)} %q_ref.5) | copy-start | bytes 884740
  15.8 2.2 %copy-start.2 = (s32[2]{0:T(128)S(1)}, s32[2]{0:T(128)}, u32[]{:S(2)}) copy-start(s32[2]{0:T(128)} %clip_ref.5) | copy-start | bytes 28
  15.9 2.2 %copy-start.3 = (s32[2]{0:T(128)S(1)}, s32[2]{0:T(128)}, u32[]{:S(2)}) copy-start(s32[2]{0:T(128)} %valid_ref.5) | copy-start | bytes 28
  15.9 2.2 %copy-start.4 = (s32[2]{0:T(128)S(1)}, s32[2]{0:T(128)}, u32[]{:S(2)}) copy-start(s32[2]{0:T(128)} %step_ref.5) | copy-start | bytes 28
  15.9 8.4 %collective-permute-start.10 = (bf16[144,1024]{1,0:T(8,128)(2,1)S(1)}, bf16[144,1024]{1,0:T(8,128)(2,1)S(1)}, u32[]{:S(2)}, u32[]{:S(2)}) collective-permute-start(bf16[144,1024]{1,0:T(8,128)(2,1)S(1)} %pad_maximum_fusion.2), channel_id=1, source_target_pairs={{0,4},{1,5},{2,6},{3,7},{4,0},{5,1},{6,2},{7,3},{8,12},{9,13},{10,... | collective-permute-start | bytes 884744 | tf_op jit(solution)/shard_map/ppermute | solution.py:259
  24.0 2.6 %collective-permute-start.5 = (bf16[384,1024]{1,0:T(8,128)(2,1)S(1)}, bf16[384,1024]{1,0:T(8,128)(2,1)S(1)}, u32[]{:S(2)}, u32[]{:S(2)}) collective-permute-start(bf16[384,1024]{1,0:T(8,128)(2,1)S(1)} %constant_dynamic-update-slice_fusion.2.refs_0_), channel_id=1, source_target_pairs={{0,1},{1,0},{2,3},{3,2},{4,5},{5,4},{6,7},{7,6},{8,9},{9,8},{10,11... | collective-permute-start | bytes 2359304 | tf_op jit(solution)/shard_map/ppermute | solution.py:259
  24.3 3.1 %collective-permute-start.11 = (bf16[384,1024]{1,0:T(8,128)(2,1)S(1)}, bf16[384,1024]{1,0:T(8,128)(2,1)S(1)}, u32[]{:S(2)}, u32[]{:S(2)}) collective-permute-start(bf16[384,1024]{1,0:T(8,128)(2,1)S(1)} %constant_dynamic-update-slice_fusion.7), channel_id=1, source_target_pairs={{0,1},{1,0},{2,3},{3,2},{4,5},{5,4},{6,7},{7,6},{8,9},{9,8},{10,11... | collective-permute-start | bytes 2359304 | tf_op jit(solution)/shard_map/ppermute | solution.py:259
